TPU v7x, 32 devices: a whole 2x2x4 slice. The times are simulated.
32 devices in a mesh: heads: 8 (over z, y), hid: 4 (over x, core).
Axes of the slice: x: 2, y: 2, z: 4, core: 2. Of those that a mesh axis runs over, the one named last changes fastest.
Arguments:
- inputs: bfloat16 [8192, 1024], P(('hid', 'heads')), may hold values from -6 to 6
- cotangent: bfloat16 [8192, 1024], P(('hid', 'heads')), may hold values from -6 to 6
- segments: int32 [8192], P(('hid', 'heads')), may hold values from 0 to 7, as said below
- attn_gain: float32 [2, 1024], replicated, may hold values from 0.5 to 1.5
- w_query: bfloat16 [2, 1024, 1024], P(None, None, 'heads'), may hold values from -0.1875 to 0.1875
- w_key: bfloat16 [2, 1024, 1024], P(None, None, 'heads'), may hold values from -0.1875 to 0.1875
- w_value: bfloat16 [2, 1024, 1024], P(None, None, 'heads'), may hold values from -0.1875 to 0.1875
- w_out: bfloat16 [2, 1024, 1024], P(None, 'heads'), may hold values from -0.75 to 0.75
- mlp_gain: float32 [2, 1024], replicated, may hold values from 0.5 to 1.5
- w_gate: bfloat16 [2, 1024, 2816], P(None, None, 'hid'), may hold values from -0.1875 to 0.1875
- w_up: bfloat16 [2, 1024, 2816], P(None, None, 'hid'), may hold values from -0.1875 to 0.1875
- w_down: bfloat16 [2, 2816, 1024], P(None, 'hid'), may hold values from -0.109375 to 0.109375
Outputs:
- block_out: bfloat16 [8192, 1024], P(('hid', 'heads'))
- input_grad: float32 [8192, 1024], P(('hid', 'heads'))
- attn_gain_grad: float32 [2, 1024], replicated
- query_grad: float32 [2, 1024, 1024], P(None, None, 'heads')
- key_grad: float32 [2, 1024, 1024], P(None, None, 'heads')
- value_grad: float32 [2, 1024, 1024], P(None, None, 'heads')
- out_grad: float32 [2, 1024, 1024], P(None, 'heads')
- mlp_gain_grad: float32 [2, 1024], replicated
- gate_grad: float32 [2, 1024, 2816], P(None, None, 'hid')
- up_grad: float32 [2, 1024, 2816], P(None, None, 'hid')
- down_grad: float32 [2, 2816, 1024], P(None, 'hid')
Inputs may be any that keep to these rules, and one draw needn't show every extreme that they name: `segments`: segment numbers never fall along the tokens; group k of 2048 consecutive tokens uses numbers from k * (2) to (k + 1) * 2 - 1 and holds whole sequences whose lengths are multiples of 1024; in one group, drawn from the seed, all tokens form one sequence.
All inputs are finite; a program needn't handle non-finite values.
Results may differ from a plain program's by a relative error of at most 0.035.
Values may be sent and summed in bfloat16 or wider, within the bound.
No kernel may reach another device: no remote copies, remote signals or barrier semaphores. Data moves between devices by JAX's collectives and lax.ppermute only.
A program may use at most 256 MiB of HBM per device.

v0:
```python
import jax
import jax.numpy as jnp
from jax import lax
from jax.sharding import PartitionSpec as P

HEAD_DIM = 64


EPSILON = 1e-06
THETA = 10000.0
NEG_LARGE = -1e30


def rms_scale(values, gain):
    return values * lax.rsqrt(jnp.mean(values * values, axis=-1, keepdims=True) + EPSILON) * gain


def positions_of(segment_row):
    row_count = segment_row.shape[0]
    row_index = jnp.arange(row_count, dtype=jnp.int32)
    changes = jnp.concatenate(
        [jnp.ones((1,), dtype=jnp.bool_), segment_row[1:] != segment_row[:-1]]
    )
    seq_starts = lax.cummax(jnp.where(changes, row_index, jnp.zeros_like(row_index)), axis=0)
    return row_index - seq_starts


def rope_tables(segment_row):
    positions = positions_of(segment_row).astype(jnp.float32)
    halfway = HEAD_DIM // 2
    frequency = THETA ** (-jnp.arange(halfway, dtype=jnp.float32) * 2.0 / HEAD_DIM)
    angles = positions[:, None] * frequency[None, :]
    return (jnp.cos(angles), jnp.sin(angles))


def rotate_pairs(flat, cosine, sine):
    shaped = flat.reshape(flat.shape[0], -1, HEAD_DIM)
    halfway = HEAD_DIM // 2
    former = shaped[..., :halfway]
    latter = shaped[..., halfway:]
    cos_rows = cosine[:, None, :]
    sin_rows = sine[:, None, :]
    turned = jnp.concatenate(
        [former * cos_rows - latter * sin_rows, latter * cos_rows + former * sin_rows], axis=-1
    )
    return turned.reshape(flat.shape)


def block_mask(segment_row, first_row, block_rows):
    group_rows = segment_row.shape[0]
    query_segments = lax.dynamic_slice_in_dim(segment_row, first_row, block_rows, 0)
    query_index = first_row + jnp.arange(block_rows, dtype=jnp.int32)
    key_index = jnp.arange(group_rows, dtype=jnp.int32)
    return (query_segments[:, None] == segment_row[None, :]) & (
        key_index[None, :] <= query_index[:, None]
    )


def rows_product(left, right):
    return jnp.dot(left, right, preferred_element_type=jnp.float32)


def rows_back(grads, weights):
    summed = None
    for grad_rows, weight in zip(grads, weights):
        product_term = jnp.einsum(
            "rc,dc->rd", grad_rows, weight, preferred_element_type=jnp.float32
        )
        summed = product_term if summed is None else summed + product_term
    return summed


def gated_unit(gate, upward):
    return gate * jax.nn.sigmoid(gate) * upward


def project_heads(gathered, w_query, w_key, w_value, value_first, cosine, sine):
    query_raw = jnp.dot(gathered, w_query, preferred_element_type=jnp.float32)
    key_raw = jnp.dot(gathered, w_key, preferred_element_type=jnp.float32)
    value_raw = jnp.dot(gathered, w_value, preferred_element_type=jnp.float32)
    queries = rotate_pairs(query_raw, cosine, sine).astype(jnp.bfloat16)
    keys = rotate_pairs(key_raw, cosine, sine).astype(jnp.bfloat16)
    if value_first is None:
        values = value_raw.astype(jnp.bfloat16)
    else:
        values = (0.5 * value_raw + 0.5 * value_first.astype(jnp.float32)).astype(jnp.bfloat16)
    return (queries, keys, values)


def attention_forward(queries, keys, values, segment_row, block_rows):
    group_rows, width = queries.shape
    heads_local = width // HEAD_DIM
    key_heads = keys.reshape(group_rows, heads_local, HEAD_DIM)
    value_heads = values.reshape(group_rows, heads_local, HEAD_DIM)
    score_scale = HEAD_DIM ** (-0.5)

    def one_block(number):
        first_row = number * block_rows
        query_block = lax.dynamic_slice_in_dim(queries, first_row, block_rows, 0).reshape(
            block_rows, heads_local, HEAD_DIM
        )
        scores = (
            jnp.einsum("qhe,khe->hqk", query_block, key_heads, preferred_element_type=jnp.float32)
            * score_scale
        )
        scores = jnp.where(block_mask(segment_row, first_row, block_rows)[None], scores, NEG_LARGE)
        highest = jnp.max(scores, axis=-1, keepdims=True)
        exponent = jnp.exp(scores - highest)
        totals = jnp.sum(exponent, axis=-1, keepdims=True)
        softmax_rows = exponent / totals
        attended = jnp.einsum(
            "hqk,khe->qhe",
            softmax_rows.astype(jnp.bfloat16),
            value_heads,
            preferred_element_type=jnp.float32,
        )
        return (
            attended.reshape(block_rows, width).astype(jnp.bfloat16),
            (highest + jnp.log(totals))[..., 0],
        )

    attended, log_totals = lax.map(one_block, jnp.arange(group_rows // block_rows, dtype=jnp.int32))
    return (attended.reshape(group_rows, width), log_totals)


def attention_backward(queries, keys, values, attended_back, log_totals, segment_row, block_rows):
    group_rows, width = queries.shape
    heads_local = width // HEAD_DIM
    key_heads = keys.reshape(group_rows, heads_local, HEAD_DIM)
    value_heads = values.reshape(group_rows, heads_local, HEAD_DIM)
    score_scale = HEAD_DIM ** (-0.5)

    def one_block(carry, number):
        key_total, value_total = carry
        first_row = number * block_rows
        query_block = lax.dynamic_slice_in_dim(queries, first_row, block_rows, 0).reshape(
            block_rows, heads_local, HEAD_DIM
        )
        grad_block = lax.dynamic_slice_in_dim(attended_back, first_row, block_rows, 0).reshape(
            block_rows, heads_local, HEAD_DIM
        )
        scores = (
            jnp.einsum("qhe,khe->hqk", query_block, key_heads, preferred_element_type=jnp.float32)
            * score_scale
        )
        scores = jnp.where(block_mask(segment_row, first_row, block_rows)[None], scores, NEG_LARGE)
        softmax_rows = jnp.exp(scores - log_totals[number][..., None])
        prob_back = jnp.einsum(
            "qhe,khe->hqk", grad_block, value_heads, preferred_element_type=jnp.float32
        )
        inner_sum = jnp.sum(prob_back * softmax_rows, axis=-1, keepdims=True)
        score_back = (softmax_rows * (prob_back - inner_sum)).astype(jnp.bfloat16)
        query_part = (
            jnp.einsum("hqk,khe->qhe", score_back, key_heads, preferred_element_type=jnp.float32)
            * score_scale
        )
        key_total = (
            key_total
            + jnp.einsum(
                "hqk,qhe->khe", score_back, query_block, preferred_element_type=jnp.float32
            )
            * score_scale
        )
        value_total = value_total + jnp.einsum(
            "hqk,qhe->khe",
            softmax_rows.astype(jnp.bfloat16),
            grad_block,
            preferred_element_type=jnp.float32,
        )
        return ((key_total, value_total), query_part.reshape(block_rows, width))

    empty_heads = jnp.zeros((group_rows, heads_local, HEAD_DIM), jnp.float32)
    carried, query_parts = lax.scan(
        one_block, (empty_heads, empty_heads), jnp.arange(group_rows // block_rows, dtype=jnp.int32)
    )
    return (
        query_parts.reshape(group_rows, width),
        carried[0].reshape(group_rows, width),
        carried[1].reshape(group_rows, width),
    )


def per_device(
    inputs,
    cotangent,
    segments,
    attn_gain,
    w_query,
    w_key,
    w_value,
    w_out,
    mlp_gain,
    w_gate,
    w_up,
    w_down,
):
    layer_count = w_query.shape[0]
    group_segments = lax.all_gather(segments, "heads", axis=0, tiled=True)
    group_rows = group_segments.shape[0]
    block_rows = min(512, group_rows)
    cosine, sine = rope_tables(group_segments)
    residual = inputs.astype(jnp.float32)
    stored = []
    value_first = None
    for layer_index in range(layer_count):
        attn_normed = rms_scale(residual, attn_gain[layer_index]).astype(jnp.bfloat16)
        gathered = lax.all_gather(attn_normed, "heads", axis=0, tiled=True)
        queries, keys, values = project_heads(
            gathered,
            w_query[layer_index],
            w_key[layer_index],
            w_value[layer_index],
            value_first if layer_index > 0 else None,
            cosine,
            sine,
        )
        attended, log_totals = attention_forward(queries, keys, values, group_segments, block_rows)
        attn_sum = lax.psum_scatter(
            rows_product(attended, w_out[layer_index]).astype(jnp.bfloat16),
            "heads",
            scatter_dimension=0,
            tiled=True,
        ).astype(jnp.float32)
        head_rows = None
        if layer_index == 0:
            value_first = values
        middle = residual + attn_sum
        mlp_normed = rms_scale(middle, mlp_gain[layer_index]).astype(jnp.bfloat16)
        mixed_rows = lax.all_gather(mlp_normed, "hid", axis=0, tiled=True)
        gate = jnp.dot(mixed_rows, w_gate[layer_index], preferred_element_type=jnp.float32)
        upward = jnp.dot(mixed_rows, w_up[layer_index], preferred_element_type=jnp.float32)
        hidden = gated_unit(gate, upward).astype(jnp.bfloat16)
        mlp_sum = lax.psum_scatter(
            rows_product(hidden, w_down[layer_index]).astype(jnp.bfloat16),
            "hid",
            scatter_dimension=0,
            tiled=True,
        ).astype(jnp.float32)
        kept_rows = None
        stored.append((residual, middle, attended, log_totals, kept_rows, head_rows))
        residual = middle + mlp_sum
    block_out = residual.astype(jnp.bfloat16)
    grad_residual = cotangent.astype(jnp.float32)
    query_grads, key_grads, value_grads, out_grads = ([], [], [], [])
    gate_grads, up_grads, down_grads = ([], [], [])
    attn_gain_grads, mlp_gain_grads = ([], [])
    value_extra = None
    for layer_index in reversed(range(layer_count)):
        before, middle, attended, log_totals, kept_rows, head_rows = stored[layer_index]
        mixed_rows = lax.all_gather(
            rms_scale(middle, mlp_gain[layer_index]).astype(jnp.bfloat16), "hid", axis=0, tiled=True
        )
        down_in = lax.all_gather(grad_residual.astype(jnp.bfloat16), "hid", axis=0, tiled=True)
        gate = jnp.dot(mixed_rows, w_gate[layer_index], preferred_element_type=jnp.float32)
        upward = jnp.dot(mixed_rows, w_up[layer_index], preferred_element_type=jnp.float32)
        hidden, pull_gate = jax.vjp(gated_unit, gate, upward)
        hidden = hidden.astype(jnp.bfloat16)
        hidden_grad = jnp.einsum(
            "rd,fd->rf", down_in, w_down[layer_index], preferred_element_type=jnp.float32
        )
        down_grads.append(
            jnp.einsum("rf,rd->fd", hidden, down_in, preferred_element_type=jnp.float32)
        )
        gate_back, up_back = pull_gate(hidden_grad)
        gate_back = gate_back.astype(jnp.bfloat16)
        up_back = up_back.astype(jnp.bfloat16)
        gate_grads.append(
            jnp.einsum("rd,rf->df", mixed_rows, gate_back, preferred_element_type=jnp.float32)
        )
        up_grads.append(
            jnp.einsum("rd,rf->df", mixed_rows, up_back, preferred_element_type=jnp.float32)
        )
        normed_back = lax.psum_scatter(
            rows_back((gate_back, up_back), (w_gate[layer_index], w_up[layer_index])).astype(
                jnp.bfloat16
            ),
            "hid",
            scatter_dimension=0,
            tiled=True,
        ).astype(jnp.float32)
        unused_norm, pull_norm = jax.vjp(rms_scale, middle, mlp_gain[layer_index])
        middle_part, mlp_gain_part = pull_norm(normed_back)
        mlp_gain_grads.append(mlp_gain_part)
        middle_back = grad_residual + middle_part
        gathered = lax.all_gather(
            rms_scale(before, attn_gain[layer_index]).astype(jnp.bfloat16),
            "heads",
            axis=0,
            tiled=True,
        )
        attn_in = lax.all_gather(middle_back.astype(jnp.bfloat16), "heads", axis=0, tiled=True)
        queries, keys, values = project_heads(
            gathered,
            w_query[layer_index],
            w_key[layer_index],
            w_value[layer_index],
            value_first if layer_index > 0 else None,
            cosine,
            sine,
        )
        out_grads.append(
            jnp.einsum("gc,gd->cd", attended, attn_in, preferred_element_type=jnp.float32)
        )
        attended_back = jnp.einsum(
            "gd,cd->gc", attn_in, w_out[layer_index], preferred_element_type=jnp.float32
        ).astype(jnp.bfloat16)
        query_back, key_back, value_back = attention_backward(
            queries, keys, values, attended_back, log_totals, group_segments, block_rows
        )
        query_raw = rotate_pairs(query_back, cosine, -sine).astype(jnp.bfloat16)
        key_raw = rotate_pairs(key_back, cosine, -sine).astype(jnp.bfloat16)
        if layer_index > 0:
            value_round = value_back.astype(jnp.bfloat16).astype(jnp.float32)
            value_extra = 0.5 * value_round
            value_raw = (0.5 * value_round).astype(jnp.bfloat16)
        else:
            value_raw = (value_back + value_extra).astype(jnp.bfloat16)
        query_grads.append(
            jnp.einsum("gd,gc->dc", gathered, query_raw, preferred_element_type=jnp.float32)
        )
        key_grads.append(
            jnp.einsum("gd,gc->dc", gathered, key_raw, preferred_element_type=jnp.float32)
        )
        value_grads.append(
            jnp.einsum("gd,gc->dc", gathered, value_raw, preferred_element_type=jnp.float32)
        )
        normed_in = lax.psum_scatter(
            rows_back(
                (query_raw, key_raw, value_raw),
                (w_query[layer_index], w_key[layer_index], w_value[layer_index]),
            ).astype(jnp.bfloat16),
            "heads",
            scatter_dimension=0,
            tiled=True,
        ).astype(jnp.float32)
        unused_norm, pull_norm = jax.vjp(rms_scale, before, attn_gain[layer_index])
        before_part, attn_gain_part = pull_norm(normed_in)
        attn_gain_grads.append(attn_gain_part)
        grad_residual = middle_back + before_part

    def stacked(listed):
        return jnp.stack(listed[::-1], axis=0)

    attn_parts = (
        stacked(query_grads),
        stacked(key_grads),
        stacked(value_grads),
        stacked(out_grads),
    )
    attn_weight_grads = (
        lax.psum(attn_parts[0].astype(jnp.bfloat16), "hid").astype(jnp.float32),
        lax.psum(attn_parts[1].astype(jnp.bfloat16), "hid").astype(jnp.float32),
        lax.psum(attn_parts[2].astype(jnp.bfloat16), "hid").astype(jnp.float32),
        lax.psum(attn_parts[3].astype(jnp.bfloat16), "hid").astype(jnp.float32),
    )
    mlp_weight_grads = (
        lax.psum(stacked(gate_grads).astype(jnp.bfloat16), "heads").astype(jnp.float32),
        lax.psum(stacked(up_grads).astype(jnp.bfloat16), "heads").astype(jnp.float32),
        lax.psum(stacked(down_grads).astype(jnp.bfloat16), "heads").astype(jnp.float32),
    )
    gain_grads = lax.psum((stacked(attn_gain_grads), stacked(mlp_gain_grads)), ("heads", "hid"))
    return (
        block_out,
        grad_residual,
        gain_grads[0],
        attn_weight_grads[0],
        attn_weight_grads[1],
        attn_weight_grads[2],
        attn_weight_grads[3],
        gain_grads[1],
        mlp_weight_grads[0],
        mlp_weight_grads[1],
        mlp_weight_grads[2],
    )


def solution(mesh):
    placed = (
        P(("hid", "heads"), None),
        P(("hid", "heads"), None),
        P(("hid", "heads")),
        P(),
        P(None, None, "heads"),
        P(None, None, "heads"),
        P(None, None, "heads"),
        P(None, "heads", None),
        P(),
        P(None, None, "hid"),
        P(None, None, "hid"),
        P(None, "hid", None),
    )
    return jax.shard_map(
        per_device,
        mesh=mesh,
        in_specs=placed,
        out_specs=(
            P(("hid", "heads"), None),
            P(("hid", "heads"), None),
            P(),
            P(None, None, "heads"),
            P(None, None, "heads"),
            P(None, None, "heads"),
            P(None, "heads", None),
            P(),
            P(None, None, "hid"),
            P(None, None, "hid"),
            P(None, "hid", None),
        ),
        check_vma=False,
    )
```

profile of v0, /device:TPU:0, one launch (start us, length us, event | category | flops | bytes accessed | tf_op | source)
XLA Modules:
  0.0 1555.9 jit_solution(16965814923954478843)
XLA Ops:
  12.5 22.6 %all-gather = s32[8,1,256]{2,1,0:T(1,128)S(1)} all-gather(s32[1,1,256]{2,1,0:T(1,128)} %bitcast.433), channel_id=1, replica_groups=mesh['heads'=8,'hid'=4] {'heads'}, dimensions={0}, use_global_device_ids=true | all-gather | bytes 9216 | tf_op jit(solution)/shard_map/all_gather | solution.py:198
  41.5 47.2 %all-gather.10.cloned.1.call-done = bf16[2048,1024]{1,0:T(8,128)(2,1)} async-done(((bf16[256,1024]{1,0:T(8,128)(2,1)}), bf16[2048,1024]{1,0:T(8,128)(2,1)}) %all-gather.10.cloned.1.call-update) | async-done | bytes 4194320 | tf_op jit(solution)/shard_map/all_gather | solution.py:207
  88.8 3.8 fusion.48
  96.8 39.4 %while.54 = (s32[]{:T(128)}, bf16[4,512,128]{2,1,0:T(8,128)(2,1)S(1)}, f32[4,2,512]{2,1,0:T(2,128)S(1)}, s32[4]{0:T(128)S(1)}, s32[2048]{0:T(1024)S(1)}, /*index...) while((s32[]{:T(128)}, ...), condition=%wide.region_6.7_spmd, body=%wide.region_3.6_spmd.sunk | while | flops 565247488 | bytes 31508684 | solution.py:122
  136.8 4.3 convolution_convert_fusion.1
  141.9 85.8 %reduce-scatter.9.cloned.1.call-done = bf16[256,1024]{1,0:T(8,128)(2,1)} async-done(((bf16[2048,1024]{1,0:T(8,128)(2,1)}), bf16[256,1024]{1,0:T(8,128)(2,1)}) %reduce-scatter.9.cloned.1.call-update) | async-done | bytes 524304 | tf_op jit(solution)/shard_map/reduce_scatter | solution.py:218
  231.2 22.4 %all-gather.12.cloned.1.call-done = bf16[1024,1024]{1,0:T(8,128)(2,1)} async-done(((bf16[256,1024]{1,0:T(8,128)(2,1)}), bf16[1024,1024]{1,0:T(8,128)(2,1)}) %all-gather.12.cloned.1.call-update) | async-done | bytes 2097168 | tf_op jit(solution)/shard_map/all_gather | solution.py:229
  253.6 3.8 fusion.86
  257.5 3.5 multiply_convert_fusion.5
  262.1 3.2 convolution_convert_fusion.6
  265.3 31.5 %reduce-scatter.11.cloned.1.call-done = bf16[256,1024]{1,0:T(8,128)(2,1)} async-done(((bf16[1024,1024]{1,0:T(8,128)(2,1)}), bf16[256,1024]{1,0:T(8,128)(2,1)}) %reduce-scatter.11.cloned.1.call-update) | async-done | bytes 524304 | tf_op jit(solution)/shard_map/reduce_scatter | solution.py:233
  300.6 72.3 %all-gather.14.cloned.1.call-done = bf16[2048,1024]{1,0:T(8,128)(2,1)} async-done(((bf16[256,1024]{1,0:T(8,128)(2,1)}), bf16[2048,1024]{1,0:T(8,128)(2,1)}) %all-gather.14.cloned.1.call-update) | async-done | bytes 4194320 | tf_op jit(solution)/shard_map/all_gather | solution.py:207
  372.9 3.8 fusion.44
  381.0 39.4 %while.55 = (s32[]{:T(128)}, bf16[4,512,128]{2,1,0:T(8,128)(2,1)S(1)}, f32[4,2,512]{2,1,0:T(2,128)S(1)}, s32[4]{0:T(128)S(1)}, s32[2048]{0:T(1024)S(1)}, /*index...) while((s32[]{:T(128)}, ...), condition=%wide.region_14.15_spmd, body=%wide.region_11.14_spmd.sunk | while | flops 565247488 | bytes 31508684 | solution.py:122
  420.4 4.4 convolution_convert_fusion
  424.9 86.3 %reduce-scatter.13.cloned.1.call-done = bf16[256,1024]{1,0:T(8,128)(2,1)} async-done(((bf16[2048,1024]{1,0:T(8,128)(2,1)}), bf16[256,1024]{1,0:T(8,128)(2,1)}) %reduce-scatter.13.cloned.1.call-update) | async-done | bytes 524304 | tf_op jit(solution)/shard_map/reduce_scatter | solution.py:218
  515.5 21.5 %all-gather.16.cloned.1.call-done = bf16[1024,1024]{1,0:T(8,128)(2,1)} async-done(((bf16[256,1024]{1,0:T(8,128)(2,1)}), bf16[1024,1024]{1,0:T(8,128)(2,1)}) %all-gather.16.cloned.1.call-update) | async-done | bytes 2097168 | tf_op jit(solution)/shard_map/all_gather | solution.py:229
  537.0 5.4 fusion.72
  542.4 3.3 fusion.76
  545.7 15.6 %all-gather.18.cloned.1.call-done = bf16[1024,1024]{1,0:T(8,128)(2,1)} async-done(((bf16[256,1024]{1,0:T(8,128)(2,1)}), bf16[1024,1024]{1,0:T(8,128)(2,1)}) %all-gather.18.cloned.1.call-update) | async-done | bytes 2097168 | tf_op jit(solution)/shard_map/all_gather | solution.py:253
  561.2 7.7 multiply_convert_fusion.3
  571.9 3.3 add_convert_fusion.3
  575.2 31.5 %reduce-scatter.17.cloned.1.call-done = bf16[256,1024]{1,0:T(8,128)(2,1)} async-done(((bf16[1024,1024]{1,0:T(8,128)(2,1)}), bf16[256,1024]{1,0:T(8,128)(2,1)}) %reduce-scatter.17.cloned.1.call-update) | async-done | bytes 524304 | tf_op jit(solution)/shard_map/reduce_scatter | solution.py:273
  611.1 73.5 %all-gather.20.cloned.1.call-done = bf16[2048,1024]{1,0:T(8,128)(2,1)} async-done(((bf16[256,1024]{1,0:T(8,128)(2,1)}), bf16[2048,1024]{1,0:T(8,128)(2,1)}) %all-gather.20.cloned.1.call-update) | async-done | bytes 4194320 | tf_op jit(solution)/shard_map/all_gather | solution.py:291
  684.6 4.3 convolution_convert_fusion.3
  690.0 106.5 %while.56 = (s32[]{:T(128)}, f32[2048,2,64]{0,2,1:T(8,128)S(1)}, f32[2048,2,64]{0,2,1:T(8,128)}, f32[4,512,128]{1,0,2:T(4,128)}, s32[4]{0:T(128)S(1)}, /*index=5...) while((s32[]{:T(128)}, f32[2048,2,64]{0,2,1:T(8,128)S(1)}, ...), condition=%wide.region_22.23_spmd.clone, body=%wide.region_20.22_spmd.clone.sunk | while | flops 1378156032 | bytes 75544856 | solution.py:173
  698.1 3.5 fusion.322
  709.8 6.1 dynamic_update_slice.37
  723.6 4.7 fusion.322
  736.6 6.1 dynamic_update_slice.37
  750.4 4.7 fusion.322
  763.4 6.1 dynamic_update_slice.37
  777.2 4.7 fusion.322
  790.2 6.1 dynamic_update_slice.37
  804.0 3.3 add_convert_fusion.1
  807.5 5.0 convolution_convert_fusion.5
  812.6 81.1 %reduce-scatter.19.cloned.1.call-done = bf16[256,1024]{1,0:T(8,128)(2,1)} async-done(((bf16[2048,1024]{1,0:T(8,128)(2,1)}), bf16[256,1024]{1,0:T(8,128)(2,1)}) %reduce-scatter.19.cloned.1.call-update) | async-done | bytes 524304 | tf_op jit(solution)/shard_map/reduce_scatter | solution.py:327
  895.7 32.4 %reduce-scatter.15.cloned.1.call-done = bf16[256,1024]{1,0:T(8,128)(2,1)} async-done(((bf16[1024,1024]{1,0:T(8,128)(2,1)}), bf16[256,1024]{1,0:T(8,128)(2,1)}) %reduce-scatter.15.cloned.1.call-update) | async-done | bytes 524304 | tf_op jit(solution)/shard_map/reduce_scatter | solution.py:233
  931.1 22.7 %all-gather.22.cloned.1.call-done = bf16[1024,1024]{1,0:T(8,128)(2,1)} async-done(((bf16[256,1024]{1,0:T(8,128)(2,1)}), bf16[1024,1024]{1,0:T(8,128)(2,1)}) %all-gather.22.cloned.1.call-update) | async-done | bytes 2097168 | tf_op jit(solution)/shard_map/all_gather | solution.py:253
  953.8 6.4 multiply_convert_fusion.2
  963.2 3.2 add_convert_fusion.2
  966.4 31.6 %reduce-scatter.21.cloned.1.call-done = bf16[256,1024]{1,0:T(8,128)(2,1)} async-done(((bf16[1024,1024]{1,0:T(8,128)(2,1)}), bf16[256,1024]{1,0:T(8,128)(2,1)}) %reduce-scatter.21.cloned.1.call-update) | async-done | bytes 524304 | tf_op jit(solution)/shard_map/reduce_scatter | solution.py:273
  1002.9 3.8 fusion.63
  1031.5 44.4 %all-gather.24.cloned.1.call-done = bf16[2048,1024]{1,0:T(8,128)(2,1)} async-done(((bf16[256,1024]{1,0:T(8,128)(2,1)}), bf16[2048,1024]{1,0:T(8,128)(2,1)}) %all-gather.24.cloned.1.call-update) | async-done | bytes 4194320 | tf_op jit(solution)/shard_map/all_gather | solution.py:291
  1075.9 4.2 convolution_convert_fusion.2
  1081.3 108.8 %while.57 = (s32[]{:T(128)}, f32[2048,2,64]{0,2,1:T(8,128)S(1)}, f32[2048,2,64]{0,2,1:T(8,128)}, f32[4,512,128]{1,0,2:T(4,128)}, s32[4]{0:T(128)S(1)}, /*index=5...) while((s32[]{:T(128)}, f32[2048,2,64]{0,2,1:T(8,128)S(1)}, ...), condition=%wide.region_29.30_spmd.clone, body=%wide.region_27.29_spmd.clone.sunk | while | flops 1378156032 | bytes 75544856 | solution.py:173
  1089.7 3.5 fusion.336
  1101.4 6.1 dynamic_update_slice.38
  1115.9 4.7 fusion.336
  1128.9 6.1 dynamic_update_slice.38
  1143.4 4.7 fusion.336
  1156.3 6.1 dynamic_update_slice.38
  1170.8 4.7 fusion.336
  1183.7 6.1 dynamic_update_slice.38
  1193.1 3.1 fusion.114
  1205.7 4.6 fusion.145
  1214.1 3.3 add_convert_fusion
  1218.1 139.7 %all-reduce.6.cloned.1.call-done = (bf16[2,1024,704]{1,2,0:T(8,128)(2,1)}, bf16[2,1024,704]{1,2,0:T(8,128)(2,1)}, bf16[2,704,1024]{2,1,0:T(8,128)(2,1)}) async-done(((bf16[2,1024,704]{1,2,0:T(8,128)(2,1)}, bf16[2,1024,704]{1,2,0:T(8,128)(2,1)}, bf16[2,704,1024]{2,1,0:T(8,128)(2,1)}), (bf16[2,1024,704]{1,2,0:T(8,128)(2,1)}, bf16[2,1024,704]{1,2,0:T(8,128)(2,1)}, ...) | async-done | bytes 8650768 | tf_op jit(solution)/shard_map/psum | solution.py:357
  1357.8 5.2 convert_element_type.357
  1363.0 3.3 convert_element_type.358
  1366.3 3.3 convert_element_type.359
  1369.6 42.1 %all-reduce.8.cloned.1.call-done = (bf16[2,1024,128]{2,1,0:T(8,128)(2,1)}, bf16[2,1024,128]{2,1,0:T(8,128)(2,1)}, bf16[2,1024,128]{2,1,0:T(8,128)(2,1)}, bf16[2,128,1024]{2,1,0:T(8,128)(2,1)}) async-done(((bf16[2,1024,128]{2,1,0:T(8,128)(2,1)}, bf16[2,1024,128]{2,1,0:T(8,128)(2,1)}, bf16[2,1024,128]{2,1,0:T(8,128)(2,1)}, bf16[2,128,1024]{2,1,0:T(8,128)(2,1)}), (bf16[2,1024,128]{2,1,0:T(8,128)(2,1)}, ...) | async-done | bytes 2097168 | tf_op jit(solution)/shard_map/psum | solution.py:351
  1419.1 84.7 %reduce-scatter.23.cloned.1.call-done = bf16[256,1024]{1,0:T(8,128)(2,1)} async-done(((bf16[2048,1024]{1,0:T(8,128)(2,1)}), bf16[256,1024]{1,0:T(8,128)(2,1)}) %reduce-scatter.23.cloned.1.call-update) | async-done | bytes 524304 | tf_op jit(solution)/shard_map/reduce_scatter | solution.py:327
  1505.4 40.5 %all-reduce = (f32[2,1024]{1,0:T(2,128)}, f32[2,1024]{1,0:T(2,128)}) all-reduce(f32[2,1024]{1,0:T(2,128)S(1)} %pad_maximum_fusion.11, f32[2,1024]{1,0:T(2,128)S(1)} %pad_maximum_fusion.12), channel_id=1, replica_groups=mesh['heads'=8,'hid'=4] {'heads','hid'}, use_global_device_ids=true, to_apply=%region_34.35 | all-reduce | flops 4096 | bytes 32768 | tf_op jit(solution)/shard_map/psum | solution.py:361
  (554 shorter events, 299.1 us)
Async XLA Ops:
  7.2 81.6 %all-gather.10.cloned.1.call-start = ((), (), s32[]{:S(2)}) async-start(), calls=%async_computation.8 | async-start | bytes 4718592 | tf_op jit(solution)/shard_map/all_gather | solution.py:207
  9.8 288.4 %copy-start.63 = (f32[1,1024]{1,0:T(1,128)}, f32[1,1024]{1,0:T(1,128)S(1)}, u32[]{:S(2)}) copy-start(f32[1,1024]{1,0:T(1,128)S(1)} %get-tuple-element.505) | copy-start | bytes 12292
  12.5 215.2 %reduce-scatter.9.cloned.1.call-start = ((), (), s32[]{:S(2)}) async-start(), calls=%async_computation.9 | async-start | bytes 4718592 | tf_op jit(solution)/shard_map/reduce_scatter | solution.py:218
  41.5 336.8 %copy-start.23 = (f32[2048,32]{0,1:T(8,128)}, f32[2048,32]{0,1:T(8,128)S(1)}, u32[]{:S(2)}) copy-start(f32[2048,32]{0,1:T(8,128)S(1)} %get-tuple-element.504) | copy-start | bytes 786436
  136.3 242.4 %copy-start.6 = (bf16[2048,2,64]{0,2,1:T(8,128)(2,1)}, bf16[2048,2,64]{0,2,1:T(8,128)(2,1)S(1)}, u32[]{:S(2)}) copy-start(bf16[2048,2,64]{0,2,1:T(8,128)(2,1)S(1)} %get-tuple-element.965) | copy-start | bytes 1572868
  141.2 86.5 %copy-start.3 = (bf16[256,1024]{1,0:T(8,128)(2,1)S(1)}, bf16[256,1024]{1,0:T(8,128)(2,1)}, u32[]{:S(2)}) copy-start(bf16[256,1024]{1,0:T(8,128)(2,1)} %param.20) | copy-start | bytes 1572868
  141.2 112.4 %all-gather.12.cloned.1.call-start = ((), (), s32[]{:S(2)}) async-start(), calls=%async_computation.10 | async-start | bytes 2621440 | tf_op jit(solution)/shard_map/all_gather | solution.py:229
  141.9 115.6 %copy-start.57 = (f32[1,1024]{1,0:T(1,128)}, f32[1,1024]{1,0:T(1,128)S(1)}, u32[]{:S(2)}) copy-start(f32[1,1024]{1,0:T(1,128)S(1)} %get-tuple-element.507) | copy-start | bytes 12292
  229.0 28.4 %copy-start.79 = (f32[256]{0:T(256)}, f32[256]{0:T(256)S(1)}, u32[]{:S(2)}) copy-start(f32[256]{0:T(256)S(1)} %multiply_reduce_fusion.4) | copy-start | bytes 3076
  229.0 28.4 %copy-start.65 = (f32[256]{0:T(256)}, f32[256]{0:T(256)S(1)}, u32[]{:S(2)}) copy-start(f32[256]{0:T(256)S(1)} %fusion.163) | copy-start | bytes 3076
  231.1 65.8 %reduce-scatter.11.cloned.1.call-start = ((), (), s32[]{:S(2)}) async-start(), calls=%async_computation.11 | async-start | bytes 2621440 | tf_op jit(solution)/shard_map/reduce_scatter | solution.py:233
  262.1 34.8 %copy-start.10 = (bf16[256,1024]{1,0:T(8,128)(2,1)S(1)}, bf16[256,1024]{1,0:T(8,128)(2,1)}, u32[]{:S(2)}) copy-start(bf16[256,1024]{1,0:T(8,128)(2,1)} %reduce-scatter.9.cloned.1.call-done) | copy-start | bytes 1572868
  265.3 34.0 %copy-start.51 = (bf16[128,1024]{0,1:T(8,128)(2,1)S(1)}, bf16[128,1024]{0,1:T(8,128)(2,1)}, u32[]{:S(2)}) copy-start(bf16[128,1024]{0,1:T(8,128)(2,1)} %get-tuple-element.498) | copy-start | bytes 786436
  265.3 107.6 %all-gather.14.cloned.1.call-start = ((), (), s32[]{:S(2)}) async-start(), calls=%async_computation.12 | async-start | bytes 4718592 | tf_op jit(solution)/shard_map/all_gather | solution.py:207
  298.2 78.5 %copy-start.81 = (f32[256]{0:T(256)}, f32[256]{0:T(256)S(1)}, u32[]{:S(2)}) copy-start(f32[256]{0:T(256)S(1)} %get-tuple-element.458) | copy-start | bytes 3076
  298.2 78.5 %copy-start.73 = (f32[256]{0:T(256)}, f32[256]{0:T(256)S(1)}, u32[]{:S(2)}) copy-start(f32[256]{0:T(256)S(1)} %fusion.164) | copy-start | bytes 3076
  299.2 211.9 %reduce-scatter.13.cloned.1.call-start = ((), (), s32[]{:S(2)}) async-start(), calls=%async_computation.13 | async-start | bytes 4718592 | tf_op jit(solution)/shard_map/reduce_scatter | solution.py:218
  424.9 112.1 %all-gather.16.cloned.1.call-start = ((), (), s32[]{:S(2)}) async-start(), calls=%async_computation.14 | async-start | bytes 2621440 | tf_op jit(solution)/shard_map/all_gather | solution.py:229
  514.5 46.8 %all-gather.18.cloned.1.call-start = ((), (), s32[]{:S(2)}) async-start(), calls=%async_computation.16 | async-start | bytes 2621440 | tf_op jit(solution)/shard_map/all_gather | solution.py:253
  515.2 91.5 %reduce-scatter.17.cloned.1.call-start = ((), (), s32[]{:S(2)}) async-start(), calls=%async_computation.17 | async-start | bytes 2621440 | tf_op jit(solution)/shard_map/reduce_scatter | solution.py:273
  561.2 7.8 copy-start.86
  571.9 34.9 %copy-start.15 = (bf16[256,1024]{1,0:T(8,128)(2,1)S(1)}, bf16[256,1024]{1,0:T(8,128)(2,1)}, u32[]{:S(2)}) copy-start(bf16[256,1024]{1,0:T(8,128)(2,1)} %reduce-scatter.13.cloned.1.call-done) | copy-start | bytes 1572868
  575.1 33.7 %copy-start.28 = (bf16[256,1024]{1,0:T(8,128)(2,1)S(1)}, bf16[256,1024]{1,0:T(8,128)(2,1)}, u32[]{:S(2)}) copy-start(bf16[256,1024]{1,0:T(8,128)(2,1)} %param.21) | copy-start | bytes 1572868
  575.2 109.4 %all-gather.20.cloned.1.call-start = ((), (), s32[]{:S(2)}) async-start(), calls=%async_computation.18 | async-start | bytes 4718592 | tf_op jit(solution)/shard_map/all_gather | solution.py:291
  611.0 79.0 %copy-start.9 = (bf16[2048,2,64]{0,2,1:T(8,128)(2,1)S(1)}, bf16[2048,2,64]{0,2,1:T(8,128)(2,1)}, u32[]{:S(2)}) copy-start(bf16[2048,2,64]{0,2,1:T(8,128)(2,1)} %copy-done.8) | copy-start | bytes 1572868
  611.0 282.7 %reduce-scatter.19.cloned.1.call-start = ((), (), s32[]{:S(2)}) async-start(), calls=%async_computation.19 | async-start | bytes 4718592 | tf_op jit(solution)/shard_map/reduce_scatter | solution.py:327
  807.4 120.6 %reduce-scatter.15.cloned.1.call-start = ((), (), s32[]{:S(2)}) async-start(), calls=%async_computation.15 | async-start | bytes 2621440 | tf_op jit(solution)/shard_map/reduce_scatter | solution.py:233
  807.4 86.3 %copy-start.64 = (f32[1,1024]{1,0:T(1,128)S(1)}, f32[1,1024]{1,0:T(1,128)}, u32[]{:S(2)}) copy-start(f32[1,1024]{1,0:T(1,128)} %copy-done.63) | copy-start | bytes 12292
  807.4 86.3 %copy-start.74 = (f32[256]{0:T(256)S(1)}, f32[256]{0:T(256)}, u32[]{:S(2)}) copy-start(f32[256]{0:T(256)} %copy-done.73) | copy-start | bytes 3076
  807.4 88.2 %copy-start.82 = (f32[256]{0:T(256)S(1)}, f32[256]{0:T(256)}, u32[]{:S(2)}) copy-start(f32[256]{0:T(256)} %copy-done.81) | copy-start | bytes 3076
  807.5 120.6 %copy-start.16 = (bf16[256,1024]{1,0:T(8,128)(2,1)S(1)}, bf16[256,1024]{1,0:T(8,128)(2,1)}, u32[]{:S(2)}) copy-start(bf16[256,1024]{1,0:T(8,128)(2,1)} %reduce-scatter.13.cloned.1.call-done) | copy-start | bytes 1572868
  807.5 120.6 %copy-start.27 = (bf16[256,1024]{1,0:T(8,128)(2,1)S(1)}, bf16[256,1024]{1,0:T(8,128)(2,1)}, u32[]{:S(2)}) copy-start(bf16[256,1024]{1,0:T(8,128)(2,1)} %reduce-scatter.17.cloned.1.call-done) | copy-start | bytes 1572868
  812.5 141.3 %all-gather.22.cloned.1.call-start = ((), (), s32[]{:S(2)}) async-start(), calls=%async_computation.20 | async-start | bytes 2621440 | tf_op jit(solution)/shard_map/all_gather | solution.py:253
  931.0 69.1 %copy-start.17 = (f32[256,1024]{1,0:T(8,128)}, f32[256,1024]{1,0:T(8,128)S(1)}, u32[]{:S(2)}) copy-start(f32[256,1024]{1,0:T(8,128)S(1)} %get-tuple-element.457) | copy-start | bytes 3145732
  931.1 66.9 %reduce-scatter.21.cloned.1.call-start = ((), (), s32[]{:S(2)}) async-start(), calls=%async_computation.21 | async-start | bytes 2621440 | tf_op jit(solution)/shard_map/reduce_scatter | solution.py:273
  953.8 6.5 copy-start.87
  963.2 34.8 %copy-start.4 = (bf16[256,1024]{1,0:T(8,128)(2,1)S(1)}, bf16[256,1024]{1,0:T(8,128)(2,1)}, u32[]{:S(2)}) copy-start(bf16[256,1024]{1,0:T(8,128)(2,1)} %param.20) | copy-start | bytes 1572868
  963.2 34.8 %copy-start.11 = (bf16[256,1024]{1,0:T(8,128)(2,1)S(1)}, bf16[256,1024]{1,0:T(8,128)(2,1)}, u32[]{:S(2)}) copy-start(bf16[256,1024]{1,0:T(8,128)(2,1)} %reduce-scatter.9.cloned.1.call-done) | copy-start | bytes 1572868
  963.2 34.8 %copy-start.58 = (f32[1,1024]{1,0:T(1,128)S(1)}, f32[1,1024]{1,0:T(1,128)}, u32[]{:S(2)}) copy-start(f32[1,1024]{1,0:T(1,128)} %copy-done.57) | copy-start | bytes 12292
  963.2 34.8 %copy-start.66 = (f32[256]{0:T(256)S(1)}, f32[256]{0:T(256)}, u32[]{:S(2)}) copy-start(f32[256]{0:T(256)} %copy-done.65) | copy-start | bytes 3076
  963.2 36.9 %copy-start.80 = (f32[256]{0:T(256)S(1)}, f32[256]{0:T(256)}, u32[]{:S(2)}) copy-start(f32[256]{0:T(256)} %copy-done.79) | copy-start | bytes 3076
  966.4 109.6 %all-gather.24.cloned.1.call-start = ((), (), s32[]{:S(2)}) async-start(), calls=%async_computation.22 | async-start | bytes 4718592 | tf_op jit(solution)/shard_map/all_gather | solution.py:291
  1000.1 6.6 copy-start.75
  1002.4 355.4 %all-reduce.6.cloned.1.call-start = ((), (), s32[]{:S(2)}) async-start(), calls=%async_computation.24 | async-start | bytes 17301504 | tf_op jit(solution)/shard_map/psum | solution.py:357
  1031.4 44.5 %copy-start.52 = (bf16[2,128,1024]{2,1,0:T(8,128)(2,1)S(1)}, bf16[2,128,1024]{2,1,0:T(8,128)(2,1)}, u32[]{:S(2)}) copy-start(bf16[2,128,1024]{2,1,0:T(8,128)(2,1)} %param.27) | copy-start | bytes 1572868
  1031.5 49.8 %copy-start.1 = (bf16[2048,2,64]{0,2,1:T(8,128)(2,1)S(1)}, bf16[2048,2,64]{0,2,1:T(8,128)(2,1)}, u32[]{:S(2)}) copy-start(bf16[2048,2,64]{0,2,1:T(8,128)(2,1)} %copy-done) | copy-start | bytes 1572868
  1031.5 49.8 %copy-start.7 = (bf16[2048,2,64]{0,2,1:T(8,128)(2,1)S(1)}, bf16[2048,2,64]{0,2,1:T(8,128)(2,1)}, u32[]{:S(2)}) copy-start(bf16[2048,2,64]{0,2,1:T(8,128)(2,1)} %copy-done.6) | copy-start | bytes 1572868
  1031.5 380.2 %all-reduce.8.cloned.1.call-start = ((), (), s32[]{:S(2)}) async-start(), calls=%async_computation.25 | async-start | bytes 4194304 | tf_op jit(solution)/shard_map/psum | solution.py:351
  1081.3 111.8 %copy-start.22 = (bf16[4,512,128]{2,1,0:T(8,128)(2,1)S(1)}, bf16[4,512,128]{2,1,0:T(8,128)(2,1)}, u32[]{:S(2)}) copy-start(bf16[4,512,128]{2,1,0:T(8,128)(2,1)} %copy-done.21) | copy-start | bytes 1572868
  1190.1 6.9 copy-start.24
  1190.1 6.9 copy-start.40
  1210.3 293.5 %reduce-scatter.23.cloned.1.call-start = ((), (), s32[]{:S(2)}) async-start(), calls=%async_computation.23 | async-start | bytes 4718592 | tf_op jit(solution)/shard_map/reduce_scatter | solution.py:327
  1369.5 134.3 %copy-start.5 = (bf16[256,1024]{1,0:T(8,128)(2,1)S(1)}, bf16[256,1024]{1,0:T(8,128)(2,1)}, u32[]{:S(2)}) copy-start(bf16[256,1024]{1,0:T(8,128)(2,1)} %param.20) | copy-start | bytes 1572868
  1369.5 134.3 %copy-start.62 = (f32[1,1024]{1,0:T(1,128)S(1)}, f32[1,1024]{1,0:T(1,128)}, u32[]{:S(2)}) copy-start(f32[1,1024]{1,0:T(1,128)} %copy-done.61) | copy-start | bytes 12292
  1369.5 134.3 %copy-start.72 = (f32[256]{0:T(256)S(1)}, f32[256]{0:T(256)}, u32[]{:S(2)}) copy-start(f32[256]{0:T(256)} %copy-done.71) | copy-start | bytes 3076
  1369.5 135.8 %copy-start.78 = (f32[256]{0:T(256)S(1)}, f32[256]{0:T(256)}, u32[]{:S(2)}) copy-start(f32[256]{0:T(256)} %copy-done.77) | copy-start | bytes 3076
  1369.5 135.8 %copy-start.69 = (f32[1024]{0:T(1024)S(1)}, f32[1024]{0:T(1024)}, u32[]{:S(2)}) copy-start(f32[1024]{0:T(1024)} %get-tuple-element.367) | copy-start | bytes 12292
  1369.5 176.3 %copy-start.12 = (bf16[256,1024]{1,0:T(8,128)(2,1)S(1)}, bf16[256,1024]{1,0:T(8,128)(2,1)}, u32[]{:S(2)}) copy-start(bf16[256,1024]{1,0:T(8,128)(2,1)} %reduce-scatter.9.cloned.1.call-done) | copy-start | bytes 1572868
  1369.5 176.3 %copy-start.18 = (f32[256,1024]{1,0:T(8,128)S(1)}, f32[256,1024]{1,0:T(8,128)}, u32[]{:S(2)}) copy-start(f32[256,1024]{1,0:T(8,128)} %copy-done.17) | copy-start | bytes 3145732
  1369.6 176.3 %copy-start.29 = (bf16[256,1024]{1,0:T(8,128)(2,1)S(1)}, bf16[256,1024]{1,0:T(8,128)(2,1)}, u32[]{:S(2)}) copy-start(bf16[256,1024]{1,0:T(8,128)(2,1)} %reduce-scatter.21.cloned.1.call-done) | copy-start | bytes 1572868
  1369.6 176.3 %copy-start.59 = (f32[1,1024]{1,0:T(1,128)S(1)}, f32[1,1024]{1,0:T(1,128)}, u32[]{:S(2)}) copy-start(f32[1,1024]{1,0:T(1,128)} %copy-done.57) | copy-start | bytes 12292
  1369.6 176.3 %copy-start.67 = (f32[256]{0:T(256)S(1)}, f32[256]{0:T(256)}, u32[]{:S(2)}) copy-start(f32[256]{0:T(256)} %copy-done.65) | copy-start | bytes 3076
  1369.6 176.3 %copy-start.76 = (f32[256]{0:T(256)S(1)}, f32[256]{0:T(256)}, u32[]{:S(2)}) copy-start(f32[256]{0:T(256)} %copy-done.75) | copy-start | bytes 3076
  1411.7 6.3 copy-start.53
  (61 other events, 170.0 us)
Sparse Core Ops, SparseCore 0:
  12.6 76.1 all-gather.9
  141.3 86.3 reduce-scatter.8
  231.2 22.3 all-gather.11
  265.4 31.4 reduce-scatter.10
  299.4 73.4 all-gather.13
  425.0 86.1 reduce-scatter.12
  514.6 22.3 all-gather.15
  538.6 22.5 all-gather.17
  575.3 31.3 reduce-scatter.16
  611.1 73.3 all-gather.19
  807.5 86.1 reduce-scatter.18
  896.8 31.1 reduce-scatter.14
  931.2 22.6 all-gather.21
  966.5 31.4 reduce-scatter.20
  1002.5 73.4 all-gather.23
  1081.3 276.4 all-reduce.5
  1360.8 50.9 all-reduce.7
  1415.6 88.1 reduce-scatter.22
where the time goes:
time: 1570 us; the launch traced here: 1560 us
  waiting for transfers between devices  967 us (62%)
  matrix products  246 us (16%)
  other arithmetic  126 us (8%)
  local copies, waits for them, and re-layouts  108 us (7%)
  blocking collectives  63.1 us (4%)
  loops' own time  27.3 us (2%)
  between operations  16.1 us (1%)
    reduce_scatter x2, waiting for transfers between devices, per_device(): lax.psum_scatter(rows_product(attended, w_out[layer_index]).astype(jnp.bf...  172 us
    reduce_scatter x2, waiting for transfers between devices, per_device(): lax.psum_scatter(rows_back((query_raw, key_raw, value_raw), (w_query[laye...  166 us
    psum x1, waiting for transfers between devices, per_device(): lax.psum(stacked(gate_grads).astype(jnp.bfloat16), 'heads')  140 us
    all_gather x2, waiting for transfers between devices, per_device(): gathered = lax.all_gather(attn_normed, 'heads', axis=0, tiled=True)  120 us
    all_gather x2, waiting for transfers between devices, per_device(): lax.all_gather(middle_back.astype(jnp.bfloat16), 'heads', axis=0, tiled=T...  118 us
    reduce_scatter x2, waiting for transfers between devices, per_device(): lax.psum_scatter(rows_product(hidden, w_down[layer_index]).astype(jnp.bfl...  63.9 us
    reduce_scatter x2, waiting for transfers between devices, per_device(): lax.psum_scatter(rows_back((gate_back, up_back), (w_gate[layer_index], w_...  63.1 us
    dynamic_update_slice x16, local copies, waits for them, and re-layouts, attention_backward(): lax.scan(one_block, (empty_heads, empty_heads), jnp.arange(group_rows //...  51.2 us
  transfers between devices with their start and end apart: 18, of which 18 were waited for; matrix products, arithmetic and copies ran while one was open for 13% of the time, Pallas kernels for 0%

commit v1 on v0

v1 whole, which is shorter than its diff:
```python
import functools

import jax
import jax.numpy as jnp
import numpy as np
from jax import lax
from jax.experimental import pallas as pl
from jax.experimental.pallas import tpu as pltpu
from jax.sharding import Mesh
from jax.sharding import PartitionSpec as P

HEAD_DIM = 64
SEQ_UNIT = 1024
EPSILON = 1e-06
THETA = 10000.0
NEG_LARGE = -1e30
BF16 = jnp.bfloat16
F32 = jnp.float32
VMEM_BYTES = 40 * 1024 * 1024

NT = (((1,), (1,)), ((), ()))
TN = (((0,), (0,)), ((), ()))


def swap(value, axes):
    axes = tuple(axes)
    size = 2 ** len(axes)
    return lax.ppermute(
        value, axes if len(axes) > 1 else axes[0], [(i, size - 1 - i) for i in range(size)]
    )


def axes_of(bits, axes):
    count = len(axes)
    return tuple(a for n, a in enumerate(axes) if bits >> (count - 1 - n) & 1)


def gather(value, axes, core):
    if len(axes) == 2:
        half = value.shape[-1] // 2
        low = swap(value, axes[1:])
        high = swap(value, axes[:1])
        both = jnp.concatenate(
            [swap(low[..., :half], axes[:1]), swap(high[..., half:], axes[1:])], axis=-1
        )
        chips = [value, low, high, both]
    else:
        chips = [value] + [swap(value, axes_of(i, axes)) for i in range(1, 2 ** len(axes))]
    return jnp.stack([jnp.stack(chips), jnp.stack([swap(c, (core,)) for c in chips])])


def scatter_sum(parts, axes, core):
    mine = parts[0].astype(F32) + swap(parts[1], (core,)).astype(F32)
    sent = mine.astype(BF16)
    total = mine[0]
    for i in range(1, 2 ** len(axes)):
        total = total + swap(sent[i], axes_of(i, axes)).astype(F32)
    return total


def heads_to_tokens(blocks, axes, core):
    other = swap(blocks[1], (core,))
    pairs = jnp.stack([blocks[0], other])
    chips = [pairs[:, 0]] + [
        swap(pairs[:, i], axes_of(i, axes)) for i in range(1, 2 ** len(axes))
    ]
    stacked = jnp.stack(chips, axis=1)
    count = stacked.shape[0] * stacked.shape[1]
    rows, width = stacked.shape[2:]
    return stacked.reshape(count, rows, width).transpose(1, 0, 2).reshape(rows, count * width)


def tokens_to_heads(rows_all, axes, core):
    chip_count = 2 ** len(axes)
    rows = rows_all.shape[0]
    width = rows_all.shape[1] // (2 * chip_count)
    blocks = rows_all.reshape(rows, 2, chip_count, width).transpose(1, 2, 0, 3)
    chips = [blocks[:, 0]] + [
        swap(blocks[:, i], axes_of(i, axes)) for i in range(1, chip_count)
    ]
    stacked = jnp.stack(chips, axis=1)
    return jnp.stack([stacked[0], swap(stacked[1], (core,))])


def exchange_sum(value, axes):
    for axis in axes:
        value = (value.astype(F32) + swap(value, (axis,)).astype(F32)).astype(BF16)
    return value


TURN = [(0, 0), (1, 2), (2, 1), (3, 3)]
CROSS = [(0, 1), (1, 3), (2, 0), (3, 2)]
CROSS_BACK = [(b, a) for a, b in CROSS]


def compiler_params():
    return pltpu.CompilerParams(vmem_limit_bytes=VMEM_BYTES)


VMEM = functools.partial(pl.BlockSpec, memory_space=pltpu.VMEM)
SMEM = functools.partial(pl.BlockSpec, memory_space=pltpu.SMEM)


def half_turn(value):
    width = value.shape[-1]
    halfway = HEAD_DIM // 2
    if width == HEAD_DIM:
        return jnp.concatenate([value[:, halfway:], value[:, :halfway]], axis=-1)
    lane = lax.broadcasted_iota(jnp.int32, value.shape, 1)
    return jnp.where(
        lane % HEAD_DIM < halfway,
        pltpu.roll(value, width - halfway, 1),
        pltpu.roll(value, halfway, 1),
    )


def head_masked(value, head):
    if value.shape[-1] == HEAD_DIM:
        return value
    lane = lax.broadcasted_iota(jnp.int32, value.shape, 1)
    return jnp.where(lane // HEAD_DIM == head, value, jnp.zeros_like(value))


def project_kernel(mixed, chips, rows, width, *refs):
    ids, normed, weights, cosine, sine = refs[:5]
    first = refs[5] if mixed else None
    queries, keys, values = refs[-3:]
    for core in range(2):
        block = normed[core].reshape(chips * rows, normed.shape[-1])
        raw = jnp.dot(block, weights[...], preferred_element_type=F32)
        for chip in range(chips):
            place = (chip ^ ids[0]) * 2 + (core ^ ids[1])
            at = pl.ds(pl.multiple_of(place * rows, rows), rows)
            piece = raw[chip * rows : (chip + 1) * rows]
            query, key, value = (piece[:, n * width : (n + 1) * width] for n in range(3))
            cos, sin = cosine[at, :], sine[at, :]
            queries[at, :] = ((query * cos + half_turn(query) * sin) * HEAD_DIM**-0.5).astype(BF16)
            keys[at, :] = (key * cos + half_turn(key) * sin).astype(BF16)
            if mixed:
                value = 0.5 * value + 0.5 * first[at, :].astype(F32)
            values[at, :] = value.astype(BF16)


def project(ids, normed, weights, cosine, sine, first):
    _, chips, rows, depth = normed.shape
    width = weights.shape[1] // 3
    count = 2 * chips * rows
    out = jax.ShapeDtypeStruct((count, width), BF16)
    operands = (ids, normed, weights, cosine, sine) + (() if first is None else (first,))
    return pl.pallas_call(
        functools.partial(project_kernel, first is not None, chips, rows, width),
        out_shape=(out, out, out),
        in_specs=[SMEM()] + [VMEM()] * (len(operands) - 1),
        out_specs=(VMEM(),) * 3,
        compiler_params=compiler_params(),
        cost_estimate=pl.CostEstimate(
            flops=2 * count * depth * 3 * width,
            bytes_accessed=2 * count * depth + 6 * depth * width + 14 * count * width,
            transcendentals=0,
        ),
        name="project_heads",
    )(*operands)


def attend_kernel(number, unit_count, chips, rows, width, *refs):
    ids = refs[0]
    queries = refs[1]
    key_refs = refs[2 : 3 + number]
    value_refs = refs[3 + number : 4 + 2 * number]
    attended, log_totals = refs[-2:]
    heads = width // HEAD_DIM
    block = 2 * rows
    count = chips * block
    units = max(count // SEQ_UNIT, 1)
    unit_rows = count // units

    def allowed(query_unit, key_unit):
        return ids[2 + query_unit * unit_count + key_unit] > 0

    for chip in range(chips):
        first = chip * block
        own_unit = number * units + first // unit_rows
        segments = []
        for part in range(number):
            for unit in range(units):
                segments.append((part, unit * unit_rows, unit_rows, part * units + unit, False))
        for unit in range(first // unit_rows):
            segments.append((number, unit * unit_rows, unit_rows, number * units + unit, False))
        unit_start = first // unit_rows * unit_rows
        if first > unit_start:
            segments.append((number, unit_start, first - unit_start, None, False))
        segments.append((number, first, block, None, True))
        query_all = queries[first : first + block, :]
        outs = None
        lane = lax.broadcasted_iota(jnp.int32, (block, 128), 1)
        totals_wide = jnp.zeros((block, 128), F32)
        for head in range(heads):
            query = head_masked(query_all, head)
            scores, biases, tops = [], [], []
            for part, start, length, unit, diagonal in segments:
                score = lax.dot_general(
                    query, key_refs[part][start : start + length, :], NT,
                    preferred_element_type=F32,
                )
                if diagonal:
                    row = lax.broadcasted_iota(jnp.int32, score.shape, 0)
                    column = lax.broadcasted_iota(jnp.int32, score.shape, 1)
                    score = jnp.where(column <= row, score, NEG_LARGE)
                bias = 0.0 if unit is None else jnp.where(allowed(own_unit, unit), 0.0, NEG_LARGE)
                scores.append(score)
                biases.append(bias)
                tops.append(jnp.max(score, axis=1, keepdims=True) + bias)
            highest = functools.reduce(jnp.maximum, tops)
            summed, total = None, None
            for (part, start, length, unit, diagonal), score, bias in zip(segments, scores, biases):
                weight = jnp.exp(score - (highest - bias))
                narrow = weight.astype(BF16)
                value = value_refs[part][start : start + length, :]
                if heads > 1:
                    value_lane = lax.broadcasted_iota(jnp.int32, value.shape, 1)
                    value = jnp.where(value_lane // HEAD_DIM == head, value, jnp.ones_like(value))
                else:
                    part_total = jnp.sum(weight, axis=1, keepdims=True)
                    total = part_total if total is None else total + part_total
                product = jnp.dot(narrow, value, preferred_element_type=F32)
                summed = product if summed is None else summed + product
            if heads > 1:
                spread = pltpu.roll(summed, HEAD_DIM, 1)
                divided = head_masked(summed / spread, head)
                other = 1 - head
                total = spread if head == 0 else spread
                total = jnp.where(lane // HEAD_DIM == head, total, summed)
                logs = highest + jnp.log(total)
            else:
                divided = summed / total
                logs = jnp.broadcast_to(highest + jnp.log(total), (block, 128))
            outs = divided if outs is None else outs + divided
            totals_wide = jnp.where(lane == head, logs, totals_wide)
        rounded = outs.astype(BF16)
        place = chip ^ ids[0]
        for core in range(2):
            attended[core ^ ids[1], place] = rounded[core * rows : (core + 1) * rows]
        log_totals[:, first : first + block] = totals_wide.T[:8]


def attend(ids, unit_count, queries, keys, values, chips, rows):
    number = len(keys) - 1
    count, width = queries.shape
    heads = width // HEAD_DIM
    pairs = count * count // 2 + number * count * count
    return pl.pallas_call(
        functools.partial(attend_kernel, number, unit_count, chips, rows, width),
        out_shape=(
            jax.ShapeDtypeStruct((2, chips, rows, width), BF16),
            jax.ShapeDtypeStruct((8, count), F32),
        ),
        in_specs=[SMEM()] + [VMEM()] * (3 + 2 * number),
        out_specs=(VMEM(),) * 2,
        compiler_params=compiler_params(),
        cost_estimate=pl.CostEstimate(
            flops=heads * pairs * 256 * 4,
            bytes_accessed=2 * count * width * (4 + 2 * number),
            transcendentals=heads * pairs,
        ),
        name="attend_forward",
    )(ids, queries, *keys, *values)


def attend_back_kernel(number, last, unit_count, chips, rows, width, layer_first, *refs):
    refs = list(refs)
    ids = refs.pop(0)
    queries = refs.pop(0)
    key_refs = [refs.pop(0) for _ in range(number + 1)]
    value_refs = [refs.pop(0) for _ in range(number + 1)]
    attended, grads, log_totals, cosine, sine = (refs.pop(0) for _ in range(5))
    later_keys, later_values = (None, None) if last else (refs.pop(0), refs.pop(0))
    later_layer = refs.pop(0) if layer_first else None
    outs = refs.pop(0)
    earlier = [(refs.pop(0), refs.pop(0)) for _ in range(number)]
    grad_rows, inner, query_total, key_total, value_total = refs
    heads = width // HEAD_DIM
    block = 2 * rows
    count = chips * block
    units = max(count // SEQ_UNIT, 1)
    unit_rows = count // units

    def allowed(query_unit, key_unit):
        return ids[2 + query_unit * unit_count + key_unit] > 0

    def place_of(core, chip):
        place = (chip ^ ids[0]) * 2 + (core ^ ids[1])
        return pl.ds(pl.multiple_of(place * rows, rows), rows)

    for core in range(2):
        for chip in range(chips):
            at = place_of(core, chip)
            grad = grads[core, chip]
            grad_rows[at, :] = grad
            query_total[at, :] = grad.astype(F32) * attended[core, chip].astype(F32)
    turned = query_total[...].T
    for head in range(heads):
        inner[head : head + 1, :] = jnp.sum(
            turned[head * HEAD_DIM : (head + 1) * HEAD_DIM], axis=0, keepdims=True
        )
    query_total[...] = jnp.zeros_like(query_total)
    if last:
        key_total[...] = jnp.zeros_like(key_total)
        value_total[...] = jnp.zeros_like(value_total)
    else:
        key_total[...] = later_keys[...]
        value_total[...] = later_values[...]
    for key_out, value_out in earlier:
        key_out[...] = jnp.zeros_like(key_out)
        value_out[...] = jnp.zeros_like(value_out)

    def work(part, key_start, key_count, query_start, diagonal):
        keys, values = key_refs[part], value_refs[part]
        key_sum, value_sum = (key_total, value_total) if part == number else earlier[part]
        at = pl.ds(key_start, key_count)
        query_at = pl.ds(query_start, block)
        key, value = keys[at, :], values[at, :]
        key_part, value_part, query_part = None, None, None
        for head in range(heads):
            query = head_masked(queries[query_at, :], head)
            grad = head_masked(grad_rows[query_at, :], head)
            score = lax.dot_general(key, query, NT, preferred_element_type=F32)
            weight = jnp.exp(score - log_totals[head : head + 1, query_at])
            if diagonal:
                row = lax.broadcasted_iota(jnp.int32, score.shape, 0)
                column = lax.broadcasted_iota(jnp.int32, score.shape, 1)
                weight = jnp.where(row + (key_start - query_start) <= column, weight, 0.0)
            back = lax.dot_general(value, grad, NT, preferred_element_type=F32)
            score_back = (weight * (back - inner[head : head + 1, query_at])).astype(BF16)
            narrow = weight.astype(BF16)
            value_term = jnp.dot(narrow, grad, preferred_element_type=F32)
            key_term = jnp.dot(score_back, query, preferred_element_type=F32)
            query_term = lax.dot_general(
                score_back, head_masked(key, head), TN, preferred_element_type=F32
            )
            if head == 0:
                key_part, value_part, query_part = key_term, value_term, query_term
            else:
                key_part, value_part, query_part = (
                    key_part + key_term, value_part + value_term, query_part + query_term,
                )
        key_sum[at, :] += key_part
        value_sum[at, :] += value_part
        query_total[query_at, :] += query_part

    for unit in range(units):
        start = unit * unit_rows
        blocks = unit_rows // block
        own_unit = number * units + unit
        others = [(part, other) for part in range(number) for other in range(units)]
        others += [(number, other) for other in range(unit)]
        for part, other in others:
            @pl.when(allowed(own_unit, part * units + other))
            def _():
                @pl.loop(0, blocks)
                def _(index):
                    work(part, other * unit_rows, unit_rows, start + index * block, False)
        for index in range(blocks):
            if index:
                work(number, start, index * block, start + index * block, False)
            work(number, start + index * block, block, start + index * block, True)

    for core in range(2):
        for chip in range(chips):
            at = place_of(core, chip)
            cos, sin = cosine[at, :], sine[at, :]
            query = query_total[at, :] * HEAD_DIM**-0.5
            key = key_total[at, :]
            value = value_total[at, :]
            query = query * cos - half_turn(query) * sin
            key = key * cos - half_turn(key) * sin
            if layer_first:
                value = value + later_layer[core, chip, :, 2 * width :].astype(F32)
            else:
                value = value.astype(BF16).astype(F32) * 0.5
            outs[core, chip] = jnp.concatenate([query, key, value], axis=1).astype(BF16)


def attend_back(
    ids, unit_count, queries, keys, values, attended, grads, log_totals, cosine, sine, later,
    later_layer,
):
    number = len(keys) - 1
    last = later is None
    _, chips, rows, width = attended.shape
    count = queries.shape[0]
    heads = width // HEAD_DIM
    pairs = count * count // 2 + number * count * count
    operands = [ids, queries, *keys, *values, attended, grads, log_totals, cosine, sine]
    if not last:
        operands += list(later)
    if later_layer is not None:
        operands.append(later_layer)
    total = jax.ShapeDtypeStruct((count, width), F32)
    return pl.pallas_call(
        functools.partial(
            attend_back_kernel, number, last, unit_count, chips, rows, width,
            later_layer is not None,
        ),
        out_shape=(jax.ShapeDtypeStruct((2, chips, rows, 3 * width), BF16),)
        + (total,) * (2 * number),
        in_specs=[SMEM()] + [VMEM()] * (len(operands) - 1),
        out_specs=(VMEM(),) * (1 + 2 * number),
        scratch_shapes=[
            pltpu.VMEM((count, width), BF16),
            pltpu.VMEM((8, count), F32),
            pltpu.VMEM((count, width), F32),
            pltpu.VMEM((count, width), F32),
            pltpu.VMEM((count, width), F32),
        ],
        compiler_params=compiler_params(),
        cost_estimate=pl.CostEstimate(
            flops=heads * pairs * 256 * 10,
            bytes_accessed=2 * count * width * 20,
            transcendentals=heads * pairs,
        ),
        name="attend_backward",
    )(*operands)


def rms_factor(values):
    return lax.rsqrt(jnp.mean(values * values, axis=-1, keepdims=True) + EPSILON)


def normed_rows(values, gain):
    return (values * rms_factor(values) * gain).astype(BF16)


def norm_back(values, gain, back):
    factor = rms_factor(values)
    scaled = back * gain
    mean = jnp.mean(scaled * values, axis=-1, keepdims=True)
    gain_grad = jnp.sum(back * values * factor, axis=0)
    return factor * scaled - values * (factor * factor * factor * mean), gain_grad


def matmul(left, right):
    return jnp.dot(left, right, preferred_element_type=F32)


def matmul_nt(left, right):
    return lax.dot_general(left, right, NT, preferred_element_type=F32)


def matmul_tn(left, right):
    return lax.dot_general(left, right, TN, preferred_element_type=F32)


def flat(blocks):
    return blocks.reshape(-1, blocks.shape[-1])


def per_device(
    head_axes, hid_axes, inputs, cotangent, segments, attn_gain, w_query, w_key, w_value, w_out,
    mlp_gain, w_gate, w_up, w_down,
):
    layers = w_query.shape[0]
    core = hid_axes[-1]
    group_axes = head_axes[1:]
    share_axes = hid_axes[:-1]
    chips = 2 ** len(group_axes)
    token_count = inputs.shape[0]
    rows = token_count // 2
    count = chips * token_count
    width = w_query.shape[2]
    units = max(count // SEQ_UNIT, 1)
    unit_count = 2 * units
    turn_axes = (head_axes[0], core)
    top = lax.axis_index(head_axes[0])
    core_at = lax.axis_index(core)
    chip_at = jnp.int32(0)
    for axis in group_axes:
        chip_at = chip_at * 2 + lax.axis_index(axis)

    def turn(value):
        return lax.ppermute(value, turn_axes, TURN)

    def take(value):
        own = lax.dynamic_slice_in_dim(value, top * rows, rows, 0)
        cross = lax.dynamic_slice_in_dim(value, (1 - top) * rows, rows, 0)
        own = lax.ppermute(own, turn_axes, TURN)
        cross = lax.ppermute(cross, turn_axes, CROSS)
        return [jnp.where(core_at == 0, own, cross), jnp.where(core_at == 0, cross, own)]

    def give(values):
        own = jnp.where(core_at == 0, values[0], values[1])
        cross = jnp.where(core_at == 0, values[1], values[0])
        own = lax.ppermute(own, turn_axes, TURN)
        cross = lax.ppermute(cross, turn_axes, CROSS_BACK)
        return jnp.where(
            top == 0,
            jnp.concatenate([own, cross], axis=0),
            jnp.concatenate([cross, own], axis=0),
        )

    number = turn(jnp.broadcast_to(segments[:1], (8, 128)))
    unit_axes = group_axes[: (units - 1).bit_length()]
    numbers = jnp.stack(
        [number] + [swap(number, axes_of(i, unit_axes)) for i in range(1, units)]
    )
    numbers = jnp.stack([numbers, swap(numbers, (core,))])[:, :, 0, 0]
    unit_at = chip_at // (chips // units)
    numbers = jnp.stack(
        [
            lax.dynamic_slice(numbers, (half ^ core_at, unit ^ unit_at), (1, 1))[0, 0]
            for half in range(2)
            for unit in range(units)
        ]
    )
    same = (numbers[:, None] == numbers[None, :]).astype(jnp.int32)
    ids = jnp.concatenate([jnp.stack([chip_at, core_at]).astype(jnp.int32), same.reshape(-1)])
    earlier_units = np.tril(np.ones((unit_count, unit_count), np.int32), -1)
    starts = jnp.sum(same * earlier_units, axis=1) * SEQ_UNIT
    frequency = np.float32(THETA) ** (-np.arange(HEAD_DIM // 2, dtype=np.float32) * 2 / HEAD_DIM)
    frequency = np.tile(frequency.astype(np.float32), 2 * width // HEAD_DIM)[None]
    signs = np.where(np.arange(width) % HEAD_DIM < HEAD_DIM // 2, -1.0, 1.0).astype(np.float32)
    within = np.arange(count, dtype=np.int32) % SEQ_UNIT
    cosines, sines = [], []
    for half in range(2):
        offset = jnp.repeat(starts[half * units : (half + 1) * units], count // units)
        angles = (offset + within).astype(F32)[:, None] * frequency
        cosines.append(jnp.cos(angles))
        sines.append(jnp.sin(angles) * signs)

    residual = [part.astype(F32) for part in take(inputs)]
    w_heads = [
        turn(jnp.concatenate([w_query[n], w_key[n], w_value[n]], axis=1)) for n in range(layers)
    ]
    w_out_all = [flat(gather(turn(w_out[n]), group_axes, core)) for n in range(layers)]

    stored = []
    first_values = [None, None]
    for layer in range(layers):
        kept = []
        keys, values = [], []
        for half in range(2):
            before = residual[half]
            gathered = gather(normed_rows(before, attn_gain[layer]), group_axes, core)
            queries, key, value = project(
                ids, gathered, w_heads[layer], cosines[half], sines[half], first_values[half]
            )
            keys.append(key)
            values.append(value)
            attended, log_totals = attend(
                ids, unit_count, queries, list(keys), list(values), chips, rows
            )
            attended_rows = heads_to_tokens(attended, group_axes, core)
            middle = before + matmul(attended_rows, w_out_all[layer])
            mixed = flat(gather(normed_rows(middle, mlp_gain[layer]), share_axes, core))
            gate = matmul(mixed, w_gate[layer])
            upward = matmul(mixed, w_up[layer])
            hidden = (gate * jax.nn.sigmoid(gate) * upward).astype(BF16)
            term = matmul(hidden, w_down[layer]).astype(BF16)
            term = term.reshape(2, -1, rows, term.shape[-1])
            residual[half] = middle + scatter_sum(term, share_axes, core)
            kept.append(
                dict(
                    before=before, gathered=gathered, queries=queries, attended=attended,
                    log_totals=log_totals, attended_rows=attended_rows, middle=middle, mixed=mixed,
                )
            )
        if layer == 0:
            first_values = values
        stored.append((kept, keys, values))
    block_out = give([part.astype(BF16) for part in residual])

    grad = [part.astype(F32) for part in take(cotangent)]
    attn_grads, out_grads, mlp_grads = [], [], []
    attn_gain_grads, mlp_gain_grads = [], []
    later_layer = [None, None]
    for layer in reversed(range(layers)):
        kept, keys, values = stored[layer]
        later = None
        sums = [None] * 7
        this_layer = [None, None]

        def accumulate(index, term):
            sums[index] = term if sums[index] is None else sums[index] + term

        for half in (1, 0):
            k = kept[half]
            down_in = flat(gather(grad[half].astype(BF16), share_axes, core))
            mixed = k["mixed"]
            gate = matmul(mixed, w_gate[layer])
            upward = matmul(mixed, w_up[layer])
            sigmoid = jax.nn.sigmoid(gate)
            hidden = (gate * sigmoid * upward).astype(BF16)
            hidden_grad = matmul_nt(down_in, w_down[layer])
            gate_back = (hidden_grad * upward * sigmoid * (1 + gate * (1 - sigmoid))).astype(BF16)
            up_back = (hidden_grad * gate * sigmoid).astype(BF16)
            term = (matmul_nt(gate_back, w_gate[layer]) + matmul_nt(up_back, w_up[layer])).astype(
                BF16
            )
            normed_back = scatter_sum(
                term.reshape(2, -1, rows, term.shape[-1]), share_axes, core
            )
            part, gain_part = norm_back(k["middle"], mlp_gain[layer], normed_back)
            accumulate(0, gain_part)
            middle_back = grad[half] + part
            attn_in = middle_back.astype(BF16)
            back_rows = matmul_nt(attn_in, w_out_all[layer]).astype(BF16)
            attended_back = tokens_to_heads(back_rows, group_axes, core)
            results = attend_back(
                ids, unit_count, k["queries"], keys[: half + 1], values[: half + 1],
                k["attended"], attended_back, k["log_totals"], cosines[half], sines[half],
                later, later_layer[half],
            )
            raws = results[0]
            later = results[1:]
            this_layer[half] = raws
            term = matmul_nt(flat(raws), w_heads[layer]).astype(BF16)
            normed_in = scatter_sum(
                term.reshape(2, chips, rows, term.shape[-1]), group_axes, core
            )
            part, gain_part = norm_back(k["before"], attn_gain[layer], normed_in)
            accumulate(1, gain_part)
            grad[half] = middle_back + part
            accumulate(2, matmul_tn(hidden, down_in))
            accumulate(3, matmul_tn(mixed, gate_back))
            accumulate(4, matmul_tn(mixed, up_back))
            accumulate(5, matmul_tn(k["attended_rows"], attn_in))
            accumulate(6, matmul_tn(flat(k["gathered"]), flat(raws)))
        later_layer = this_layer
        mlp_gain_grads.append(sums[0])
        attn_gain_grads.append(sums[1])
        mlp_grads.append(
            [lax.psum(part.astype(BF16), head_axes).astype(F32) for part in sums[2:5]]
        )
        out_grad = scatter_sum(
            sums[5].astype(BF16).reshape(2, chips, width, -1), group_axes, core
        )
        back_axes = (core,) + share_axes
        out_grads.append(exchange_sum(turn(out_grad.astype(BF16)), back_axes).astype(F32))
        attn_grads.append(exchange_sum(turn(sums[6].astype(BF16)), back_axes).astype(F32))

    input_grad = give([part.astype(BF16) for part in grad]).astype(F32)
    gains = lax.psum(
        jnp.stack(attn_gain_grads[::-1] + mlp_gain_grads[::-1]), head_axes + hid_axes
    )

    def stacked(parts):
        return jnp.stack(parts[::-1])

    return (
        block_out,
        input_grad,
        gains[:layers],
        stacked([part[:, :width] for part in attn_grads]),
        stacked([part[:, width : 2 * width] for part in attn_grads]),
        stacked([part[:, 2 * width :] for part in attn_grads]),
        stacked(out_grads),
        gains[layers:],
        stacked([part[1] for part in mlp_grads]),
        stacked([part[2] for part in mlp_grads]),
        stacked([part[0] for part in mlp_grads]),
    )


def solution(mesh):
    head_bits = (mesh.shape["heads"] - 1).bit_length()
    hid_bits = (mesh.shape["hid"] - 1).bit_length()
    head_axes = tuple(f"heads{n}" for n in range(head_bits))
    hid_axes = tuple(f"hid{n}" for n in range(hid_bits))
    binary = Mesh(mesh.devices.reshape((2,) * (head_bits + hid_bits)), head_axes + hid_axes)
    tokens = hid_axes + head_axes
    in_specs = (
        P(tokens, None),
        P(tokens, None),
        P(tokens),
        P(),
        P(None, None, head_axes),
        P(None, None, head_axes),
        P(None, None, head_axes),
        P(None, head_axes, None),
        P(),
        P(None, None, hid_axes),
        P(None, None, hid_axes),
        P(None, hid_axes, None),
    )
    out_specs = (
        P(tokens, None),
        P(tokens, None),
        P(),
        P(None, None, head_axes),
        P(None, None, head_axes),
        P(None, None, head_axes),
        P(None, head_axes, None),
        P(),
        P(None, None, hid_axes),
        P(None, None, hid_axes),
        P(None, hid_axes, None),
    )
    return jax.shard_map(
        functools.partial(per_device, head_axes, hid_axes),
        mesh=binary,
        in_specs=in_specs,
        out_specs=out_specs,
        check_vma=False,
    )
```

time: 1570 us -> 829 us (0.53)
  waiting for transfers between devices: 967 us -> 285 us
  starting transfers between devices: 1.92 us -> 202 us
  matrix products: 246 us -> 81.6 us
  other arithmetic: 126 us -> 72.8 us
  Pallas kernels: 0 us -> 52.9 us
  local copies, waits for them, and re-layouts: 108 us -> 56.1 us
  loops' own time: 27.3 us -> 0 us
    reduce_scatter x8 -> x0, waiting for transfers between devices: 465 us -> none  [the longest x2 172 us: per_device(): lax.psum_scatter(rows_product(attended, w_out[layer_index]).astype(jnp.bf...]
    all_gather x8 -> x0, waiting for transfers between devices: 320 us -> none  [the longest x2 120 us: per_device(): gathered = lax.all_gather(attn_normed, 'heads', axis=0, tiled=True)]
    ppermute x0 -> x170, waiting for transfers between devices: none -> 223 us  [the longest x153 223 us: swap(): lax.ppermute(value, axes if len(axes) > 1 else axes[0], [(i, size - 1 - i...]
    ppermute x0 -> x170, starting transfers between devices: none -> 202 us  [the longest x153 171 us: swap(): lax.ppermute(value, axes if len(axes) > 1 else axes[0], [(i, size - 1 - i...]
    dot_general x98 -> x56, matrix products: 246 us -> 81.6 us  [the longest x20 35 us: matmul_tn(): return lax.dot_general(left, right, TN, preferred_element_type=F32)]
    psum x2 -> x1, waiting for transfers between devices: 182 us -> 62.7 us  [per_device(): lax.psum(part.astype(BF16), head_axes).astype(F32)]
    pallas_call x0 -> x12, Pallas kernels: none -> 52.9 us  [the longest x4 23.2 us: attend_back(): pl.pallas_call(functools.partial(attend_back_kernel, number, last, unit_c...]
    dynamic_update_slice x32 -> x0, local copies, waits for them, and re-layouts: 52.3 us -> none  [the longest x16 51.2 us: attention_backward(): lax.scan(one_block, (empty_heads, empty_heads), jnp.arange(group_rows //...]
  transfers between devices with their start and end apart: 18 -> 171, of which waited for: 18 -> 60; matrix products, arithmetic and copies ran while one was open for 13% -> 21% of each run, Pallas kernels for 0% -> 6%
where the time goes in v1:
time: 829 us; the launch traced here: 820 us
  waiting for transfers between devices  285 us (34%)
  starting transfers between devices  202 us (24%)
  matrix products  81.6 us (10%)
  other arithmetic  72.8 us (9%)
  local copies, waits for them, and re-layouts  56.1 us (7%)
  Pallas kernels  52.9 us (6%)
  blocking collectives  48.4 us (6%)
  between operations  20.3 us (2%)
    ppermute x153, waiting for transfers between devices, swap(): lax.ppermute(value, axes if len(axes) > 1 else axes[0], [(i, size - 1 - i...  223 us
    ppermute x153, starting transfers between devices, swap(): lax.ppermute(value, axes if len(axes) > 1 else axes[0], [(i, size - 1 - i...  171 us
    psum x1, waiting for transfers between devices, per_device(): lax.psum(part.astype(BF16), head_axes).astype(F32)  62.7 us
    psum x1, blocking collectives, per_device(): lax.psum(jnp.stack(attn_gain_grads[::-1] + mlp_gain_grads[::-1]), head_ax...  48.4 us
    dot_general x20, matrix products, matmul_tn(): return lax.dot_general(left, right, TN, preferred_element_type=F32)  35 us
    dot_general x20, matrix products, matmul_nt(): return lax.dot_general(left, right, NT, preferred_element_type=F32)  25.3 us
    pallas_call x4, Pallas kernels, attend_back(): pl.pallas_call(functools.partial(attend_back_kernel, number, last, unit_c...  23.2 us
    pallas_call x4, Pallas kernels, attend(): pl.pallas_call(functools.partial(attend_kernel, number, unit_count, chips...  21.7 us
  transfers between devices with their start and end apart: 171, of which 60 were waited for; matrix products, arithmetic and copies ran while one was open for 21% of the time, Pallas kernels for 6%

profile of v1, /device:TPU:0, one launch (start us, length us, event | category | flops | bytes accessed | tf_op | source)
XLA Modules:
  0.0 819.7 jit_solution(1539684608666204720)
XLA Ops:
  11.7 5.4 collective-permute-start.1
  25.0 3.2 collective-permute-start.3
  29.1 3.6 collective-permute-start.17
  43.3 3.7 fusion.75
  47.6 3.0 collective-permute-done.58
  51.0 3.1 collective-permute-done.4
  59.8 4.0 collective-permute-done.19
  70.2 2.8 collective-permute-done.7
  75.9 3.4 collective-permute-start.8
  84.5 13.6 %collective-permute-start.25 = (bf16[128,1024]{1,0:T(8,128)(2,1)S(1)}, bf16[128,1024]{1,0:T(8,128)(2,1)S(1)}, u32[]{:S(2)}, u32[]{:S(2)}) collective-permute-start(bf16[128,1024]{1,0:T(8,128)(2,1)S(1)} %constant_dynamic-update-slice_fusion.2), channel_id=1, source_target_pairs={{0,1},{1,0},{2,3},{3,2},{4,5},{5,4},{6,7},{7,6},{8,9},{9,8},{10,11... | collective-permute-start | bytes 786440 | tf_op jit(solution)/shard_map/ppermute | solution.py:28
  100.1 4.0 attend_forward.4
  106.2 6.9 attend_forward.6
  136.0 3.6 collective-permute-start.44
  170.0 7.3 collective-permute-done.74
  178.1 6.5 collective-permute-done.30
  189.5 4.8 collective-permute-done.32
  204.1 2.9 collective-permute-done.33
  207.0 9.0 %collective-permute-start.37 = (bf16[128,1024]{1,0:T(8,128)(2,1)S(1)}, bf16[128,1024]{1,0:T(8,128)(2,1)S(1)}, u32[]{:S(2)}, u32[]{:S(2)}) collective-permute-start(bf16[128,1024]{1,0:T(8,128)(2,1)S(1)} %collective-permute-done.32), channel_id=1, source_target_pairs={{0,1},{1,0},{2,3},{3,2},{4,5},{5,4},{6,7},{7,6},{8,9},{9,8},{10,11... | collective-permute-start | bytes 786440 | tf_op jit(solution)/shard_map/ppermute | solution.py:28
  216.3 4.8 collective-permute-start.38
  225.9 4.0 attend_forward.5
  233.7 6.9 attend_forward.7
  265.2 5.1 collective-permute-done.53
  305.7 9.8 %collective-permute-done.109 = bf16[128,1024]{1,0:T(8,128)(2,1)S(1)} collective-permute-done((bf16[128,1024]{1,0:T(8,128)(2,1)S(1)}, bf16[128,1024]{1,0:T(8,128)(2,1)S(1)}, u32[]{:S(2)}, u32[]{:S(2)}) %collective-permute-start.109) | collective-permute-done | bytes 262176 | tf_op jit(solution)/shard_map/ppermute | solution.py:28
  315.5 5.6 collective-permute-done.100
  323.5 2.7 fusion.146
  329.5 2.8 collective-permute-start.93
  332.3 3.6 collective-permute-start.92
  349.2 3.1 add_convert_fusion
  362.1 6.2 attend_backward.4
  369.7 5.5 attend_backward.5.refs_11_
  378.9 6.9 collective-permute-start.114
  399.7 6.5 collective-permute-start.116
  409.3 4.2 collective-permute-done.165
  413.6 3.8 collective-permute-start.129
  419.7 5.0 collective-permute-done.116
  425.4 5.6 collective-permute-done.130
  431.0 7.5 collective-permute-done.129
  443.4 6.6 collective-permute-done.131
  451.4 4.3 collective-permute-done.118
  489.7 4.5 collective-permute-done.122
  494.2 5.2 collective-permute-done.135
  503.3 2.7 fusion.139
  522.1 3.1 add_convert_fusion.1
  525.1 5.2 collective-permute-done.125
  530.9 3.3 collective-permute-done.124
  534.3 4.7 collective-permute-done.138
  539.0 2.9 collective-permute-done.137
  543.8 6.0 attend_backward.6
  549.8 5.5 attend_backward.7
  561.5 9.1 %collective-permute-start.144 = (bf16[4,128,1024]{2,1,0:T(8,128)(2,1)S(1)}, bf16[4,128,1024]{2,1,0:T(8,128)(2,1)S(1)}, u32[]{:S(2)}, u32[]{:S(2)}) collective-permute-start(bf16[4,128,1024]{2,1,0:T(8,128)(2,1)S(1)} %bitcast.841), channel_id=1, source_target_pairs={{0,1},{1,0},{2,3},{3,2},{4,5},{5,4},{6,7},{7,6},{8,9},{9,8},{10,11... | collective-permute-start | bytes 3145736 | tf_op jit(solution)/shard_map/ppermute | solution.py:28
  573.6 3.4 collective-permute-start.159
  585.7 13.6 %collective-permute-done.159 = bf16[128,1024]{1,0:T(8,128)(2,1)S(1)} collective-permute-done((bf16[128,1024]{1,0:T(8,128)(2,1)S(1)}, bf16[128,1024]{1,0:T(8,128)(2,1)S(1)}, u32[]{:S(2)}, u32[]{:S(2)}) %collective-permute-start.159) | collective-permute-done | bytes 262176 | tf_op jit(solution)/shard_map/ppermute | solution.py:28
  600.6 4.2 collective-permute-done.158
  608.7 7.8 collective-permute-done.147
  616.4 5.5 collective-permute-start.151
  622.0 3.9 collective-permute-done.146
  627.4 11.4 %collective-permute-done.143 = bf16[128,1024]{1,0:T(8,128)(2,1)S(1)} collective-permute-done((bf16[128,1024]{1,0:T(8,128)(2,1)S(1)}, bf16[128,1024]{1,0:T(8,128)(2,1)S(1)}, u32[]{:S(2)}, u32[]{:S(2)}) %collective-permute-start.143) | collective-permute-done | bytes 262176 | tf_op jit(solution)/shard_map/ppermute | solution.py:28
  638.9 14.6 %collective-permute-done.142 = bf16[128,1024]{1,0:T(8,128)(2,1)S(1)} collective-permute-done((bf16[128,1024]{1,0:T(8,128)(2,1)S(1)}, bf16[128,1024]{1,0:T(8,128)(2,1)S(1)}, u32[]{:S(2)}, u32[]{:S(2)}) %collective-permute-start.142) | collective-permute-done | bytes 262176 | tf_op jit(solution)/shard_map/ppermute | solution.py:28
  657.7 48.4 %psum.49 = f32[4,1024]{1,0:T(4,128)S(1)} all-reduce(f32[4,1024]{1,0:T(4,128)S(1)} %pad_maximum_fusion.35), channel_id=1, replica_groups=mesh['heads0'=2,'heads1'=2,'heads2'=2,'hid0'=2,'hid1'=2] {'heads0','head..., use_global_device_ids=true, to_apply=%region_25.26 | all-reduce | flops 4096 | bytes 32768 | tf_op jit(solution)/shard_map/psum | solution.py:641
  711.8 21.9 %collective-permute-done.162 = bf16[128,1024]{1,0:T(8,128)(2,1)S(1)} collective-permute-done((bf16[128,1024]{1,0:T(8,128)(2,1)S(1)}, bf16[128,1024]{1,0:T(8,128)(2,1)S(1)}, u32[]{:S(2)}, u32[]{:S(2)}) %collective-permute-start.162) | collective-permute-done | bytes 262176 | tf_op jit(solution)/shard_map/ppermute | solution.py:28
  739.2 62.7 %all-reduce.3.cloned.1.call-done = (bf16[1,1024,704]{1,2,0:T(8,128)(2,1)}, bf16[1,1024,704]{1,2,0:T(8,128)(2,1)}, bf16[1,1024,704]{1,2,0:T(8,128)(2,1)}, bf16[1,...) async-done(((bf16[1,1024,704]{1,2,0:T(8,128)(2,1)}, bf16[1,1024,704]{1,2,0:T(8,128)(2,1)}, bf16[1,1024,704]{1,2,0:T(8,128)(2,1)}, ...) | async-done | bytes 8650768 | tf_op jit(solution)/shard_map/psum | solution.py:631
  801.9 4.8 maximum_convert_fusion
  806.8 2.9 maximum_convert_fusion.1
  809.7 2.9 maximum_convert_fusion.2
  (903 shorter events, 338.2 us)
Async XLA Ops:
  7.2 794.7 %all-reduce.3.cloned.1.call-start = ((), (), s32[]{:S(2)}) async-start(), calls=%async_computation | async-start | bytes 17301504 | tf_op jit(solution)/shard_map/psum | solution.py:631
  11.7 26.4 %collective-permute-start.1 = (bf16[128,1024]{1,0:T(8,128)(2,1)}, bf16[128,1024]{1,0:T(8,128)(2,1)S(1)}, u32[]{:S(2)}, u32[]{:S(2)}) collective-permute-start(bf16[128,1024]{1,0:T(8,128)(2,1)} %get-tuple-element.195), channel_id=1, source_target_pairs={{0,1},{1,17},{16,0},{17,16},{2,3},{3,19},{18,2},{19,18},{4,5},{5,2... | collective-permute-start | bytes 786440 | tf_op jit(solution)/shard_map/ppermute | solution.py:486
  17.1 21.0 %collective-permute-start = (bf16[128,1024]{1,0:T(8,128)(2,1)S(1)}, bf16[128,1024]{1,0:T(8,128)(2,1)}, u32[]{:S(2)}, u32[]{:S(2)}) collective-permute-start(bf16[128,1024]{1,0:T(8,128)(2,1)S(1)} %get-tuple-element.196), channel_id=1, source_target_pairs={{0,0},{1,16},{16,1},{17,17},{2,2},{3,18},{18,3},{19,19},{4,4},{5,2... | collective-permute-start | bytes 786440 | tf_op jit(solution)/shard_map/ppermute | solution.py:485
  19.6 23.2 %collective-permute-start.95 = (bf16[128,1024]{1,0:T(8,128)(2,1)S(1)}, bf16[128,1024]{1,0:T(8,128)(2,1)}, u32[]{:S(2)}, u32[]{:S(2)}) collective-permute-start(bf16[128,1024]{1,0:T(8,128)(2,1)S(1)} %get-tuple-element.183), channel_id=1, source_target_pairs={{0,1},{1,17},{16,0},{17,16},{2,3},{3,19},{18,2},{19,18},{4,5},{5,2... | collective-permute-start | bytes 786440 | tf_op jit(solution)/shard_map/ppermute | solution.py:486
  20.2 35.5 %collective-permute-start.94 = (bf16[128,1024]{1,0:T(8,128)(2,1)S(1)}, bf16[128,1024]{1,0:T(8,128)(2,1)}, u32[]{:S(2)}, u32[]{:S(2)}) collective-permute-start(bf16[128,1024]{1,0:T(8,128)(2,1)S(1)} %get-tuple-element.184), channel_id=1, source_target_pairs={{0,0},{1,16},{16,1},{17,17},{2,2},{3,18},{18,3},{19,19},{4,4},{5,2... | collective-permute-start | bytes 786440 | tf_op jit(solution)/shard_map/ppermute | solution.py:485
  29.1 18.0 %collective-permute-start.17 = (bf16[128,1024]{1,0:T(8,128)(2,1)}, bf16[128,1024]{1,0:T(8,128)(2,1)}, u32[]{:S(2)}, u32[]{:S(2)}) collective-permute-start(bf16[128,1024]{1,0:T(8,128)(2,1)} %get-tuple-element.188), channel_id=1, source_target_pairs={{0,0},{1,16},{16,1},{17,17},{2,2},{3,18},{18,3},{19,19},{4,4},{5,2... | collective-permute-start | bytes 786440 | tf_op jit(solution)/shard_map/ppermute | solution.py:480
  39.6 16.5 %collective-permute-start.59 = (bf16[128,1024]{1,0:T(8,128)(2,1)S(1)}, bf16[128,1024]{1,0:T(8,128)(2,1)S(1)}, u32[]{:S(2)}, u32[]{:S(2)}) collective-permute-start(bf16[128,1024]{1,0:T(8,128)(2,1)S(1)} %get-tuple-element.277), channel_id=1, source_target_pairs={{0,8},{8,0},{1,9},{9,1},{2,10},{10,2},{3,11},{11,3},{4,12},{12,4},... | collective-permute-start | bytes 786440 | tf_op jit(solution)/shard_map/ppermute | solution.py:28
  59.7 16.2 %collective-permute-start.62 = (bf16[128,1024]{1,0:T(8,128)(2,1)S(1)}, bf16[128,1024]{1,0:T(8,128)(2,1)S(1)}, u32[]{:S(2)}, u32[]{:S(2)}) collective-permute-start(bf16[128,1024]{1,0:T(8,128)(2,1)S(1)} %get-tuple-element.277), channel_id=1, source_target_pairs={{0,1},{1,0},{2,3},{3,2},{4,5},{5,4},{6,7},{7,6},{8,9},{9,8},{10,11... | collective-permute-start | bytes 786440 | tf_op jit(solution)/shard_map/ppermute | solution.py:28
  81.2 60.5 %collective-permute-start.96 = (bf16[128,1024]{1,0:T(8,128)(2,1)}, bf16[128,1024]{1,0:T(8,128)(2,1)}, u32[]{:S(2)}, u32[]{:S(2)}) collective-permute-start(bf16[128,1024]{1,0:T(8,128)(2,1)} %get-tuple-element.182), channel_id=1, source_target_pairs={{0,2},{2,0},{1,3},{3,1},{4,6},{6,4},{5,7},{7,5},{8,10},{10,8},{9,1... | collective-permute-start | bytes 786440 | tf_op jit(solution)/shard_map/ppermute | solution.py:28
  82.7 30.4 %collective-permute-start.22 = (bf16[128,1024]{1,0:T(8,128)(2,1)}, bf16[128,1024]{1,0:T(8,128)(2,1)S(1)}, u32[]{:S(2)}, u32[]{:S(2)}) collective-permute-start(bf16[128,1024]{1,0:T(8,128)(2,1)} %collective-permute-done.17), channel_id=1, source_target_pairs={{0,1},{1,0},{2,3},{3,2},{4,5},{5,4},{6,7},{7,6},{8,9},{9,8},{10,11... | collective-permute-start | bytes 786440 | tf_op jit(solution)/shard_map/ppermute | solution.py:28
  82.9 30.3 %collective-permute-start.24 = (bf16[128,1024]{1,0:T(8,128)(2,1)S(1)}, bf16[128,1024]{1,0:T(8,128)(2,1)S(1)}, u32[]{:S(2)}, u32[]{:S(2)}) collective-permute-start(bf16[128,1024]{1,0:T(8,128)(2,1)S(1)} %collective-permute-done.19), channel_id=1, source_target_pairs={{0,1},{1,0},{2,3},{3,2},{4,5},{5,4},{6,7},{7,6},{8,9},{9,8},{10,11... | collective-permute-start | bytes 786440 | tf_op jit(solution)/shard_map/ppermute | solution.py:28
  83.3 30.5 %collective-permute-start.23 = (bf16[128,1024]{1,0:T(8,128)(2,1)S(1)}, bf16[128,1024]{1,0:T(8,128)(2,1)S(1)}, u32[]{:S(2)}, u32[]{:S(2)}) collective-permute-start(bf16[128,1024]{1,0:T(8,128)(2,1)S(1)} %collective-permute-done.18), channel_id=1, source_target_pairs={{0,1},{1,0},{2,3},{3,2},{4,5},{5,4},{6,7},{7,6},{8,9},{9,8},{10,11... | collective-permute-start | bytes 786440 | tf_op jit(solution)/shard_map/ppermute | solution.py:28
  84.5 29.2 %collective-permute-start.25 = (bf16[128,1024]{1,0:T(8,128)(2,1)S(1)}, bf16[128,1024]{1,0:T(8,128)(2,1)S(1)}, u32[]{:S(2)}, u32[]{:S(2)}) collective-permute-start(bf16[128,1024]{1,0:T(8,128)(2,1)S(1)} %constant_dynamic-update-slice_fusion.2), channel_id=1, source_target_pairs={{0,1},{1,0},{2,3},{3,2},{4,5},{5,4},{6,7},{7,6},{8,9},{9,8},{10,11... | collective-permute-start | bytes 786440 | tf_op jit(solution)/shard_map/ppermute | solution.py:28
  141.1 46.6 %collective-permute-start.97 = (bf16[128,1024]{1,0:T(8,128)(2,1)}, bf16[128,1024]{1,0:T(8,128)(2,1)S(1)}, u32[]{:S(2)}, u32[]{:S(2)}) collective-permute-start(bf16[128,1024]{1,0:T(8,128)(2,1)} %get-tuple-element.182), channel_id=1, source_target_pairs={{0,1},{1,0},{2,3},{3,2},{4,5},{5,4},{6,7},{7,6},{8,9},{9,8},{10,11... | collective-permute-start | bytes 786440 | tf_op jit(solution)/shard_map/ppermute | solution.py:28
  145.2 19.2 %collective-permute-start.105 = (bf16[128,1024]{1,0:T(8,128)(2,1)}, bf16[128,1024]{1,0:T(8,128)(2,1)}, u32[]{:S(2)}, u32[]{:S(2)}) collective-permute-start(bf16[128,1024]{1,0:T(8,128)(2,1)} %get-tuple-element.181), channel_id=1, source_target_pairs={{0,2},{2,0},{1,3},{3,1},{4,6},{6,4},{5,7},{7,5},{8,10},{10,8},{9,1... | collective-permute-start | bytes 786440 | tf_op jit(solution)/shard_map/ppermute | solution.py:28
  148.8 18.0 %collective-permute-start.46 = (bf16[128,1024]{1,0:T(8,128)(2,1)}, bf16[128,1024]{1,0:T(8,128)(2,1)S(1)}, u32[]{:S(2)}, u32[]{:S(2)}) collective-permute-start(bf16[128,1024]{1,0:T(8,128)(2,1)} %collective-permute-done.44), channel_id=1, source_target_pairs={{0,8},{8,0},{1,9},{9,1},{2,10},{10,2},{3,11},{11,3},{4,12},{12,4},... | collective-permute-start | bytes 786440 | tf_op jit(solution)/shard_map/ppermute | solution.py:28
  166.8 21.0 %collective-permute-start.49 = (bf16[128,1024]{1,0:T(8,128)(2,1)}, bf16[128,1024]{1,0:T(8,128)(2,1)S(1)}, u32[]{:S(2)}, u32[]{:S(2)}) collective-permute-start(bf16[128,1024]{1,0:T(8,128)(2,1)} %collective-permute-done.44), channel_id=1, source_target_pairs={{0,1},{1,0},{2,3},{3,2},{4,5},{5,4},{6,7},{7,6},{8,9},{9,8},{10,11... | collective-permute-start | bytes 786440 | tf_op jit(solution)/shard_map/ppermute | solution.py:28
  166.9 18.7 %collective-permute-start.48 = (bf16[128,512]{1,0:T(8,128)(2,1)S(1)}, bf16[128,512]{1,0:T(8,128)(2,1)S(1)}, u32[]{:S(2)}, u32[]{:S(2)}) collective-permute-start(bf16[128,512]{1,0:T(8,128)(2,1)S(1)} %slice.730), channel_id=1, source_target_pairs={{0,4},{4,0},{1,5},{5,1},{2,6},{6,2},{3,7},{7,3},{8,12},{12,8},{9,1... | collective-permute-start | bytes 393224 | tf_op jit(solution)/shard_map/ppermute | solution.py:28
  167.8 18.8 %collective-permute-start.47 = (bf16[128,512]{1,0:T(8,128)(2,1)S(1)}, bf16[128,512]{1,0:T(8,128)(2,1)S(1)}, u32[]{:S(2)}, u32[]{:S(2)}) collective-permute-start(bf16[128,512]{1,0:T(8,128)(2,1)S(1)} %slice.729), channel_id=1, source_target_pairs={{0,8},{8,0},{1,9},{9,1},{2,10},{10,2},{3,11},{11,3},{4,12},{12,4},... | collective-permute-start | bytes 393224 | tf_op jit(solution)/shard_map/ppermute | solution.py:28
  197.3 26.4 %collective-permute-start.39 = (bf16[1024,384]{1,0:T(8,128)(2,1)S(1)}, bf16[1024,384]{1,0:T(8,128)(2,1)S(1)}, u32[]{:S(2)}, u32[]{:S(2)}) collective-permute-start(bf16[1024,384]{1,0:T(8,128)(2,1)S(1)} %copy-done.101), channel_id=1, source_target_pairs={{0,0},{1,16},{16,1},{17,17},{2,2},{3,18},{18,3},{19,19},{4,4},{5,2... | collective-permute-start | bytes 2359304 | tf_op jit(solution)/shard_map/ppermute | solution.py:480
  202.2 19.0 %collective-permute-start.35 = (bf16[128,1024]{1,0:T(8,128)(2,1)S(1)}, bf16[128,1024]{1,0:T(8,128)(2,1)S(1)}, u32[]{:S(2)}, u32[]{:S(2)}) collective-permute-start(bf16[128,1024]{1,0:T(8,128)(2,1)S(1)} %get-tuple-element.274), channel_id=1, source_target_pairs={{0,1},{1,0},{2,3},{3,2},{4,5},{5,4},{6,7},{7,6},{8,9},{9,8},{10,11... | collective-permute-start | bytes 786440 | tf_op jit(solution)/shard_map/ppermute | solution.py:28
  221.3 42.7 %collective-permute-start.106 = (bf16[128,1024]{1,0:T(8,128)(2,1)}, bf16[128,1024]{1,0:T(8,128)(2,1)}, u32[]{:S(2)}, u32[]{:S(2)}) collective-permute-start(bf16[128,1024]{1,0:T(8,128)(2,1)} %get-tuple-element.181), channel_id=1, source_target_pairs={{0,1},{1,0},{2,3},{3,2},{4,5},{5,4},{6,7},{7,6},{8,9},{9,8},{10,11... | collective-permute-start | bytes 786440 | tf_op jit(solution)/shard_map/ppermute | solution.py:28
  229.9 34.1 %collective-permute-start.107 = (bf16[128,1024]{1,0:T(8,128)(2,1)}, bf16[128,1024]{1,0:T(8,128)(2,1)}, u32[]{:S(2)}, u32[]{:S(2)}) collective-permute-start(bf16[128,1024]{1,0:T(8,128)(2,1)} %collective-permute-done.105), channel_id=1, source_target_pairs={{0,1},{1,0},{2,3},{3,2},{4,5},{5,4},{6,7},{7,6},{8,9},{9,8},{10,11... | collective-permute-start | bytes 786440 | tf_op jit(solution)/shard_map/ppermute | solution.py:28
  287.5 17.1 %collective-permute-start.90 = (bf16[2,128,1024]{2,1,0:T(8,128)(2,1)S(1)}, bf16[2,128,1024]{2,1,0:T(8,128)(2,1)S(1)}, u32[]{:S(2)}, u32[]{:S(2)}) collective-permute-start(bf16[2,128,1024]{2,1,0:T(8,128)(2,1)S(1)} %bitcast.867), channel_id=1, source_target_pairs={{0,1},{1,0},{2,3},{3,2},{4,5},{5,4},{6,7},{7,6},{8,9},{9,8},{10,11... | collective-permute-start | bytes 1572872 | tf_op jit(solution)/shard_map/ppermute | solution.py:28
  300.7 27.1 %collective-permute-start.57 = (bf16[128,1024]{1,0:T(8,128)(2,1)S(1)}, bf16[128,1024]{1,0:T(8,128)(2,1)S(1)}, u32[]{:S(2)}, u32[]{:S(2)}) collective-permute-start(bf16[128,1024]{1,0:T(8,128)(2,1)S(1)} %fusion.132), channel_id=1, source_target_pairs={{0,2},{2,0},{1,3},{3,1},{4,6},{6,4},{5,7},{7,5},{8,10},{10,8},{9,1... | collective-permute-start | bytes 786440 | tf_op jit(solution)/shard_map/ppermute | solution.py:28
  303.3 17.8 %collective-permute-start.100 = (bf16[128,1024]{1,0:T(8,128)(2,1)S(1)}, bf16[128,1024]{1,0:T(8,128)(2,1)S(1)}, u32[]{:S(2)}, u32[]{:S(2)}) collective-permute-start(bf16[128,1024]{1,0:T(8,128)(2,1)S(1)} %fusion.135), channel_id=1, source_target_pairs={{0,2},{2,0},{1,3},{3,1},{4,6},{6,4},{5,7},{7,5},{8,10},{10,8},{9,1... | collective-permute-start | bytes 786440 | tf_op jit(solution)/shard_map/ppermute | solution.py:28
  304.9 22.9 %collective-permute-start.91 = (bf16[128,1024]{1,0:T(8,128)(2,1)S(1)}, bf16[128,1024]{1,0:T(8,128)(2,1)S(1)}, u32[]{:S(2)}, u32[]{:S(2)}) collective-permute-start(bf16[128,1024]{1,0:T(8,128)(2,1)S(1)} %fusion.134), channel_id=1, source_target_pairs={{0,2},{2,0},{1,3},{3,1},{4,6},{6,4},{5,7},{7,5},{8,10},{10,8},{9,1... | collective-permute-start | bytes 786440 | tf_op jit(solution)/shard_map/ppermute | solution.py:28
  329.5 57.7 %collective-permute-start.93 = (bf16[128,1024]{1,0:T(8,128)(2,1)}, bf16[128,1024]{1,0:T(8,128)(2,1)}, u32[]{:S(2)}, u32[]{:S(2)}) collective-permute-start(bf16[128,1024]{1,0:T(8,128)(2,1)} %broadcast_select_fusion.4), channel_id=1, source_target_pairs={{1,0},{17,1},{0,16},{16,17},{3,2},{19,3},{2,18},{18,19},{5,4},{21,... | collective-permute-start | bytes 786440 | tf_op jit(solution)/shard_map/ppermute | solution.py:493
  332.3 55.0 %collective-permute-start.92 = (bf16[128,1024]{1,0:T(8,128)(2,1)}, bf16[128,1024]{1,0:T(8,128)(2,1)}, u32[]{:S(2)}, u32[]{:S(2)}) collective-permute-start(bf16[128,1024]{1,0:T(8,128)(2,1)} %get-tuple-element.96), channel_id=1, source_target_pairs={{0,0},{1,16},{16,1},{17,17},{2,2},{3,18},{18,3},{19,19},{4,4},{5,2... | collective-permute-start | bytes 786440 | tf_op jit(solution)/shard_map/ppermute | solution.py:492
  359.1 30.5 %collective-permute-start.163 = (bf16[4,128,1024]{2,1,0:T(8,128)(2,1)S(1)}, bf16[4,128,1024]{2,1,0:T(8,128)(2,1)S(1)}, u32[]{:S(2)}, u32[]{:S(2)}) collective-permute-start(bf16[4,128,1024]{2,1,0:T(8,128)(2,1)S(1)} %bitcast.836), channel_id=1, source_target_pairs={{0,1},{1,0},{2,3},{3,2},{4,5},{5,4},{6,7},{7,6},{8,9},{9,8},{10,11... | collective-permute-start | bytes 3145736 | tf_op jit(solution)/shard_map/ppermute | solution.py:28
  376.5 19.3 %collective-permute-start.153 = (bf16[1024,384]{1,0:T(8,128)(2,1)S(1)}, bf16[1024,384]{1,0:T(8,128)(2,1)S(1)}, u32[]{:S(2)}, u32[]{:S(2)}) collective-permute-start(bf16[1024,384]{1,0:T(8,128)(2,1)S(1)} %fusion), channel_id=1, source_target_pairs={{0,0},{1,16},{16,1},{17,17},{2,2},{3,18},{18,3},{19,19},{4,4},{5,2... | collective-permute-start | bytes 2359304 | tf_op jit(solution)/shard_map/ppermute | solution.py:480
  391.2 17.3 %collective-permute-start.166 = (bf16[128,1024]{1,0:T(8,128)(2,1)S(1)}, bf16[128,1024]{1,0:T(8,128)(2,1)S(1)}, u32[]{:S(2)}, u32[]{:S(2)}) collective-permute-start(bf16[128,1024]{1,0:T(8,128)(2,1)S(1)} %get-tuple-element.151), channel_id=1, source_target_pairs={{0,12},{4,8},{8,4},{12,0},{1,13},{5,9},{9,5},{13,1},{2,14},{6,10},... | collective-permute-start | bytes 786440 | tf_op jit(solution)/shard_map/ppermute | solution.py:28
  392.9 20.6 %collective-permute-start.165 = (bf16[128,1024]{1,0:T(8,128)(2,1)S(1)}, bf16[128,1024]{1,0:T(8,128)(2,1)S(1)}, u32[]{:S(2)}, u32[]{:S(2)}) collective-permute-start(bf16[128,1024]{1,0:T(8,128)(2,1)S(1)} %get-tuple-element.152), channel_id=1, source_target_pairs={{0,8},{8,0},{1,9},{9,1},{2,10},{10,2},{3,11},{11,3},{4,12},{12,4},... | collective-permute-start | bytes 786440 | tf_op jit(solution)/shard_map/ppermute | solution.py:28
  394.2 19.4 %collective-permute-start.115 = (bf16[128,1024]{1,0:T(8,128)(2,1)S(1)}, bf16[128,1024]{1,0:T(8,128)(2,1)S(1)}, u32[]{:S(2)}, u32[]{:S(2)}) collective-permute-start(bf16[128,1024]{1,0:T(8,128)(2,1)S(1)} %get-tuple-element.166), channel_id=1, source_target_pairs={{0,4},{4,0},{1,5},{5,1},{2,6},{6,2},{3,7},{7,3},{8,12},{12,8},{9,1... | collective-permute-start | bytes 786440 | tf_op jit(solution)/shard_map/ppermute | solution.py:28
  395.9 23.9 %collective-permute-start.117 = (bf16[128,1024]{1,0:T(8,128)(2,1)S(1)}, bf16[128,1024]{1,0:T(8,128)(2,1)S(1)}, u32[]{:S(2)}, u32[]{:S(2)}) collective-permute-start(bf16[128,1024]{1,0:T(8,128)(2,1)S(1)} %get-tuple-element.167), channel_id=1, source_target_pairs={{0,12},{4,8},{8,4},{12,0},{1,13},{5,9},{9,5},{13,1},{2,14},{6,10},... | collective-permute-start | bytes 786440 | tf_op jit(solution)/shard_map/ppermute | solution.py:28
  399.7 25.1 %collective-permute-start.116 = (bf16[128,1024]{1,0:T(8,128)(2,1)S(1)}, bf16[128,1024]{1,0:T(8,128)(2,1)S(1)}, u32[]{:S(2)}, u32[]{:S(2)}) collective-permute-start(bf16[128,1024]{1,0:T(8,128)(2,1)S(1)} %get-tuple-element.168), channel_id=1, source_target_pairs={{0,8},{8,0},{1,9},{9,1},{2,10},{10,2},{3,11},{11,3},{4,12},{12,4},... | collective-permute-start | bytes 786440 | tf_op jit(solution)/shard_map/ppermute | solution.py:28
  408.5 17.0 %collective-permute-start.128 = (bf16[128,1024]{1,0:T(8,128)(2,1)S(1)}, bf16[128,1024]{1,0:T(8,128)(2,1)S(1)}, u32[]{:S(2)}, u32[]{:S(2)}) collective-permute-start(bf16[128,1024]{1,0:T(8,128)(2,1)S(1)} %get-tuple-element.161), channel_id=1, source_target_pairs={{0,4},{4,0},{1,5},{5,1},{2,6},{6,2},{3,7},{7,3},{8,12},{12,8},{9,1... | collective-permute-start | bytes 786440 | tf_op jit(solution)/shard_map/ppermute | solution.py:28
  413.5 17.5 %collective-permute-start.130 = (bf16[128,1024]{1,0:T(8,128)(2,1)S(1)}, bf16[128,1024]{1,0:T(8,128)(2,1)S(1)}, u32[]{:S(2)}, u32[]{:S(2)}) collective-permute-start(bf16[128,1024]{1,0:T(8,128)(2,1)S(1)} %get-tuple-element.162), channel_id=1, source_target_pairs={{0,12},{4,8},{8,4},{12,0},{1,13},{5,9},{9,5},{13,1},{2,14},{6,10},... | collective-permute-start | bytes 786440 | tf_op jit(solution)/shard_map/ppermute | solution.py:28
  413.6 24.8 %collective-permute-start.129 = (bf16[128,1024]{1,0:T(8,128)(2,1)S(1)}, bf16[128,1024]{1,0:T(8,128)(2,1)S(1)}, u32[]{:S(2)}, u32[]{:S(2)}) collective-permute-start(bf16[128,1024]{1,0:T(8,128)(2,1)S(1)} %get-tuple-element.163), channel_id=1, source_target_pairs={{0,8},{8,0},{1,9},{9,1},{2,10},{10,2},{3,11},{11,3},{4,12},{12,4},... | collective-permute-start | bytes 786440 | tf_op jit(solution)/shard_map/ppermute | solution.py:28
  419.7 23.5 %collective-permute-start.154 = (bf16[1024,384]{1,0:T(8,128)(2,1)S(1)}, bf16[1024,384]{1,0:T(8,128)(2,1)S(1)}, u32[]{:S(2)}, u32[]{:S(2)}) collective-permute-start(bf16[1024,384]{1,0:T(8,128)(2,1)S(1)} %collective-permute-done.153), channel_id=1, source_target_pairs={{0,1},{1,0},{2,3},{3,2},{4,5},{5,4},{6,7},{7,6},{8,9},{9,8},{10,11... | collective-permute-start | bytes 2359304 | tf_op jit(solution)/shard_map/ppermute | solution.py:28
  424.8 17.7 %collective-permute-start.167 = (bf16[128,1024]{1,0:T(8,128)(2,1)S(1)}, bf16[128,1024]{1,0:T(8,128)(2,1)S(1)}, u32[]{:S(2)}, u32[]{:S(2)}) collective-permute-start(bf16[128,1024]{1,0:T(8,128)(2,1)S(1)} %fusion.97), channel_id=1, source_target_pairs={{0,0},{1,16},{16,1},{17,17},{2,2},{3,18},{18,3},{19,19},{4,4},{5,2... | collective-permute-start | bytes 786440 | tf_op jit(solution)/shard_map/ppermute | solution.py:480
  440.9 16.2 %collective-permute-start.132 = (bf16[128,1024]{1,0:T(8,128)(2,1)S(1)}, bf16[128,1024]{1,0:T(8,128)(2,1)S(1)}, u32[]{:S(2)}, u32[]{:S(2)}) collective-permute-start(bf16[128,1024]{1,0:T(8,128)(2,1)S(1)} %get-tuple-element.93), channel_id=1, source_target_pairs={{0,1},{1,0},{2,3},{3,2},{4,5},{5,4},{6,7},{7,6},{8,9},{9,8},{10,11... | collective-permute-start | bytes 786440 | tf_op jit(solution)/shard_map/ppermute | solution.py:28
  442.2 18.7 %collective-permute-start.119 = (bf16[128,1024]{1,0:T(8,128)(2,1)S(1)}, bf16[128,1024]{1,0:T(8,128)(2,1)S(1)}, u32[]{:S(2)}, u32[]{:S(2)}) collective-permute-start(bf16[128,1024]{1,0:T(8,128)(2,1)S(1)} %get-tuple-element.262), channel_id=1, source_target_pairs={{0,1},{1,0},{2,3},{3,2},{4,5},{5,4},{6,7},{7,6},{8,9},{9,8},{10,11... | collective-permute-start | bytes 786440 | tf_op jit(solution)/shard_map/ppermute | solution.py:28
  450.0 32.1 %collective-permute-start.155 = (bf16[1024,384]{1,0:T(8,128)(2,1)S(1)}, bf16[1024,384]{1,0:T(8,128)(2,1)}, u32[]{:S(2)}, u32[]{:S(2)}) collective-permute-start(bf16[1024,384]{1,0:T(8,128)(2,1)S(1)} %add_convert_fusion.13), channel_id=1, source_target_pairs={{0,2},{2,0},{1,3},{3,1},{4,6},{6,4},{5,7},{7,5},{8,10},{10,8},{9,1... | collective-permute-start | bytes 2359304 | tf_op jit(solution)/shard_map/ppermute | solution.py:28
  457.1 23.2 %collective-permute-start.169 = (bf16[128,1024]{1,0:T(8,128)(2,1)}, bf16[128,1024]{1,0:T(8,128)(2,1)}, u32[]{:S(2)}, u32[]{:S(2)}) collective-permute-start(bf16[128,1024]{1,0:T(8,128)(2,1)} %add_convert_fusion.17), channel_id=1, source_target_pairs={{0,2},{2,0},{1,3},{3,1},{4,6},{6,4},{5,7},{7,5},{8,10},{10,8},{9,1... | collective-permute-start | bytes 786440 | tf_op jit(solution)/shard_map/ppermute | solution.py:28
  516.8 17.4 %collective-permute-start.124 = (bf16[2,128,128]{2,1,0:T(8,128)(2,1)S(1)}, bf16[2,128,128]{2,1,0:T(8,128)(2,1)S(1)}, u32[]{:S(2)}, u32[]{:S(2)}) collective-permute-start(bf16[2,128,128]{2,1,0:T(8,128)(2,1)S(1)} %get-tuple-element.207), channel_id=1, source_target_pairs={{0,8},{8,0},{1,9},{9,1},{2,10},{10,2},{3,11},{11,3},{4,12},{12,4},... | collective-permute-start | bytes 196616 | tf_op jit(solution)/shard_map/ppermute | solution.py:28
  520.2 18.7 %collective-permute-start.138 = (bf16[2,128,128]{2,1,0:T(8,128)(2,1)S(1)}, bf16[2,128,128]{2,1,0:T(8,128)(2,1)S(1)}, u32[]{:S(2)}, u32[]{:S(2)}) collective-permute-start(bf16[2,128,128]{2,1,0:T(8,128)(2,1)S(1)} %get-tuple-element.200), channel_id=1, source_target_pairs={{0,12},{4,8},{8,4},{12,0},{1,13},{5,9},{9,5},{13,1},{2,14},{6,10},... | collective-permute-start | bytes 196616 | tf_op jit(solution)/shard_map/ppermute | solution.py:28
  520.3 21.5 %collective-permute-start.137 = (bf16[2,128,128]{2,1,0:T(8,128)(2,1)S(1)}, bf16[2,128,128]{2,1,0:T(8,128)(2,1)S(1)}, u32[]{:S(2)}, u32[]{:S(2)}) collective-permute-start(bf16[2,128,128]{2,1,0:T(8,128)(2,1)S(1)} %get-tuple-element.201), channel_id=1, source_target_pairs={{0,8},{8,0},{1,9},{9,1},{2,10},{10,2},{3,11},{11,3},{4,12},{12,4},... | collective-permute-start | bytes 196616 | tf_op jit(solution)/shard_map/ppermute | solution.py:28
  542.8 29.4 %collective-permute-start.156 = (bf16[4,128,1024]{2,1,0:T(8,128)(2,1)S(1)}, bf16[4,128,1024]{2,1,0:T(8,128)(2,1)S(1)}, u32[]{:S(2)}, u32[]{:S(2)}) collective-permute-start(bf16[4,128,1024]{2,1,0:T(8,128)(2,1)S(1)} %bitcast.837), channel_id=1, source_target_pairs={{0,1},{1,0},{2,3},{3,2},{4,5},{5,4},{6,7},{7,6},{8,9},{9,8},{10,11... | collective-permute-start | bytes 3145736 | tf_op jit(solution)/shard_map/ppermute | solution.py:28
  558.2 20.9 %collective-permute-start.150 = (bf16[1024,384]{1,0:T(8,128)(2,1)S(1)}, bf16[1024,384]{1,0:T(8,128)(2,1)}, u32[]{:S(2)}, u32[]{:S(2)}) collective-permute-start(bf16[1024,384]{1,0:T(8,128)(2,1)S(1)} %fusion.1), channel_id=1, source_target_pairs={{0,0},{1,16},{16,1},{17,17},{2,2},{3,18},{18,3},{19,19},{4,4},{5,2... | collective-permute-start | bytes 2359304 | tf_op jit(solution)/shard_map/ppermute | solution.py:480
  573.6 25.8 %collective-permute-start.159 = (bf16[128,1024]{1,0:T(8,128)(2,1)S(1)}, bf16[128,1024]{1,0:T(8,128)(2,1)S(1)}, u32[]{:S(2)}, u32[]{:S(2)}) collective-permute-start(bf16[128,1024]{1,0:T(8,128)(2,1)S(1)} %get-tuple-element.148), channel_id=1, source_target_pairs={{0,12},{4,8},{8,4},{12,0},{1,13},{5,9},{9,5},{13,1},{2,14},{6,10},... | collective-permute-start | bytes 786440 | tf_op jit(solution)/shard_map/ppermute | solution.py:28
  576.9 27.9 %collective-permute-start.158 = (bf16[128,1024]{1,0:T(8,128)(2,1)S(1)}, bf16[128,1024]{1,0:T(8,128)(2,1)S(1)}, u32[]{:S(2)}, u32[]{:S(2)}) collective-permute-start(bf16[128,1024]{1,0:T(8,128)(2,1)S(1)} %get-tuple-element.149), channel_id=1, source_target_pairs={{0,8},{8,0},{1,9},{9,1},{2,10},{10,2},{3,11},{11,3},{4,12},{12,4},... | collective-permute-start | bytes 786440 | tf_op jit(solution)/shard_map/ppermute | solution.py:28
  577.5 27.8 %collective-permute-start.145 = (bf16[128,1024]{1,0:T(8,128)(2,1)S(1)}, bf16[128,1024]{1,0:T(8,128)(2,1)S(1)}, u32[]{:S(2)}, u32[]{:S(2)}) collective-permute-start(bf16[128,1024]{1,0:T(8,128)(2,1)S(1)} %get-tuple-element.153), channel_id=1, source_target_pairs={{0,4},{4,0},{1,5},{5,1},{2,6},{6,2},{3,7},{7,3},{8,12},{12,8},{9,1... | collective-permute-start | bytes 786440 | tf_op jit(solution)/shard_map/ppermute | solution.py:28
  579.1 37.3 %collective-permute-start.147 = (bf16[128,1024]{1,0:T(8,128)(2,1)S(1)}, bf16[128,1024]{1,0:T(8,128)(2,1)S(1)}, u32[]{:S(2)}, u32[]{:S(2)}) collective-permute-start(bf16[128,1024]{1,0:T(8,128)(2,1)S(1)} %get-tuple-element.154), channel_id=1, source_target_pairs={{0,12},{4,8},{8,4},{12,0},{1,13},{5,9},{9,5},{13,1},{2,14},{6,10},... | collective-permute-start | bytes 786440 | tf_op jit(solution)/shard_map/ppermute | solution.py:28
  583.4 42.5 %collective-permute-start.146 = (bf16[128,1024]{1,0:T(8,128)(2,1)S(1)}, bf16[128,1024]{1,0:T(8,128)(2,1)S(1)}, u32[]{:S(2)}, u32[]{:S(2)}) collective-permute-start(bf16[128,1024]{1,0:T(8,128)(2,1)S(1)} %get-tuple-element.155), channel_id=1, source_target_pairs={{0,8},{8,0},{1,9},{9,1},{2,10},{10,2},{3,11},{11,3},{4,12},{12,4},... | collective-permute-start | bytes 786440 | tf_op jit(solution)/shard_map/ppermute | solution.py:28
  599.4 28.1 %collective-permute-start.141 = (bf16[128,1024]{1,0:T(8,128)(2,1)S(1)}, bf16[128,1024]{1,0:T(8,128)(2,1)S(1)}, u32[]{:S(2)}, u32[]{:S(2)}) collective-permute-start(bf16[128,1024]{1,0:T(8,128)(2,1)S(1)} %get-tuple-element.156), channel_id=1, source_target_pairs={{0,4},{4,0},{1,5},{5,1},{2,6},{6,2},{3,7},{7,3},{8,12},{12,8},{9,1... | collective-permute-start | bytes 786440 | tf_op jit(solution)/shard_map/ppermute | solution.py:28
  604.9 34.0 %collective-permute-start.143 = (bf16[128,1024]{1,0:T(8,128)(2,1)S(1)}, bf16[128,1024]{1,0:T(8,128)(2,1)S(1)}, u32[]{:S(2)}, u32[]{:S(2)}) collective-permute-start(bf16[128,1024]{1,0:T(8,128)(2,1)S(1)} %get-tuple-element.157), channel_id=1, source_target_pairs={{0,12},{4,8},{8,4},{12,0},{1,13},{5,9},{9,5},{13,1},{2,14},{6,10},... | collective-permute-start | bytes 786440 | tf_op jit(solution)/shard_map/ppermute | solution.py:28
  605.3 48.1 %collective-permute-start.142 = (bf16[128,1024]{1,0:T(8,128)(2,1)S(1)}, bf16[128,1024]{1,0:T(8,128)(2,1)S(1)}, u32[]{:S(2)}, u32[]{:S(2)}) collective-permute-start(bf16[128,1024]{1,0:T(8,128)(2,1)S(1)} %get-tuple-element.158), channel_id=1, source_target_pairs={{0,8},{8,0},{1,9},{9,1},{2,10},{10,2},{3,11},{11,3},{4,12},{12,4},... | collective-permute-start | bytes 786440 | tf_op jit(solution)/shard_map/ppermute | solution.py:28
  616.4 89.6 %collective-permute-start.151 = (bf16[1024,384]{1,0:T(8,128)(2,1)}, bf16[1024,384]{1,0:T(8,128)(2,1)}, u32[]{:S(2)}, u32[]{:S(2)}) collective-permute-start(bf16[1024,384]{1,0:T(8,128)(2,1)} %collective-permute-done.150), channel_id=1, source_target_pairs={{0,1},{1,0},{2,3},{3,2},{4,5},{5,4},{6,7},{7,6},{8,9},{9,8},{10,11... | collective-permute-start | bytes 2359304 | tf_op jit(solution)/shard_map/ppermute | solution.py:28
  625.8 80.2 %collective-permute-start.160 = (bf16[128,1024]{1,0:T(8,128)(2,1)}, bf16[128,1024]{1,0:T(8,128)(2,1)S(1)}, u32[]{:S(2)}, u32[]{:S(2)}) collective-permute-start(bf16[128,1024]{1,0:T(8,128)(2,1)} %fusion.101), channel_id=1, source_target_pairs={{0,0},{1,16},{16,1},{17,17},{2,2},{3,18},{18,3},{19,19},{4,4},{5,2... | collective-permute-start | bytes 786440 | tf_op jit(solution)/shard_map/ppermute | solution.py:480
  655.6 55.2 %collective-permute-start.149 = (bf16[128,1024]{1,0:T(8,128)(2,1)S(1)}, bf16[128,1024]{1,0:T(8,128)(2,1)S(1)}, u32[]{:S(2)}, u32[]{:S(2)}) collective-permute-start(bf16[128,1024]{1,0:T(8,128)(2,1)S(1)} %broadcast_select_fusion), channel_id=1, source_target_pairs={{1,0},{17,1},{0,16},{16,17},{3,2},{19,3},{2,18},{18,19},{5,4},{21,... | collective-permute-start | bytes 786440 | tf_op jit(solution)/shard_map/ppermute | solution.py:493
  656.0 54.7 %collective-permute-start.148 = (bf16[128,1024]{1,0:T(8,128)(2,1)}, bf16[128,1024]{1,0:T(8,128)(2,1)S(1)}, u32[]{:S(2)}, u32[]{:S(2)}) collective-permute-start(bf16[128,1024]{1,0:T(8,128)(2,1)} %get-tuple-element.85), channel_id=1, source_target_pairs={{0,0},{1,16},{16,1},{17,17},{2,2},{3,18},{18,3},{19,19},{4,4},{5,2... | collective-permute-start | bytes 786440 | tf_op jit(solution)/shard_map/ppermute | solution.py:492
  707.6 27.3 %collective-permute-start.152 = (bf16[1024,384]{1,0:T(8,128)(2,1)S(1)}, bf16[1024,384]{1,0:T(8,128)(2,1)S(1)}, u32[]{:S(2)}, u32[]{:S(2)}) collective-permute-start(bf16[1024,384]{1,0:T(8,128)(2,1)S(1)} %add_convert_fusion.15), channel_id=1, source_target_pairs={{0,2},{2,0},{1,3},{3,1},{4,6},{6,4},{5,7},{7,5},{8,10},{10,8},{9,1... | collective-permute-start | bytes 2359304 | tf_op jit(solution)/shard_map/ppermute | solution.py:28
  710.0 23.8 %collective-permute-start.162 = (bf16[128,1024]{1,0:T(8,128)(2,1)S(1)}, bf16[128,1024]{1,0:T(8,128)(2,1)S(1)}, u32[]{:S(2)}, u32[]{:S(2)}) collective-permute-start(bf16[128,1024]{1,0:T(8,128)(2,1)S(1)} %add_convert_fusion.19), channel_id=1, source_target_pairs={{0,2},{2,0},{1,3},{3,1},{4,6},{6,4},{5,7},{7,5},{8,10},{10,8},{9,1... | collective-permute-start | bytes 786440 | tf_op jit(solution)/shard_map/ppermute | solution.py:28
  (266 other events, 2573.3 us)
Sparse Core Ops, SparseCore 0:
  480.4 321.4 all-reduce.2

commit v2 on v1

v2 whole, which is shorter than its diff:
```python
import functools

import jax
import jax.numpy as jnp
import numpy as np
from jax import lax
from jax.experimental import pallas as pl
from jax.experimental.pallas import tpu as pltpu
from jax.sharding import Mesh
from jax.sharding import PartitionSpec as P

HEAD_DIM = 64
SEQ_UNIT = 1024
EPSILON = 1e-06
THETA = 10000.0
NEG_LARGE = -1e30
BF16 = jnp.bfloat16
F32 = jnp.float32
VMEM_BYTES = 36 * 1024 * 1024
COST_SCALE = 50

NT = (((1,), (1,)), ((), ()))
TN = (((0,), (0,)), ((), ()))


def swap(value, axes):
    axes = tuple(sorted(axes))
    size = 2 ** len(axes)
    return lax.ppermute(
        value, axes if len(axes) > 1 else axes[0], [(i, size - 1 - i) for i in range(size)]
    )


def axes_of(bits, axes):
    count = len(axes)
    return tuple(a for n, a in enumerate(axes) if bits >> (count - 1 - n) & 1)


def gather_chips(value, axes):
    return [value] + [swap(value, axes_of(i, axes)) for i in range(1, 2 ** len(axes))]


def after(value, *others):
    return lax.optimization_barrier((value, *others))[0]


def gather(value, axes, core, *ties):
    if len(axes) == 2:
        half = value.shape[-1] // 2
        own = swap(value, (core,))
        low = swap(value, axes[1:])
        high = swap(value, axes[:1])
        low, high, own, *_ = lax.optimization_barrier((low, high, own, *ties))
        both = jnp.concatenate(
            [swap(low[..., :half], axes[:1]), swap(high[..., half:], axes[1:])], axis=-1
        )
        chips = [value, low, high, both]
        return chips, [own] + [swap(c, (core,)) for c in chips[1:]]
    chips = gather_chips(value, axes)
    return chips, [swap(c, (core,)) for c in chips]


def reduce_blocks(kept, received, axes):
    for axis in axes:
        if axis != axes[0]:
            received = swap(sent, (axis,))
        total = (kept.astype(F32) + received.astype(F32)).astype(BF16)
        half = total.shape[0] // 2
        kept, sent = total[:half], total[half:]
    return total


def spread_blocks(block, axes):
    for axis in reversed(axes):
        block = jnp.concatenate([block, swap(block, (axis,))], axis=0)
    return block


def scatter_sum(mine, others, axes, core, *ties):
    mine = mine + swap(others, (core,)).astype(F32)
    sent = after(mine.astype(BF16), *ties)
    total = mine[0]
    for i in range(1, 2 ** len(axes)):
        total = total + swap(sent[i], axes_of(i, axes)).astype(F32)
    return total


def exchange(blocks, axes, core):
    got = [blocks[0]] + [swap(blocks[i], axes_of(i, axes)) for i in range(1, 2 ** len(axes))]
    return got, swap(jnp.stack([g[1] for g in got]), (core,))


def exchange_sum(value, axes, kind=BF16):
    for axis in axes:
        value = (value.astype(F32) + swap(value, (axis,)).astype(F32)).astype(kind)
    return value


TURN = [(0, 0), (1, 2), (2, 1), (3, 3)]


def compiler_params():
    return pltpu.CompilerParams(vmem_limit_bytes=VMEM_BYTES)


def cost(flops, bytes_accessed, transcendentals):
    return pl.CostEstimate(
        flops=flops // COST_SCALE,
        bytes_accessed=bytes_accessed // COST_SCALE,
        transcendentals=transcendentals // COST_SCALE,
    )


VMEM = functools.partial(pl.BlockSpec, memory_space=pltpu.VMEM)
SMEM = functools.partial(pl.BlockSpec, memory_space=pltpu.SMEM)


def half_turn(value):
    width = value.shape[-1]
    halfway = HEAD_DIM // 2
    if width == HEAD_DIM:
        return jnp.concatenate([value[:, halfway:], value[:, :halfway]], axis=-1)
    lane = lax.broadcasted_iota(jnp.int32, value.shape, 1)
    return jnp.where(
        lane % HEAD_DIM < halfway,
        pltpu.roll(value, width - halfway, 1),
        pltpu.roll(value, halfway, 1),
    )


def head_masked(value, head):
    if value.shape[-1] == HEAD_DIM:
        return value
    lane = lax.broadcasted_iota(jnp.int32, value.shape, 1)
    return jnp.where(lane // HEAD_DIM == head, value, jnp.zeros_like(value))


def place_of(ids, core, chip, chips, rows):
    place = (core ^ ids[1]) * chips + (chip ^ ids[0])
    return pl.ds(pl.multiple_of(place * rows, rows), rows)


def pack_kernel(width, places, *refs):
    out = refs[-1]
    layers = out.shape[0]
    for layer in range(layers):
        for half in range(2):
            @pl.when(places[0] == half)
            def _():
                for n in range(2):
                    part = refs[2 * half + n][layer]
                    out[layer, n * width : (n + 1) * width] = part if half and n else part.T


def pack_heads(places, weights):
    layers, depth, width = weights[0].shape
    return pl.pallas_call(
        functools.partial(pack_kernel, width),
        out_shape=jax.ShapeDtypeStruct((layers, 2 * width, depth), BF16),
        in_specs=[SMEM()] + [VMEM()] * 4,
        out_specs=VMEM(),
        compiler_params=compiler_params(),
        cost_estimate=cost(
            flops=0, bytes_accessed=12 * layers * width * depth, transcendentals=0
        ),
        name="pack_head_weights",
    )(places, *weights)


def table_rows(ids, core, chip, chips, rows):
    count = 2 * chips * rows
    units = max(count // SEQ_UNIT, 1)
    first = ((core ^ ids[1]) * chips + (chip ^ ids[0])) * rows
    unit = first // (count // units)
    start = ids[2 + units * units + unit]
    return pl.ds(pl.multiple_of(start + first % (count // units), rows), rows)


def project_kernel(mixed, chips, rows, width, *refs):
    refs = list(refs)
    ids = refs.pop(0)
    blocks = [refs.pop(0) for _ in range(2 * chips)]
    weights, cosine, sine = (refs.pop(0) for _ in range(3))
    first = refs.pop(0) if mixed else None
    queries, keys, values = refs
    for number, block in enumerate(blocks):
        raw = lax.dot_general(block[...], weights[: 3 * width, :], NT, preferred_element_type=F32)
        at = place_of(ids, number // chips, number % chips, chips, rows)
        query, key, value = (raw[:, n * width : (n + 1) * width] for n in range(3))
        turn_at = table_rows(ids, number // chips, number % chips, chips, rows)
        cos, sin = cosine[turn_at, :], sine[turn_at, :]
        queries[at, :] = ((query * cos + half_turn(query) * sin) * HEAD_DIM**-0.5).astype(BF16)
        keys[at, :] = (key * cos + half_turn(key) * sin).astype(BF16)
        if mixed:
            value = 0.5 * value + 0.5 * first[at, :].astype(F32)
        values[at, :] = value.astype(BF16)


def project(ids, blocks, weights, cosine, sine, first):
    chips = len(blocks) // 2
    rows, depth = blocks[0].shape
    width = weights.shape[0] // 4
    count = 2 * chips * rows
    out = jax.ShapeDtypeStruct((count, width), BF16)
    operands = (ids, *blocks, weights, cosine, sine) + (() if first is None else (first,))
    return pl.pallas_call(
        functools.partial(project_kernel, first is not None, chips, rows, width),
        out_shape=(out, out, out),
        in_specs=[SMEM()] + [VMEM()] * (len(operands) - 1),
        out_specs=(VMEM(),) * 3,
        compiler_params=compiler_params(),
        cost_estimate=cost(
            flops=2 * count * depth * 3 * width,
            bytes_accessed=2 * count * depth + 6 * depth * width + 14 * count * width,
            transcendentals=0,
        ),
        name="project_heads",
    )(*operands)


def lanes_joined(pieces):
    return jnp.concatenate(pieces, axis=1)


def middle_kernel(chips, *refs):
    refs = list(refs)
    near = [refs.pop(0) for _ in range(chips)]
    far, weights, before, gain, attended_rows, middle, normed = refs
    rows = lanes_joined([n[0] for n in near] + [far[i] for i in range(chips)])
    attended_rows[...] = rows
    value = before[...] + jnp.dot(rows, weights[...], preferred_element_type=F32)
    middle[...] = value
    normed[...] = normed_rows(value, gain[...])


def middle_step(near, far, weights, before, gain):
    chips = len(near)
    rows, depth = before.shape
    features = weights.shape[0]
    return pl.pallas_call(
        functools.partial(middle_kernel, chips),
        out_shape=(
            jax.ShapeDtypeStruct((rows, features), BF16),
            jax.ShapeDtypeStruct((rows, depth), F32),
            jax.ShapeDtypeStruct((rows, depth), BF16),
        ),
        in_specs=[VMEM()] * (chips + 4),
        out_specs=(VMEM(),) * 3,
        compiler_params=compiler_params(),
        cost_estimate=cost(
            flops=2 * rows * features * depth,
            bytes_accessed=2 * features * depth + 14 * rows * depth,
            transcendentals=0,
        ),
        name="attention_out",
    )(*near, far, weights, before, gain)


def middle_back_kernel(chips, width, *refs):
    refs = list(refs)
    kept = refs.pop(0)
    middle, gain, weights, grad = refs[-8:-4]
    received = refs[:-8]
    total, rounded, gain_part, blocks = refs[-4:]
    back = kept[...]
    for term in received:
        back = back + term[...].astype(F32)
    part, gains = norm_back(middle[...], gain[...], back)
    value = grad[...] + part
    total[...] = value
    narrow = value.astype(BF16)
    rounded[...] = narrow
    gain_part[...] = jnp.broadcast_to(gains, gain_part.shape)
    heads = lax.dot_general(narrow, weights[...], NT, preferred_element_type=F32).astype(BF16)
    for core in range(2):
        for chip in range(chips):
            at = (core * chips + chip) * width
            blocks[chip, core] = heads[:, at : at + width]


def middle_back_step(kept, received, middle, gain, weights, grad, chips):
    rows, depth = middle.shape
    width = weights.shape[0] // (2 * chips)
    return pl.pallas_call(
        functools.partial(middle_back_kernel, chips, width),
        out_shape=(
            jax.ShapeDtypeStruct((rows, depth), F32),
            jax.ShapeDtypeStruct((rows, depth), BF16),
            jax.ShapeDtypeStruct((8, depth), F32),
            jax.ShapeDtypeStruct((chips, 2, rows, width), BF16),
        ),
        in_specs=[VMEM()] * (5 + len(received)),
        out_specs=(VMEM(),) * 4,
        compiler_params=compiler_params(),
        cost_estimate=cost(
            flops=2 * rows * weights.shape[0] * depth,
            bytes_accessed=2 * weights.shape[0] * depth + 20 * rows * depth,
            transcendentals=0,
        ),
        name="attention_out_back",
    )(kept, *received, middle, gain, weights, grad)


def weights_copies(layer, refs, held, arrived):
    copies = [
        pltpu.make_async_copy(ref.at[layer], held.at[n], arrived.at[n])
        for n, ref in enumerate(refs)
    ]
    for copy in copies:
        copy.start()
    return copies


def feed_kernel(layer, shares, shards, *refs):
    refs = list(refs)
    held, arrived = refs[-2:]
    copies = weights_copies(layer, refs[shares : shares + 3 * shards], held, arrived)
    kept, sent = refs[-4:-2]
    mixed = jnp.concatenate([ref[...] for ref in refs[:shares]], axis=0)
    rows = kept.shape[0]
    total = None
    for at in range(0, 3 * shards, 3):
        copies[at].wait()
        gate = lax.dot_general(mixed, held[at], NT, preferred_element_type=F32)
        copies[at + 1].wait()
        upward = lax.dot_general(mixed, held[at + 1], NT, preferred_element_type=F32)
        hidden = (gate * jax.nn.sigmoid(gate) * upward).astype(BF16)
        copies[at + 2].wait()
        term = jnp.dot(hidden, held[at + 2], preferred_element_type=F32)
        total = term if total is None else total + term
    kept[...] = total[:rows]
    for share in range(1, shares):
        sent[share - 1] = total[share * rows : (share + 1) * rows].astype(BF16)


def held_weights(weights):
    return [
        pltpu.VMEM((len(weights), *weights[0].shape[1:]), BF16),
        pltpu.SemaphoreType.DMA((len(weights),)),
    ]


def feed_forward(layer, blocks, weights):
    shares = len(blocks)
    rows, depth = blocks[0].shape
    units = weights[0].shape[1] * len(weights) // 3
    return pl.pallas_call(
        functools.partial(feed_kernel, layer, shares, len(weights) // 3),
        out_shape=(
            jax.ShapeDtypeStruct((rows, depth), F32),
            jax.ShapeDtypeStruct((shares - 1, rows, depth), BF16),
        ),
        in_specs=[VMEM()] * shares + [pl.BlockSpec(memory_space=pl.ANY)] * len(weights),
        out_specs=(VMEM(),) * 2,
        scratch_shapes=held_weights(weights),
        compiler_params=compiler_params(),
        cost_estimate=cost(
            flops=6 * shares * rows * units * depth,
            bytes_accessed=6 * units * depth,
            transcendentals=shares * rows * units,
        ),
        name="feed_forward",
    )(*blocks, *weights)


def feed_back_kernel(layer, shares, shards, forward, *refs):
    refs = list(refs)
    held, arrived = refs[-2:]
    copies = weights_copies(layer, refs[2 * shares : 2 * shares + 3 * shards], held, arrived)
    mixed = jnp.concatenate([ref[...] for ref in refs[:shares]], axis=0)
    grads = jnp.concatenate([ref[...] for ref in refs[shares : 2 * shares]], axis=0)
    outs = refs[2 * shares + 3 * shards : -2]
    kept, sent = outs[:2]
    rows = kept.shape[0]
    total, forward_total = None, None
    for at in range(0, 3 * shards, 3):
        hidden_out, gate_out, up_out = outs[2 + at : 5 + at]
        copies[at].wait()
        gate = lax.dot_general(mixed, held[at], NT, preferred_element_type=F32)
        copies[at + 1].wait()
        upward = lax.dot_general(mixed, held[at + 1], NT, preferred_element_type=F32)
        sigmoid = jax.nn.sigmoid(gate)
        swish = gate * sigmoid
        hidden = (swish * upward).astype(BF16)
        hidden_out[...] = hidden
        copies[at + 2].wait()
        hidden_grad = lax.dot_general(grads, held[at + 2], NT, preferred_element_type=F32)
        gate_back = (hidden_grad * upward * (sigmoid + swish * (1 - sigmoid))).astype(BF16)
        up_back = (hidden_grad * swish).astype(BF16)
        gate_out[...] = gate_back
        up_out[...] = up_back
        term = jnp.dot(gate_back, held[at], preferred_element_type=F32)
        term = term + jnp.dot(up_back, held[at + 1], preferred_element_type=F32)
        total = term if total is None else total + term
        if forward:
            term = jnp.dot(hidden, held[at + 2], preferred_element_type=F32)
            forward_total = term if forward_total is None else forward_total + term
    kept[...] = total[:rows]
    for share in range(1, shares):
        sent[share - 1] = total[share * rows : (share + 1) * rows].astype(BF16)
    if forward:
        forward_kept, forward_sent = outs[-2:]
        forward_kept[...] = forward_total[:rows]
        for share in range(1, shares):
            forward_sent[share - 1] = forward_total[share * rows : (share + 1) * rows].astype(BF16)


def feed_back(layer, blocks, grads, weights, forward):
    shares = len(blocks)
    rows, depth = blocks[0].shape
    units = weights[0].shape[1]
    wide = jax.ShapeDtypeStruct((shares * rows, units), BF16)
    terms = (
        jax.ShapeDtypeStruct((rows, depth), F32),
        jax.ShapeDtypeStruct((shares - 1, rows, depth), BF16),
    )
    out_shape = terms + (wide,) * len(weights) + (terms if forward else ())
    return pl.pallas_call(
        functools.partial(feed_back_kernel, layer, shares, len(weights) // 3, forward),
        out_shape=out_shape,
        in_specs=[VMEM()] * (2 * shares) + [pl.BlockSpec(memory_space=pl.ANY)] * len(weights),
        out_specs=(VMEM(),) * len(out_shape),
        scratch_shapes=held_weights(weights),
        compiler_params=compiler_params(),
        cost_estimate=cost(
            flops=4 * shares * rows * units * len(weights) * depth,
            bytes_accessed=2 * units * len(weights) * depth,
            transcendentals=shares * rows * units,
        ),
        name="feed_backward",
    )(*blocks, *grads, *weights)


def feed_weights_kernel(shares, added, blocks, *refs):
    refs = list(refs)
    places = refs.pop(0) if blocks else None
    hidden, gate_back, up_back = (refs.pop(0)[...] for _ in range(3))
    mixed = jnp.concatenate([refs.pop(0)[...] for _ in range(shares)], axis=0)
    grads = jnp.concatenate([refs.pop(0)[...] for _ in range(shares)], axis=0)
    received = refs.pop(0) if added else None
    units = hidden.shape[1]
    half = 3 * units // 2
    for index, (left, right) in enumerate(((gate_back, mixed), (up_back, mixed), (hidden, grads))):
        start = index * units
        term = lax.dot_general(left, right, TN, preferred_element_type=F32)
        if added:
            term = term + received[start : start + units, :].astype(F32)
        term = term.astype(BF16)
        if not blocks:
            refs[0][start : start + units, :] = term
            continue
        size = term.shape[1] // blocks
        for part in range(2):
            low, high = max(start, part * half), min(start + units, (part + 1) * half)
            if low >= high:
                continue
            for block in range(blocks):
                piece = term[low - start : high - start, block * size : (block + 1) * size]
                refs[part][block ^ places[part], low - part * half : high - part * half, :] = piece


def feed_weights(activations, mixed, grads, received, places=None, blocks=0):
    shares = len(mixed)
    units = activations[0].shape[1]
    rows, depth = mixed[0].shape
    operands = [*activations, *mixed, *grads] + ([] if received is None else [received])
    specs = [VMEM()] * len(operands)
    if blocks:
        operands = [places] + operands
        specs = [SMEM()] + specs
        out = jax.ShapeDtypeStruct((blocks, 3 * units // 2, depth // blocks), BF16)
        out_shape, out_specs = (out, out), (VMEM(), VMEM())
    else:
        out_shape, out_specs = jax.ShapeDtypeStruct((3 * units, depth), BF16), VMEM()
    return pl.pallas_call(
        functools.partial(feed_weights_kernel, shares, received is not None, blocks),
        out_shape=out_shape,
        in_specs=specs,
        out_specs=out_specs,
        compiler_params=compiler_params(),
        cost_estimate=cost(
            flops=6 * shares * rows * units * depth,
            bytes_accessed=6 * units * depth,
            transcendentals=0,
        ),
        name="feed_weight_grads",
    )(*operands)


def place_kernel(units, places, first, second, summed, *outs):
    layer = pl.program_id(0)

    def write(rows):
        rows = rows.astype(F32)
        for n, out in enumerate(outs):
            out[0] = rows[n * units : (n + 1) * units]

    @pl.when(layer == 0)
    def _():
        write(jnp.concatenate([first[0], second[0]], axis=0))

    @pl.when(layer > 0)
    def _():
        write(summed[0])


def place_feed(places, first, second, summed):
    blocks, half, size = first.shape
    layers = summed.shape[0] + 1
    units = 2 * half // 3
    out = jax.ShapeDtypeStruct((layers, units, blocks * size), F32)

    def part(index):
        return pl.BlockSpec(
            (1, half, size),
            lambda layer, block, places: (
                jnp.where(layer == 0, block ^ places[index], (blocks - 1) ^ places[index]), 0, 0,
            ),
        )

    return pl.pallas_call(
        functools.partial(place_kernel, units),
        out_shape=(out,) * 3,
        grid_spec=pltpu.PrefetchScalarGridSpec(
            num_scalar_prefetch=1,
            grid=(layers, blocks),
            in_specs=[
                part(0),
                part(1),
                pl.BlockSpec(
                    (1, 2 * half, size),
                    lambda layer, block, places: (
                        jnp.maximum(layer - 1, 0), 0, jnp.where(layer == 0, 0, block),
                    ),
                ),
            ],
            out_specs=[
                pl.BlockSpec((1, units, size), lambda layer, block, places: (layer, 0, block))
            ]
            * 3,
        ),
        compiler_params=compiler_params(),
        name="place_feed_grads",
    )(places, first, second, summed)


def head_weights_kernel(raws, *refs):
    out = refs[-1]
    rows = jnp.concatenate([ref[...] for ref in refs[:-1]], axis=0)
    left = raws[...].reshape(rows.shape[0], raws.shape[-1])
    out[...] = lax.dot_general(left, rows, TN, preferred_element_type=F32).astype(BF16)


def head_weights(raws, blocks):
    rows, depth = blocks[0].shape
    wide = raws.shape[-1]
    return pl.pallas_call(
        head_weights_kernel,
        out_shape=jax.ShapeDtypeStruct((wide, depth), BF16),
        in_specs=[VMEM()] * (1 + len(blocks)),
        out_specs=VMEM(),
        compiler_params=compiler_params(),
        cost_estimate=cost(
            flops=2 * len(blocks) * rows * wide * depth,
            bytes_accessed=2 * len(blocks) * rows * (wide + depth),
            transcendentals=0,
        ),
        name="head_weight_grads",
    )(raws, *blocks)


def attend_kernel(chips, rows, width, *refs):
    ids, queries, keys, values, attended, log_totals = refs
    heads = width // HEAD_DIM
    count = 2 * chips * rows
    units = max(count // SEQ_UNIT, 1)
    unit_rows = count // units
    for block in range(2 * chips):
        first = block * rows
        own_unit = first // unit_rows
        segments = [(unit * unit_rows, unit_rows, unit, False) for unit in range(own_unit)]
        if first > own_unit * unit_rows:
            segments.append((own_unit * unit_rows, first - own_unit * unit_rows, None, False))
        segments.append((first, rows, None, True))
        query_all = queries[first : first + rows, :]
        outs = None
        lane = lax.broadcasted_iota(jnp.int32, (rows, 128), 1)
        totals_wide = jnp.zeros((rows, 128), F32)
        for head in range(heads):
            query = head_masked(query_all, head)
            scores, biases, tops = [], [], []
            for start, length, unit, diagonal in segments:
                score = lax.dot_general(
                    query, keys[start : start + length, :], NT, preferred_element_type=F32
                )
                if diagonal:
                    row = lax.broadcasted_iota(jnp.int32, score.shape, 0)
                    column = lax.broadcasted_iota(jnp.int32, score.shape, 1)
                    score = jnp.where(column <= row, score, NEG_LARGE)
                bias = 0.0
                if unit is not None:
                    bias = jnp.where(ids[2 + own_unit * units + unit] > 0, 0.0, NEG_LARGE)
                scores.append(score)
                biases.append(bias)
                tops.append(jnp.max(score, axis=1, keepdims=True) + bias)
            highest = functools.reduce(jnp.maximum, tops)
            summed, total = None, None
            for (start, length, unit, diagonal), score, bias in zip(segments, scores, biases):
                weight = jnp.exp(score - (highest - bias))
                narrow = weight.astype(BF16)
                value = values[start : start + length, :]
                if heads > 1:
                    value_lane = lax.broadcasted_iota(jnp.int32, value.shape, 1)
                    value = jnp.where(value_lane // HEAD_DIM == head, value, jnp.ones_like(value))
                else:
                    part_total = jnp.sum(weight, axis=1, keepdims=True)
                    total = part_total if total is None else total + part_total
                product = jnp.dot(narrow, value, preferred_element_type=F32)
                summed = product if summed is None else summed + product
            if heads > 1:
                spread = pltpu.roll(summed, HEAD_DIM, 1)
                divided = head_masked(summed / spread, head)
                total = jnp.where(lane // HEAD_DIM == head, spread, summed)
                logs = highest + jnp.log(total)
            else:
                divided = summed / total
                logs = jnp.broadcast_to(highest + jnp.log(total), (rows, 128))
            outs = divided if outs is None else outs + divided
            totals_wide = jnp.where(lane == head, logs, totals_wide)
        attended[(block % chips) ^ ids[0], (block // chips) ^ ids[1]] = outs.astype(BF16)
        log_totals[:, first : first + rows] = totals_wide.T[:8]


def attend(ids, queries, keys, values, chips, rows):
    count, width = queries.shape
    heads = width // HEAD_DIM
    pairs = count * count // 2
    return pl.pallas_call(
        functools.partial(attend_kernel, chips, rows, width),
        out_shape=(
            jax.ShapeDtypeStruct((chips, 2, rows, width), BF16),
            jax.ShapeDtypeStruct((8, count), F32),
        ),
        in_specs=[SMEM()] + [VMEM()] * 3,
        out_specs=(VMEM(),) * 2,
        compiler_params=compiler_params(),
        cost_estimate=cost(
            flops=heads * pairs * 256 * 8,
            bytes_accessed=2 * count * width * 4,
            transcendentals=heads * pairs,
        ),
        name="attend_forward",
    )(ids, queries, keys, values)


def attend_back_kernel(chips, rows, width, layer_first, *refs):
    refs = list(refs)
    ids, queries, keys, values, attended = (refs.pop(0) for _ in range(5))
    near = [refs.pop(0) for _ in range(chips)]
    far, log_totals, cosine, sine = (refs.pop(0) for _ in range(4))
    later_layer = refs.pop(0) if layer_first else None
    outs, grad_rows, inner, query_total, key_total, value_total = refs
    heads = width // HEAD_DIM
    count = 2 * chips * rows
    units = max(count // SEQ_UNIT, 1)
    unit_rows = count // units

    for core in range(2):
        for chip in range(chips):
            at = place_of(ids, core, chip, chips, rows)
            grad = near[chip][0] if core == 0 else far[chip]
            grad_rows[at, :] = grad
            query_total[at, :] = grad.astype(F32) * attended[chip, core].astype(F32)
    turned = query_total[...].T
    for head in range(heads):
        inner[head : head + 1, :] = jnp.sum(
            turned[head * HEAD_DIM : (head + 1) * HEAD_DIM], axis=0, keepdims=True
        )
    query_total[...] = jnp.zeros_like(query_total)
    key_total[...] = jnp.zeros_like(key_total)
    value_total[...] = jnp.zeros_like(value_total)

    def work(key_start, key_count, query_start, diagonal):
        at = pl.ds(key_start, key_count)
        query_at = pl.ds(query_start, rows)
        key, value = keys[at, :], values[at, :]
        key_part, value_part, query_part = None, None, None
        for head in range(heads):
            query = head_masked(queries[query_at, :], head)
            grad = head_masked(grad_rows[query_at, :], head)
            score = lax.dot_general(key, query, NT, preferred_element_type=F32)
            weight = jnp.exp(score - log_totals[head : head + 1, query_at])
            if diagonal:
                row = lax.broadcasted_iota(jnp.int32, score.shape, 0)
                column = lax.broadcasted_iota(jnp.int32, score.shape, 1)
                weight = jnp.where(row <= column, weight, 0.0)
            back = lax.dot_general(value, grad, NT, preferred_element_type=F32)
            score_back = (weight * (back - inner[head : head + 1, query_at])).astype(BF16)
            narrow = weight.astype(BF16)
            value_term = jnp.dot(narrow, grad, preferred_element_type=F32)
            key_term = jnp.dot(score_back, query, preferred_element_type=F32)
            query_term = lax.dot_general(
                score_back, head_masked(key, head), TN, preferred_element_type=F32
            )
            if head == 0:
                key_part, value_part, query_part = key_term, value_term, query_term
            else:
                key_part, value_part, query_part = (
                    key_part + key_term, value_part + value_term, query_part + query_term,
                )
        key_total[at, :] += key_part
        value_total[at, :] += value_part
        query_total[query_at, :] += query_part

    for unit in range(units):
        start = unit * unit_rows
        blocks = unit_rows // rows
        for other in range(unit):
            @pl.when(ids[2 + unit * units + other] > 0)
            def _():
                @pl.loop(0, blocks)
                def _(index):
                    at = pl.multiple_of(start + index * rows, rows)
                    work(other * unit_rows, unit_rows, at, False)
        for index in range(blocks):
            if index:
                work(start, index * rows, start + index * rows, False)
            work(start + index * rows, rows, start + index * rows, True)

    for core in range(2):
        for chip in range(chips):
            at = place_of(ids, core, chip, chips, rows)
            turn_at = table_rows(ids, core, chip, chips, rows)
            cos, sin = cosine[turn_at, :], sine[turn_at, :]
            query = query_total[at, :] * HEAD_DIM**-0.5
            key = key_total[at, :]
            value = value_total[at, :]
            query = query * cos - half_turn(query) * sin
            key = key * cos - half_turn(key) * sin
            if layer_first:
                value = value + later_layer[core, chip, :, 2 * width :].astype(F32)
            else:
                value = value.astype(BF16).astype(F32) * 0.5
            outs[core, chip] = jnp.concatenate([query, key, value], axis=1).astype(BF16)


def attend_back(
    ids, queries, keys, values, attended, near, far, log_totals, cosine, sine, later_layer
):
    chips, _, rows, width = attended.shape
    count = queries.shape[0]
    heads = width // HEAD_DIM
    pairs = count * count // 2
    operands = [ids, queries, keys, values, attended, *near, far, log_totals, cosine, sine]
    if later_layer is not None:
        operands.append(later_layer)
    return pl.pallas_call(
        functools.partial(attend_back_kernel, chips, rows, width, later_layer is not None),
        out_shape=jax.ShapeDtypeStruct((2, chips, rows, 3 * width), BF16),
        in_specs=[SMEM()] + [VMEM()] * (len(operands) - 1),
        out_specs=VMEM(),
        scratch_shapes=[
            pltpu.VMEM((count, width), BF16),
            pltpu.VMEM((8, count), F32),
            pltpu.VMEM((count, width), F32),
            pltpu.VMEM((count, width), F32),
            pltpu.VMEM((count, width), F32),
        ],
        compiler_params=compiler_params(),
        cost_estimate=cost(
            flops=heads * pairs * 256 * 20,
            bytes_accessed=2 * count * width * 20,
            transcendentals=heads * pairs,
        ),
        name="attend_backward",
    )(*operands)


def rms_factor(values):
    return lax.rsqrt(jnp.mean(values * values, axis=-1, keepdims=True) + EPSILON)


def normed_rows(values, gain):
    return (values * rms_factor(values) * gain).astype(BF16)


def norm_back(values, gain, back):
    factor = rms_factor(values)
    scaled = back * gain
    mean = jnp.mean(scaled * values, axis=-1, keepdims=True)
    gain_grad = jnp.sum(back * values * factor, axis=0)
    return factor * scaled - values * (factor * factor * factor * mean), gain_grad


def matmul(left, right):
    return jnp.dot(left, right, preferred_element_type=F32)


def matmul_nt(left, right):
    return lax.dot_general(left, right, NT, preferred_element_type=F32)


def matmul_tn(left, right):
    return lax.dot_general(left, right, TN, preferred_element_type=F32)


def flat(blocks):
    return blocks.reshape(-1, blocks.shape[-1])


def per_device(
    head_axes, hid_axes, inputs, cotangent, segments, attn_gain, w_query, w_key, w_value, w_out,
    mlp_gain, w_gate, w_up, w_down,
):
    layers = w_query.shape[0]
    core = hid_axes[-1]
    group_axes = head_axes[1:]
    share_axes = hid_axes[:-1]
    chips = 2 ** len(group_axes)
    rows = inputs.shape[0]
    count = 2 * chips * rows
    width = w_query.shape[2]
    units = max(count // SEQ_UNIT, 1)
    share_at = lax.axis_index(share_axes[0])

    def index_of(axes):
        at = jnp.int32(0)
        for axis in axes:
            at = at * 2 + lax.axis_index(axis)
        return at

    def turn(value):
        return lax.ppermute(value, (head_axes[0], core), TURN)

    unit_axes = ((core,) + group_axes)[: (units - 1).bit_length()]
    number = turn(jnp.broadcast_to(segments[:1], (8, 128)))
    unit_at = index_of(unit_axes)
    def group_ids(number):
        numbers = jnp.stack(
            [number] + [swap(number, axes_of(i, unit_axes)) for i in range(1, units)]
        )[:, 0, 0]
        numbers = jnp.stack(
            [lax.dynamic_index_in_dim(numbers, unit ^ unit_at, 0, False) for unit in range(units)]
        )
        same = (numbers[:, None] == numbers[None, :]).astype(jnp.int32)
        places = jnp.stack([index_of(group_axes), lax.axis_index(core)]).astype(jnp.int32)
        earlier_units = np.tril(np.ones((units, units), np.int32), -1)
        starts = jnp.sum(same * earlier_units, axis=1) * SEQ_UNIT
        return jnp.concatenate([places, same.reshape(-1), starts])

    feed_orders = (head_axes[::-1], (head_axes[1], *head_axes[:1:-1], head_axes[0]))
    feed_places = jnp.stack([index_of(order) for order in feed_orders]).astype(jnp.int32)
    frequency = np.float32(THETA) ** (-np.arange(HEAD_DIM // 2, dtype=np.float32) * 2 / HEAD_DIM)
    frequency = np.tile(frequency.astype(np.float32), 2 * width // HEAD_DIM)[None]
    signs = np.where(np.arange(width) % HEAD_DIM < HEAD_DIM // 2, -1.0, 1.0).astype(np.float32)
    angles = jnp.arange(count, dtype=jnp.int32).astype(F32)[:, None] * frequency
    cosine, sine = jnp.cos(angles), jnp.sin(angles) * signs

    feed_all = (w_gate.transpose(0, 2, 1), w_up.transpose(0, 2, 1), w_down)

    def joined_shares(piece):
        other = swap(piece, share_axes[:1])
        return jnp.where(
            share_at == 0,
            jnp.concatenate([piece, other], axis=0),
            jnp.concatenate([other, piece], axis=0),
        )

    packed = pack_heads(share_at[None].astype(jnp.int32), (w_query, w_key, w_value, w_out))

    def add_received(total, sent):
        for i in range(1, 1 + sent.shape[0]):
            total = total + swap(sent[i - 1], axes_of(i, share_axes)).astype(F32)
        return total

    attn_gains = [attn_gain[n][None] for n in range(layers)]
    mlp_gains = [mlp_gain[n][None] for n in range(layers)]
    residual = turn(inputs)
    w_heads = [turn(packed[0])] + [None] * (layers - 1)
    residual, cosine, sine, w_heads[0] = lax.optimization_barrier(
        (residual, cosine, sine, w_heads[0])
    )
    residual = residual.astype(F32)
    w_outs = [None] * layers

    stored = []
    first_values = None
    for layer in range(layers):
        final = layer == layers - 1
        before = residual
        w_heads[layer] = joined_shares(after(w_heads[layer], before))
        near, far = gather(
            normed_rows(before, attn_gains[layer]), group_axes, core, w_heads[layer]
        )
        blocks = near + far
        if layer == 0:
            ids = group_ids(after(number, near[1]))
        queries, keys, values = project(ids, blocks, w_heads[layer], cosine, sine, first_values)
        if layer == 0:
            first_values = values
            feeds = [swap(after(w, queries), (core,)) for w in feed_all[:2]]
        out_chips = gather_chips(after(w_heads[layer][3 * width :], queries), group_axes)
        attended, log_totals = attend(ids, queries, keys, values, chips, rows)
        attended = after(attended, *out_chips[1:], *(feeds if layer == 0 else ()))
        if layer == 1:
            down_in = gather_chips(after(grad, queries), share_axes)
        near, far = exchange(attended, group_axes, core)
        out_chips = after(jnp.concatenate(out_chips, axis=0), near[-1])
        w_outs[layer] = jnp.concatenate([out_chips, swap(out_chips, (core,))], axis=0)
        if layer == 0:
            feeds.append(swap(after(feed_all[2], far), (core,)))
            feed_all = feed_all + tuple(feeds)
            grad = turn(after(cotangent, far))
        if layer == 1:
            far = after(far, down_in[-1])
        attended_rows, middle, normed = middle_step(
            near, far, w_outs[layer], before, mlp_gains[layer]
        )
        mixed = gather_chips(normed, share_axes)
        stored.append(
            dict(
                before=before, blocks=blocks, queries=queries, keys=keys, values=values,
                attended=attended, log_totals=log_totals, attended_rows=attended_rows,
                middle=middle, mixed=mixed,
            )
        )
        if not final:
            w_heads[layer + 1] = turn(after(packed[layer + 1], far))
            first_mixed = after(mixed[0], w_heads[layer + 1])
            own_term, sent = feed_forward(layer, [first_mixed] + mixed[1:], feed_all)
            residual = add_received(middle + own_term, sent)
            if layer == 0:
                residual = after(residual, grad)

    grad = grad.astype(F32)
    attn_grads, mlp_grads = [], []
    attn_gain_grads, mlp_gain_grads = [], []
    later_layer = None
    by_blocks = inputs.shape[1] % (128 * 2 ** len(head_axes)) == 0
    for layer in reversed(range(layers)):
        final = layer == layers - 1
        k = stored[layer]
        mixed = k["mixed"]
        if not final:
            down_in = gather_chips(grad.astype(BF16), share_axes)
        own_term, sent, *rest = feed_back(layer, mixed, down_in, feed_all, final)
        received = [swap(sent[i - 1], axes_of(i, share_axes)) for i in range(1, len(mixed))]
        other = swap(feed_weights(rest[3:6], mixed, down_in, None), (core,))
        ties = ()
        if layer:
            mlp_part = feed_weights(rest[:3], mixed, down_in, other)
            block = lax.psum_scatter(mlp_part, head_axes, scatter_dimension=0, tiled=True)
            mlp_grads.append(block)
            mlp_part = (mlp_part,)
        elif by_blocks:
            mlp_part = feed_weights(
                rest[:3], mixed, down_in, other, feed_places, 2 ** len(head_axes)
            )
            half = mlp_part[0].shape[0] // 2
            ties = [swap(p[half:], order[:1]) for p, order in zip(mlp_part, feed_orders)]
        else:
            mlp_part = (feed_weights(rest[:3], mixed, down_in, other),)
            mlp_grads.append(lax.psum(mlp_part[0], head_axes[::-1]))
        if not final:
            own_term = after(own_term, mlp_grads[0])
            mlp_grads[0] = lax.all_gather(mlp_grads[0], head_axes, axis=0, tiled=True)
        middle_back, attn_in, gain_part, heads_back = middle_back_step(
            own_term, received, k["middle"], mlp_gains[layer], w_outs[layer], grad, chips
        )
        mlp_gain_grads.append(gain_part[0])
        near, far = exchange(heads_back, group_axes, core)
        if final:
            block_out = add_received(k["middle"] + rest[6], after(rest[7], far)).astype(BF16)
        raws = attend_back(
            ids, after(k["queries"], *mlp_part), k["keys"], k["values"], k["attended"], near, far,
            k["log_totals"], cosine, sine, later_layer,
        )
        later_layer = raws
        into = w_heads[layer][: 3 * width]
        others = matmul(flat(raws[1]), into).astype(BF16).reshape(chips, rows, -1)
        mine = matmul(flat(raws[0]), into).reshape(chips, rows, -1)
        normed_in = scatter_sum(mine, others, group_axes, core, *ties)
        part, gain_part = norm_back(k["before"], attn_gains[layer], normed_in)
        attn_gain_grads.append(gain_part)
        grad = middle_back + part
        if not final:
            grad = after(grad, mlp_grads[0])
        attn_in = after(attn_in, grad)
        out_terms = matmul_tn(k["attended_rows"], attn_in).reshape(2, chips, width, -1)
        out_grad = scatter_sum(out_terms[0], out_terms[1].astype(BF16), group_axes, core)
        heads_grad = head_weights(after(raws, grad), k["blocks"])
        attn_grads.append(jnp.concatenate([heads_grad, out_grad.astype(BF16)], axis=0))

    joined = jnp.stack(attn_grads[::-1], axis=1)
    kept_part = lax.dynamic_slice_in_dim(joined, share_at * 2 * width, 2 * width, 0)
    sent_part = lax.dynamic_slice_in_dim(joined, (1 - share_at) * 2 * width, 2 * width, 0)
    summed = kept_part.astype(F32) + swap(sent_part, share_axes[:1]).astype(F32)
    summed = exchange_sum(turn(summed.astype(BF16)), (core,) + share_axes[1:])
    attn_all = joined_shares(summed).astype(F32).transpose(1, 0, 2)

    given = turn(jnp.stack([block_out, grad.astype(BF16)]))
    gains = exchange_sum(
        jnp.stack(attn_gain_grads[::-1] + mlp_gain_grads[::-1]), hid_axes[::-1] + head_axes, F32
    )
    if by_blocks:
        spread = [
            spread_blocks(reduce_blocks(part[:half], received, order), order)
            for part, received, order in zip(mlp_part, ties, feed_orders)
        ]
        feed_grads = place_feed(feed_places, *spread, jnp.stack(mlp_grads[::-1]))
    else:
        mlp_all = jnp.stack(mlp_grads[::-1]).astype(F32)
        size = w_gate.shape[2]
        feed_grads = [mlp_all[:, n * size : (n + 1) * size] for n in range(3)]
    return (
        given[0],
        given[1].astype(F32),
        gains[:layers],
        attn_all[:, :width].transpose(0, 2, 1),
        attn_all[:, width : 2 * width].transpose(0, 2, 1),
        attn_all[:, 2 * width : 3 * width].transpose(0, 2, 1),
        attn_all[:, 3 * width :],
        gains[layers:],
        feed_grads[0].transpose(0, 2, 1),
        feed_grads[1].transpose(0, 2, 1),
        feed_grads[2],
    )


def solution(mesh):
    head_bits = (mesh.shape["heads"] - 1).bit_length()
    hid_bits = (mesh.shape["hid"] - 1).bit_length()
    head_axes = tuple(f"heads{n}" for n in range(head_bits))
    hid_axes = tuple(f"hid{n}" for n in range(hid_bits))
    binary = Mesh(mesh.devices.reshape((2,) * (head_bits + hid_bits)), head_axes + hid_axes)
    tokens = hid_axes + head_axes
    in_specs = (
        P(tokens, None),
        P(tokens, None),
        P(tokens),
        P(),
        P(None, None, head_axes),
        P(None, None, head_axes),
        P(None, None, head_axes),
        P(None, head_axes, None),
        P(),
        P(None, None, hid_axes),
        P(None, None, hid_axes),
        P(None, hid_axes, None),
    )
    out_specs = (
        P(tokens, None),
        P(tokens, None),
        P(),
        P(None, None, head_axes),
        P(None, None, head_axes),
        P(None, None, head_axes),
        P(None, head_axes, None),
        P(),
        P(None, None, hid_axes),
        P(None, None, hid_axes),
        P(None, hid_axes, None),
    )
    return jax.shard_map(
        functools.partial(per_device, head_axes, hid_axes),
        mesh=binary,
        in_specs=in_specs,
        out_specs=out_specs,
        check_vma=False,
    )
```

time: 829 us -> 709 us (0.86)
  starting transfers between devices: 202 us -> 113 us
  matrix products: 81.6 us -> 8.74 us
  Pallas kernels: 52.9 us -> 122 us
  waiting for transfers between devices: 285 us -> 353 us
  blocking collectives: 48.4 us -> 0 us
  other arithmetic: 72.8 us -> 26.3 us
    ppermute x153 -> x92, waiting for transfers between devices: 223 us -> 352 us  [swap(): lax.ppermute(value, axes if len(axes) > 1 else axes[0], [(i, size - 1 - i...]
    pallas_call x8 -> x19, Pallas kernels: 44.8 us -> 114 us  [the longest x2 29.3 us: feed_back(): pl.pallas_call(functools.partial(feed_back_kernel, layer, shares, len(wei...]
    ppermute x153 -> x92, starting transfers between devices: 171 us -> 106 us  [swap(): lax.ppermute(value, axes if len(axes) > 1 else axes[0], [(i, size - 1 - i...]
    psum x1 -> x0, waiting for transfers between devices: 62.7 us -> none  [per_device(): lax.psum(part.astype(BF16), head_axes).astype(F32)]
    psum x1 -> x0, blocking collectives: 48.4 us -> none  [per_device(): lax.psum(jnp.stack(attn_gain_grads[::-1] + mlp_gain_grads[::-1]), head_ax...]
    another operation x64 -> x11, other arithmetic: 35.4 us -> 1.59 us  [the longest x4 0.85 us: exchange(): return (got, swap(jnp.stack([g[1] for g in got]), (core,)))]
    dot_general x20 -> x2, matrix products: 35 us -> 1.72 us  [matmul_tn(): return lax.dot_general(left, right, TN, preferred_element_type=F32)]
    unnamed x324 -> x285, local copies, waits for them, and re-layouts: 17.1 us -> 44.7 us
  transfers between devices with their start and end apart: 171 -> 101, of which waited for: 60 -> 53; matrix products, arithmetic and copies ran while one was open for 21% -> 6% of each run, Pallas kernels for 6% -> 12%
where the time goes in v2:
time: 709 us; the launch traced here: 699 us
  waiting for transfers between devices  353 us (50%)
  Pallas kernels  122 us (17%)
  starting transfers between devices  113 us (16%)
  local copies, waits for them, and re-layouts  57.1 us (8%)
  other arithmetic  26.3 us (4%)
  between operations  19 us (3%)
  matrix products  8.74 us (1%)
    ppermute x92, waiting for transfers between devices, swap(): lax.ppermute(value, axes if len(axes) > 1 else axes[0], [(i, size - 1 - i...  352 us
    ppermute x92, starting transfers between devices, swap(): lax.ppermute(value, axes if len(axes) > 1 else axes[0], [(i, size - 1 - i...  106 us
    unnamed x285, local copies, waits for them, and re-layouts  44.7 us
    pallas_call x2, Pallas kernels, feed_back(): pl.pallas_call(functools.partial(feed_back_kernel, layer, shares, len(wei...  29.3 us
    pallas_call x2, Pallas kernels, attend_back(): pl.pallas_call(functools.partial(attend_back_kernel, chips, rows, width,...  21.8 us
    pallas_call x2, Pallas kernels, attend(): pl.pallas_call(functools.partial(attend_kernel, chips, rows, width), out_...  19.8 us
    pallas_call x4, Pallas kernels, feed_weights(): pl.pallas_call(functools.partial(feed_weights_kernel, shares, received is...  15 us
  transfers between devices with their start and end apart: 101, of which 53 were waited for; matrix products, arithmetic and copies ran while one was open for 6% of the time, Pallas kernels for 12%

profile of v2, /device:TPU:0, one launch (start us, length us, event | category | flops | bytes accessed | tf_op | source)
XLA Modules:
  0.0 698.8 jit_solution(14255475670107634542)
XLA Ops:
  15.1 3.7 fusion.8
  20.2 2.8 collective-permute-start.6
  24.0 16.7 %collective-permute-start.5 = (bf16[256,1024]{1,0:T(8,128)(2,1)}, bf16[256,1024]{1,0:T(8,128)(2,1)}, u32[]{:S(2)}, u32[]{:S(2)}) collective-permute-start(bf16[256,1024]{1,0:T(8,128)(2,1)} %fusion.2.refs_1_.refs_0_), channel_id=1, source_target_pairs={{0,1},{1,0},{2,3},{3,2},{4,5},{5,4},{6,7},{7,6},{8,9},{9,8},{10,11... | collective-permute-start | bytes 1572872 | tf_op jit(solution)/shard_map/ppermute | solution.py:29
  47.2 7.7 %collective-permute-done.4.refs_3_.refs_2_ = bf16[256,1024]{1,0:T(8,128)(2,1)} collective-permute-done((bf16[256,1024]{1,0:T(8,128)(2,1)}, bf16[256,1024]{1,0:T(8,128)(2,1)}, u32[]{:S(2)}, u32[]{:S(2)}) %collective-permute-start.4) | collective-permute-done | bytes 524320 | tf_op jit(solution)/shard_map/ppermute | solution.py:29
  65.9 2.0 collective-permute-done.9
  70.9 4.7 project_heads.2
  79.8 10.1 %attend_forward.2 = (bf16[4,2,256,128]{3,2,1,0:T(8,128)(2,1)S(1)}, f32[8,2048]{1,0:T(8,128)S(1)}) custom-call(s32[8]{0:T(128)S(1)} %pad_add_fusion.1.refs_0_, bf16[2048,128]{1,0:T(8,128)(2,1)S(1)} %get-tuple-element.167.refs_1_, bf16[2048,128]{1,0:T(8,128)(2,1)S(1)} %get-tuple-element.108.refs_2_, bf16[2048,128]{1,0:T(8,128)(2,1)S(1)} %get-tuple-element.109.refs_3_.refs_12_), custom_call_target="tpu_custom_call" | custom-call | flops 171798688 | bytes 41943 | tf_op jit(solution)/shard_map/attend_forward/pallas_call | solution.py:638
  97.5 3.0 collective-permute-done.20.refs_3_
  105.6 5.2 collective-permute-done.22
  113.1 13.4 %collective-permute-done.24.refs_1_.refs_4_.refs_5_ = bf16[256,1024]{1,0:T(8,128)(2,1)S(1)} collective-permute-done((bf16[256,1024]{1,0:T(8,128)(2,1)S(1)}, bf16[256,1024]{1,0:T(8,128)(2,1)S(1)}, u32[]{:S(2)}, u32[]{:S(2)}) %collective-permute-start.24) | collective-permute-done | bytes 524320 | tf_op jit(solution)/shard_map/ppermute | solution.py:29
  128.3 8.4 %feed_forward.1 = (f32[256,1024]{1,0:T(8,128)S(1)}, bf16[1,256,1024]{2,1,0:T(8,128)(2,1)S(1)}) custom-call(bf16[256,1024]{1,0:T(8,128)(2,1)S(1)} %get-tuple-element.119.refs_0_.refs_3_.refs_4_, bf16[256,1024]{1,0:T(8,128)(2,1)S(1)} %collective-permute-done.24.refs_1_.refs_4_.refs_5_, bf16[2,704,1024]{2,1,0:T(8,128)(2,1)S(1)} %bitcast.188, ...), custom_call_target="tpu_custom_call" | custom-call | flops 88583696 | bytes 173015 | tf_op jit(solution)/shard_map/feed_forward/pallas_call | solution.py:347
  138.2 11.7 %collective-permute-done.26 = bf16[256,1024]{1,0:T(8,128)(2,1)S(1)} collective-permute-done((bf16[256,1024]{1,0:T(8,128)(2,1)S(1)}, bf16[256,1024]{1,0:T(8,128)(2,1)S(1)}, u32[]{:S(2)}, u32[]{:S(2)}) %collective-permute-start.26) | collective-permute-done | bytes 524320 | tf_op jit(solution)/shard_map/ppermute | solution.py:29
  151.1 5.4 collective-permute-start.30
  158.7 2.7 collective-permute-done.31
  161.9 8.5 %collective-permute-done.29.refs_3_.refs_2_ = bf16[256,1024]{1,0:T(8,128)(2,1)S(1)} collective-permute-done((bf16[256,1024]{1,0:T(8,128)(2,1)S(1)}, bf16[256,1024]{1,0:T(8,128)(2,1)S(1)}, u32[]{:S(2)}, u32[]{:S(2)}) %collective-permute-start.29) | collective-permute-done | bytes 524320 | tf_op jit(solution)/shard_map/ppermute | solution.py:29
  174.3 3.8 collective-permute-done.32
  181.2 3.0 project_heads.3
  187.9 9.7 %attend_forward.3 = (bf16[4,2,256,128]{3,2,1,0:T(8,128)(2,1)S(1)}, f32[8,2048]{1,0:T(8,128)S(1)}) custom-call(s32[8]{0:T(128)S(1)} %pad_add_fusion.1.refs_0_, bf16[2048,128]{1,0:T(8,128)(2,1)S(1)} %get-tuple-element.153.refs_1_, bf16[2048,128]{1,0:T(8,128)(2,1)S(1)} %get-tuple-element.130.refs_2_, bf16[2048,128]{1,0:T(8,128)(2,1)S(1)} %get-tuple-element.131.refs_3_), custom_call_target="tpu_custom_call" | custom-call | flops 171798688 | bytes 41943 | tf_op jit(solution)/shard_map/attend_forward/pallas_call | solution.py:638
  201.1 4.6 collective-permute-done.42.refs_3_
  208.4 3.5 collective-permute-done.41.refs_2_
  212.5 7.5 %collective-permute-done.44.refs_3_.refs_6_ = bf16[256,1024]{1,0:T(8,128)(2,1)S(1)} collective-permute-done((bf16[256,1024]{1,0:T(8,128)(2,1)S(1)}, bf16[256,1024]{1,0:T(8,128)(2,1)S(1)}, u32[]{:S(2)}, u32[]{:S(2)}) %collective-permute-start.44) | collective-permute-done | bytes 524320 | tf_op jit(solution)/shard_map/ppermute | solution.py:29
  223.3 13.0 %collective-permute-done.46.refs_1_.refs_4_ = bf16[256,1024]{1,0:T(8,128)(2,1)S(1)} collective-permute-done((bf16[256,1024]{1,0:T(8,128)(2,1)S(1)}, bf16[256,1024]{1,0:T(8,128)(2,1)S(1)}, u32[]{:S(2)}, u32[]{:S(2)}) %collective-permute-start.46) | collective-permute-done | bytes 524320 | tf_op jit(solution)/shard_map/ppermute | solution.py:29
  238.1 14.7 %feed_backward.2 = (f32[256,1024]{1,0:T(8,128)S(1)}, bf16[1,256,1024]{2,1,0:T(8,128)(2,1)S(1)}, bf16[512,704]{1,0:T(8,128)(2,1)S(1)}, bf16[512,704]{1,0:T(8,128)...) custom-call(bf16[256,1024]{1,0:T(8,128)(2,1)S(1)} %get-tuple-element, ...), custom_call_target="tpu_custom_call" | custom-call | flops 177167392 | bytes 173015 | tf_op jit(solution)/shard_map/feed_backward/pallas_call | solution.py:418
  253.7 2.4 feed_weight_grads.4
  256.2 7.3 %collective-permute-done.53.refs_7_ = bf16[2112,1024]{1,0:T(8,128)(2,1)S(1)} collective-permute-done((bf16[2112,1024]{1,0:T(8,128)(2,1)S(1)}, bf16[2112,1024]{1,0:T(8,128)(2,1)S(1)}, u32[]{:S(2)}, u32[]{:S(2)}) %collective-permute-start.53) | collective-permute-done | bytes 4325408 | tf_op jit(solution)/shard_map/ppermute | solution.py:29
  263.6 2.9 feed_weight_grads.5
  266.5 2.0 copy-done.14
  270.3 12.5 %collective-permute-done.47.refs_1_ = bf16[256,1024]{1,0:T(8,128)(2,1)S(1)} collective-permute-done((bf16[256,1024]{1,0:T(8,128)(2,1)}, bf16[256,1024]{1,0:T(8,128)(2,1)S(1)}, u32[]{:S(2)}, u32[]{:S(2)}) %collective-permute-start.47) | collective-permute-done | bytes 524320 | tf_op jit(solution)/shard_map/ppermute | solution.py:29
  290.5 10.9 %collective-permute-done.50.refs_8_ = bf16[2,256,128]{2,1,0:T(8,128)(2,1)S(1)} collective-permute-done((bf16[2,256,128]{2,1,0:T(8,128)(2,1)S(1)}, bf16[2,256,128]{2,1,0:T(8,128)(2,1)S(1)}, u32[]{:S(2)}, u32[]{:S(2)}) %collective-permute-start.50) | collective-permute-done | bytes 131104 | tf_op jit(solution)/shard_map/ppermute | solution.py:29
  301.4 7.2 %collective-permute-done.49.refs_7_ = bf16[2,256,128]{2,1,0:T(8,128)(2,1)S(1)} collective-permute-done((bf16[2,256,128]{2,1,0:T(8,128)(2,1)S(1)}, bf16[2,256,128]{2,1,0:T(8,128)(2,1)S(1)}, u32[]{:S(2)}, u32[]{:S(2)}) %collective-permute-start.49) | collective-permute-done | bytes 131104 | tf_op jit(solution)/shard_map/ppermute | solution.py:29
  310.2 10.5 %attend_backward.2.refs_13_.raws = bf16[2,4,256,384]{3,2,1,0:T(8,128)(2,1)S(1)} custom-call(s32[8]{0:T(128)S(1)} %pad_add_fusion.1.refs_0_, bf16[2048,128]{1,0:T(8,128)(2,1)S(1)} %copy-done.74, bf16[2048,128]{1,0:T(8,128)(2,1)S(1)} %copy-done.76, bf16[2048,128]{1,0:T(8,128)(2,1)S(1)} %copy-done.78, bf16[4,2,256,128]{3,2,1,0:T(8,128)(2,1)S(1)} %copy-done.56, ...), custom_call_target="tpu_custom_call" | custom-call | flops 429496736 | bytes 209715 | tf_op jit(solution)/shard_map/attend_backward/pallas_call | solution.py:757
  322.4 4.0 collective-permute-done.54
  328.5 2.8 collective-permute-start.56
  331.3 25.3 %collective-permute-done.55 = bf16[256,1024]{1,0:T(8,128)(2,1)S(1)} collective-permute-done((bf16[256,1024]{1,0:T(8,128)(2,1)S(1)}, bf16[256,1024]{1,0:T(8,128)(2,1)S(1)}, u32[]{:S(2)}, u32[]{:S(2)}) %collective-permute-start.55) | collective-permute-done | bytes 524320 | tf_op jit(solution)/shard_map/ppermute | solution.py:29
  359.9 12.3 %collective-permute-done.58.refs_3_.refs_6_.refs_7_ = bf16[256,1024]{1,0:T(8,128)(2,1)S(1)} collective-permute-done((bf16[256,1024]{1,0:T(8,128)(2,1)S(1)}, bf16[256,1024]{1,0:T(8,128)(2,1)S(1)}, u32[]{:S(2)}, u32[]{:S(2)}) %collective-permute-start.58) | collective-permute-done | bytes 524320 | tf_op jit(solution)/shard_map/ppermute | solution.py:29
  372.2 14.6 %feed_backward.3 = (f32[256,1024]{1,0:T(8,128)S(1)}, bf16[1,256,1024]{2,1,0:T(8,128)(2,1)S(1)}, bf16[512,704]{1,0:T(8,128)(2,1)S(1)}, bf16[512,704]{1,0:T(8,128)...) custom-call(bf16[256,1024]{1,0:T(8,128)(2,1)S(1)} %copy-done.26, ...), custom_call_target="tpu_custom_call" | custom-call | flops 177167392 | bytes 173015 | tf_op jit(solution)/shard_map/feed_backward/pallas_call | solution.py:418
  386.9 4.5 feed_weight_grads.6
  393.0 13.1 %collective-permute-done.59.refs_1_ = bf16[256,1024]{1,0:T(8,128)(2,1)S(1)} collective-permute-done((bf16[256,1024]{1,0:T(8,128)(2,1)}, bf16[256,1024]{1,0:T(8,128)(2,1)S(1)}, u32[]{:S(2)}, u32[]{:S(2)}) %collective-permute-start.59) | collective-permute-done | bytes 524320 | tf_op jit(solution)/shard_map/ppermute | solution.py:29
  416.6 10.2 %collective-permute-done.63.refs_8_ = bf16[2,256,128]{2,1,0:T(8,128)(2,1)S(1)} collective-permute-done((bf16[2,256,128]{2,1,0:T(8,128)(2,1)S(1)}, bf16[2,256,128]{2,1,0:T(8,128)(2,1)S(1)}, u32[]{:S(2)}, u32[]{:S(2)}) %collective-permute-start.63) | collective-permute-done | bytes 131104 | tf_op jit(solution)/shard_map/ppermute | solution.py:29
  426.7 2.3 collective-permute-done.62.refs_7_
  436.7 5.2 feed_weight_grads.7
  442.0 11.2 %attend_backward.3.raws = bf16[2,4,256,384]{3,2,1,0:T(8,128)(2,1)S(1)} custom-call(s32[8]{0:T(128)S(1)} %pad_add_fusion.1.refs_0_, bf16[2048,128]{1,0:T(8,128)(2,1)S(1)} %copy-done.70, bf16[2048,128]{1,0:T(8,128)(2,1)S(1)} %copy-done.72, bf16[2048,128]{1,0:T(8,128)(2,1)S(1)} %copy-done.37, bf16[4,2,256,128]{3,2,1,0:T(8,128)(2,1)S(1)} %copy-done.54, ...), custom_call_target="tpu_custom_call" | custom-call | flops 429496736 | bytes 209715 | tf_op jit(solution)/shard_map/attend_backward/pallas_call | solution.py:757
  466.7 3.3 fusion.47
  470.0 26.4 %collective-permute-done.67 = bf16[4,1056,128]{2,1,0:T(8,128)(2,1)S(1)} collective-permute-done((bf16[4,1056,128]{2,1,0:T(8,128)(2,1)S(1)}, bf16[4,1056,128]{2,1,0:T(8,128)(2,1)S(1)}, u32[]{:S(2)}, u32[]{:S(2)}) %collective-permute-start.67) | collective-permute-done | bytes 1081376 | tf_op jit(solution)/shard_map/ppermute | solution.py:29
  499.7 2.1 collective-permute-start.69
  510.3 14.7 %collective-permute-done.68 = bf16[256,1024]{1,0:T(8,128)(2,1)} collective-permute-done((bf16[256,1024]{1,0:T(8,128)(2,1)}, bf16[256,1024]{1,0:T(8,128)(2,1)}, u32[]{:S(2)}, u32[]{:S(2)}) %collective-permute-start.68) | collective-permute-done | bytes 524320 | tf_op jit(solution)/shard_map/ppermute | solution.py:29
  525.1 4.7 collective-permute-done.69
  529.7 2.3 fusion.7
  539.7 2.7 collective-permute-start.80
  542.7 8.9 %collective-permute-done.94 = bf16[2,1056,128]{2,1,0:T(8,128)(2,1)S(1)} collective-permute-done((bf16[2,1056,128]{2,1,0:T(8,128)(2,1)S(1)}, bf16[2,1056,128]{2,1,0:T(8,128)(2,1)S(1)}, u32[]{:S(2)}, u32[]{:S(2)}) %collective-permute-start.94) | collective-permute-done | bytes 540704 | tf_op jit(solution)/shard_map/ppermute | solution.py:29
  551.7 2.9 collective-permute-start.95
  554.6 4.0 head_weight_grads.2
  558.6 6.0 collective-permute-done.80
  564.6 4.2 collective-permute-done.79
  574.0 17.6 %collective-permute-done.90 = bf16[1,1056,128]{2,1,0:T(8,128)(2,1)S(1)} collective-permute-done((bf16[1,1056,128]{2,1,0:T(8,128)(2,1)S(1)}, bf16[1,1056,128]{2,1,0:T(8,128)(2,1)S(1)}, u32[]{:S(2)}, u32[]{:S(2)}) %collective-permute-start.90) | collective-permute-done | bytes 270368 | tf_op jit(solution)/shard_map/ppermute | solution.py:29
  594.1 20.3 %collective-permute-done.96 = bf16[1,1056,128]{2,1,0:T(8,128)(2,1)S(1)} collective-permute-done((bf16[1,1056,128]{2,1,0:T(8,128)(2,1)S(1)}, bf16[1,1056,128]{2,1,0:T(8,128)(2,1)S(1)}, u32[]{:S(2)}, u32[]{:S(2)}) %collective-permute-start.96) | collective-permute-done | bytes 270368 | tf_op jit(solution)/shard_map/ppermute | solution.py:29
  619.2 6.5 collective-permute-done.97
  627.5 2.4 collective-permute-start.87
  630.6 11.1 %collective-permute-done.92 = bf16[2,1056,128]{2,1,0:T(8,128)(2,1)S(1)} collective-permute-done((bf16[2,1056,128]{2,1,0:T(8,128)(2,1)S(1)}, bf16[2,1056,128]{2,1,0:T(8,128)(2,1)S(1)}, u32[]{:S(2)}, u32[]{:S(2)}) %collective-permute-start.92) | collective-permute-done | bytes 540704 | tf_op jit(solution)/shard_map/ppermute | solution.py:29
  644.1 10.1 %collective-permute-done.74 = f32[4,1024]{1,0:T(4,128)S(1)} collective-permute-done((f32[4,1024]{1,0:T(4,128)S(1)}, f32[4,1024]{1,0:T(4,128)S(1)}, u32[]{:S(2)}, u32[]{:S(2)}) %collective-permute-start.74) | collective-permute-done | bytes 16416 | tf_op jit(solution)/shard_map/ppermute | solution.py:29
  654.2 4.1 collective-permute-start.75
  660.0 5.4 collective-permute-done.98
  670.0 9.9 %place_feed_grads.1 = (f32[2,704,1024]{2,1,0:T(8,128)}, f32[2,704,1024]{2,1,0:T(8,128)}, f32[2,704,1024]{2,1,0:T(8,128)}) custom-call(s32[2]{0:T(128)S(1)} %pad_add_fusion.2.refs_0_.places, bf16[8,1056,128]{2,1,0:T(8,128)(2,1)S(1)} %pad_maximum_fusion.first, bf16[8,1056,128]{2,1,0:T(8,128)(2,1)S(1)} %pad_maximum_fusion.1.second, ...), custom_call_target="tpu_custom_call" | custom-call | tf_op jit(solution)/shard_map/place_feed_grads/pallas_call | solution.py:521
  681.2 4.4 collective-permute-done.88
  (575 shorter events, 178.8 us)
Async XLA Ops:
  7.2 384.3 %reduce-scatter.2.cloned.1.call-start = ((), (), s32[]{:S(2)}) async-start(), calls=%async_computation.1 | async-start | bytes 4866048 | tf_op jit(solution)/shard_map/reduce_scatter | solution.py:952
  20.2 24.9 %collective-permute-start.6 = (bf16[256,1024]{1,0:T(8,128)(2,1)S(1)}, bf16[256,1024]{1,0:T(8,128)(2,1)}, u32[]{:S(2)}, u32[]{:S(2)}) collective-permute-start(bf16[256,1024]{1,0:T(8,128)(2,1)S(1)} %collective-permute-done.2), channel_id=1, source_target_pairs={{0,2},{2,0},{1,3},{3,1},{4,6},{6,4},{5,7},{7,5},{8,10},{10,8},{9,1... | collective-permute-start | bytes 1572872 | tf_op jit(solution)/shard_map/ppermute | solution.py:29
  24.0 23.2 %collective-permute-start.5 = (bf16[256,1024]{1,0:T(8,128)(2,1)}, bf16[256,1024]{1,0:T(8,128)(2,1)}, u32[]{:S(2)}, u32[]{:S(2)}) collective-permute-start(bf16[256,1024]{1,0:T(8,128)(2,1)} %fusion.2.refs_1_.refs_0_), channel_id=1, source_target_pairs={{0,1},{1,0},{2,3},{3,2},{4,5},{5,4},{6,7},{7,6},{8,9},{9,8},{10,11... | collective-permute-start | bytes 1572872 | tf_op jit(solution)/shard_map/ppermute | solution.py:29
  40.7 14.2 %collective-permute-start.4 = (bf16[256,1024]{1,0:T(8,128)(2,1)}, bf16[256,1024]{1,0:T(8,128)(2,1)}, u32[]{:S(2)}, u32[]{:S(2)}) collective-permute-start(bf16[256,1024]{1,0:T(8,128)(2,1)} %fusion.2.refs_1_.refs_0_), channel_id=1, source_target_pairs={{0,8},{8,0},{1,9},{9,1},{2,10},{10,2},{3,11},{11,3},{4,12},{12,4},... | collective-permute-start | bytes 1572872 | tf_op jit(solution)/shard_map/ppermute | solution.py:29
  41.4 13.9 %collective-permute-start.3 = (bf16[256,1024]{1,0:T(8,128)(2,1)}, bf16[256,1024]{1,0:T(8,128)(2,1)}, u32[]{:S(2)}, u32[]{:S(2)}) collective-permute-start(bf16[256,1024]{1,0:T(8,128)(2,1)} %fusion.2.refs_1_.refs_0_), channel_id=1, source_target_pairs={{0,4},{4,0},{1,5},{5,1},{2,6},{6,2},{3,7},{7,3},{8,12},{12,8},{9,1... | collective-permute-start | bytes 1572872 | tf_op jit(solution)/shard_map/ppermute | solution.py:29
  44.1 12.2 %collective-permute-start = (s32[8,128]{1,0:T(8,128)S(1)}, s32[8,128]{1,0:T(8,128)S(1)}, u32[]{:S(2)}, u32[]{:S(2)}) collective-permute-start(s32[8,128]{1,0:T(8,128)S(1)} %broadcast_in_dim.4), channel_id=1, source_target_pairs={{0,0},{1,16},{16,1},{17,17},{2,2},{3,18},{18,3},{19,19},{4,4},{5,2... | collective-permute-start | bytes 12296 | tf_op jit(solution)/shard_map/ppermute | solution.py:833
  56.2 12.8 %collective-permute-start.10 = (bf16[256,1024]{1,0:T(8,128)(2,1)}, bf16[256,1024]{1,0:T(8,128)(2,1)}, u32[]{:S(2)}, u32[]{:S(2)}) collective-permute-start(bf16[256,1024]{1,0:T(8,128)(2,1)} %collective-permute-done.3.refs_2_.refs_1_), channel_id=1, source_target_pairs={{0,1},{1,0},{2,3},{3,2},{4,5},{5,4},{6,7},{7,6},{8,9},{9,8},{10,11... | collective-permute-start | bytes 1572872 | tf_op jit(solution)/shard_map/ppermute | solution.py:29
  75.6 15.9 %collective-permute-start.16 = (bf16[2,704,1024]{2,1,0:T(8,128)(2,1)S(1)}, bf16[2,704,1024]{2,1,0:T(8,128)(2,1)S(1)}, u32[]{:S(2)}, u32[]{:S(2)}) collective-permute-start(bf16[2,704,1024]{2,1,0:T(8,128)(2,1)S(1)} %bitcast.187), channel_id=1, source_target_pairs={{0,1},{1,0},{2,3},{3,2},{4,5},{5,4},{6,7},{7,6},{8,9},{9,8},{10,11... | collective-permute-start | bytes 8650760 | tf_op jit(solution)/shard_map/ppermute | solution.py:29
  76.1 15.4 %collective-permute-start.17 = (bf16[2,704,1024]{2,1,0:T(8,128)(2,1)S(1)}, bf16[2,704,1024]{2,1,0:T(8,128)(2,1)S(1)}, u32[]{:S(2)}, u32[]{:S(2)}) collective-permute-start(bf16[2,704,1024]{2,1,0:T(8,128)(2,1)S(1)} %bitcast.191), channel_id=1, source_target_pairs={{0,1},{1,0},{2,3},{3,2},{4,5},{5,4},{6,7},{7,6},{8,9},{9,8},{10,11... | collective-permute-start | bytes 8650760 | tf_op jit(solution)/shard_map/ppermute | solution.py:29
  76.2 14.3 %collective-permute-start.15 = (bf16[128,1024]{1,0:T(8,128)(2,1)S(1)}, bf16[128,1024]{1,0:T(8,128)(2,1)S(1)}, u32[]{:S(2)}, u32[]{:S(2)}) collective-permute-start(bf16[128,1024]{1,0:T(8,128)(2,1)S(1)} %slice.406), channel_id=1, source_target_pairs={{0,12},{4,8},{8,4},{12,0},{1,13},{5,9},{9,5},{13,1},{2,14},{6,10},... | collective-permute-start | bytes 786440 | tf_op jit(solution)/shard_map/ppermute | solution.py:29
  78.0 13.5 %collective-permute-start.14 = (bf16[128,1024]{1,0:T(8,128)(2,1)S(1)}, bf16[128,1024]{1,0:T(8,128)(2,1)S(1)}, u32[]{:S(2)}, u32[]{:S(2)}) collective-permute-start(bf16[128,1024]{1,0:T(8,128)(2,1)S(1)} %slice.406), channel_id=1, source_target_pairs={{0,8},{8,0},{1,9},{9,1},{2,10},{10,2},{3,11},{11,3},{4,12},{12,4},... | collective-permute-start | bytes 786440 | tf_op jit(solution)/shard_map/ppermute | solution.py:29
  79.3 12.2 %collective-permute-start.13 = (bf16[128,1024]{1,0:T(8,128)(2,1)S(1)}, bf16[128,1024]{1,0:T(8,128)(2,1)S(1)}, u32[]{:S(2)}, u32[]{:S(2)}) collective-permute-start(bf16[128,1024]{1,0:T(8,128)(2,1)S(1)} %slice.406), channel_id=1, source_target_pairs={{0,4},{4,0},{1,5},{5,1},{2,6},{6,2},{3,7},{7,3},{8,12},{12,8},{9,1... | collective-permute-start | bytes 786440 | tf_op jit(solution)/shard_map/ppermute | solution.py:29
  104.0 22.5 %collective-permute-start.25 = (bf16[2,704,1024]{2,1,0:T(8,128)(2,1)S(1)}, bf16[2,704,1024]{2,1,0:T(8,128)(2,1)S(1)}, u32[]{:S(2)}, u32[]{:S(2)}) collective-permute-start(bf16[2,704,1024]{2,1,0:T(8,128)(2,1)S(1)} %copy-done.4), channel_id=1, source_target_pairs={{0,1},{1,0},{2,3},{3,2},{4,5},{5,4},{6,7},{7,6},{8,9},{9,8},{10,11... | collective-permute-start | bytes 8650760 | tf_op jit(solution)/shard_map/ppermute | solution.py:29
  112.5 14.0 %collective-permute-start.24 = (bf16[256,1024]{1,0:T(8,128)(2,1)S(1)}, bf16[256,1024]{1,0:T(8,128)(2,1)S(1)}, u32[]{:S(2)}, u32[]{:S(2)}) collective-permute-start(bf16[256,1024]{1,0:T(8,128)(2,1)S(1)} %get-tuple-element.119.refs_0_.refs_3_.refs_4_), channel_id=1, source_target_pairs={{0,2},{2,0},{1,3},{3,1},{4,6},{6,4},{5,7},{7,5},{8,10},{10,8},{9,1... | collective-permute-start | bytes 1572872 | tf_op jit(solution)/shard_map/ppermute | solution.py:29
  136.7 13.2 %collective-permute-start.26 = (bf16[256,1024]{1,0:T(8,128)(2,1)S(1)}, bf16[256,1024]{1,0:T(8,128)(2,1)S(1)}, u32[]{:S(2)}, u32[]{:S(2)}) collective-permute-start(bf16[256,1024]{1,0:T(8,128)(2,1)S(1)} %bitcast.201), channel_id=1, source_target_pairs={{0,2},{2,0},{1,3},{3,1},{4,6},{6,4},{5,7},{7,5},{8,10},{10,8},{9,1... | collective-permute-start | bytes 1572872 | tf_op jit(solution)/shard_map/ppermute | solution.py:29
  137.3 12.8 %collective-permute-start.27 = (bf16[256,1024]{1,0:T(8,128)(2,1)S(1)}, bf16[256,1024]{1,0:T(8,128)(2,1)S(1)}, u32[]{:S(2)}, u32[]{:S(2)}) collective-permute-start(bf16[256,1024]{1,0:T(8,128)(2,1)S(1)} %copy-done.135), channel_id=1, source_target_pairs={{0,0},{1,16},{16,1},{17,17},{2,2},{3,18},{18,3},{19,19},{4,4},{5,2... | collective-permute-start | bytes 1572872 | tf_op jit(solution)/shard_map/ppermute | solution.py:833
  156.5 13.9 %collective-permute-start.29 = (bf16[256,1024]{1,0:T(8,128)(2,1)S(1)}, bf16[256,1024]{1,0:T(8,128)(2,1)S(1)}, u32[]{:S(2)}, u32[]{:S(2)}) collective-permute-start(bf16[256,1024]{1,0:T(8,128)(2,1)S(1)} %multiply_convert_fusion.refs_1_.refs_0_), channel_id=1, source_target_pairs={{0,8},{8,0},{1,9},{9,1},{2,10},{10,2},{3,11},{11,3},{4,12},{12,4},... | collective-permute-start | bytes 1572872 | tf_op jit(solution)/shard_map/ppermute | solution.py:29
  157.2 13.6 %collective-permute-start.28 = (bf16[256,1024]{1,0:T(8,128)(2,1)S(1)}, bf16[256,1024]{1,0:T(8,128)(2,1)S(1)}, u32[]{:S(2)}, u32[]{:S(2)}) collective-permute-start(bf16[256,1024]{1,0:T(8,128)(2,1)S(1)} %multiply_convert_fusion.refs_1_.refs_0_), channel_id=1, source_target_pairs={{0,4},{4,0},{1,5},{5,1},{2,6},{6,2},{3,7},{7,3},{8,12},{12,8},{9,1... | collective-permute-start | bytes 1572872 | tf_op jit(solution)/shard_map/ppermute | solution.py:29
  184.3 13.3 %collective-permute-start.39 = (bf16[128,1024]{1,0:T(8,128)(2,1)S(1)}, bf16[128,1024]{1,0:T(8,128)(2,1)S(1)}, u32[]{:S(2)}, u32[]{:S(2)}) collective-permute-start(bf16[128,1024]{1,0:T(8,128)(2,1)S(1)} %slice.411), channel_id=1, source_target_pairs={{0,12},{4,8},{8,4},{12,0},{1,13},{5,9},{9,5},{13,1},{2,14},{6,10},... | collective-permute-start | bytes 786440 | tf_op jit(solution)/shard_map/ppermute | solution.py:29
  186.0 13.3 %collective-permute-start.38 = (bf16[128,1024]{1,0:T(8,128)(2,1)S(1)}, bf16[128,1024]{1,0:T(8,128)(2,1)S(1)}, u32[]{:S(2)}, u32[]{:S(2)}) collective-permute-start(bf16[128,1024]{1,0:T(8,128)(2,1)S(1)} %slice.411), channel_id=1, source_target_pairs={{0,8},{8,0},{1,9},{9,1},{2,10},{10,2},{3,11},{11,3},{4,12},{12,4},... | collective-permute-start | bytes 786440 | tf_op jit(solution)/shard_map/ppermute | solution.py:29
  205.7 14.3 %collective-permute-start.45 = (bf16[512,1024]{1,0:T(8,128)(2,1)S(1)}, bf16[512,1024]{1,0:T(8,128)(2,1)S(1)}, u32[]{:S(2)}, u32[]{:S(2)}) collective-permute-start(bf16[512,1024]{1,0:T(8,128)(2,1)S(1)} %pad_maximum_fusion.5), channel_id=1, source_target_pairs={{0,1},{1,0},{2,3},{3,2},{4,5},{5,4},{6,7},{7,6},{8,9},{9,8},{10,11... | collective-permute-start | bytes 3145736 | tf_op jit(solution)/shard_map/ppermute | solution.py:29
  205.7 14.3 %collective-permute-start.44 = (bf16[256,1024]{1,0:T(8,128)(2,1)S(1)}, bf16[256,1024]{1,0:T(8,128)(2,1)S(1)}, u32[]{:S(2)}, u32[]{:S(2)}) collective-permute-start(bf16[256,1024]{1,0:T(8,128)(2,1)S(1)} %collective-permute-done.27.refs_2_.refs_5_), channel_id=1, source_target_pairs={{0,2},{2,0},{1,3},{3,1},{4,6},{6,4},{5,7},{7,5},{8,10},{10,8},{9,1... | collective-permute-start | bytes 1572872 | tf_op jit(solution)/shard_map/ppermute | solution.py:29
  222.8 13.6 %collective-permute-start.46 = (bf16[256,1024]{1,0:T(8,128)(2,1)S(1)}, bf16[256,1024]{1,0:T(8,128)(2,1)S(1)}, u32[]{:S(2)}, u32[]{:S(2)}) collective-permute-start(bf16[256,1024]{1,0:T(8,128)(2,1)S(1)} %get-tuple-element.139.refs_0_.refs_3_), channel_id=1, source_target_pairs={{0,2},{2,0},{1,3},{3,1},{4,6},{6,4},{5,7},{7,5},{8,10},{10,8},{9,1... | collective-permute-start | bytes 1572872 | tf_op jit(solution)/shard_map/ppermute | solution.py:29
  268.5 264.6 %all-gather.2.cloned.1.call-start = ((), (), s32[]{:S(2)}) async-start(), calls=%async_computation.2 | async-start | bytes 4866048 | tf_op jit(solution)/shard_map/all_gather | solution.py:966
  268.6 14.2 %collective-permute-start.47 = (bf16[256,1024]{1,0:T(8,128)(2,1)}, bf16[256,1024]{1,0:T(8,128)(2,1)S(1)}, u32[]{:S(2)}, u32[]{:S(2)}) collective-permute-start(bf16[256,1024]{1,0:T(8,128)(2,1)} %bitcast.199), channel_id=1, source_target_pairs={{0,2},{2,0},{1,3},{3,1},{4,6},{6,4},{5,7},{7,5},{8,10},{10,8},{9,1... | collective-permute-start | bytes 1572872 | tf_op jit(solution)/shard_map/ppermute | solution.py:29
  286.9 14.4 %collective-permute-start.50 = (bf16[2,256,128]{2,1,0:T(8,128)(2,1)S(1)}, bf16[2,256,128]{2,1,0:T(8,128)(2,1)S(1)}, u32[]{:S(2)}, u32[]{:S(2)}) collective-permute-start(bf16[2,256,128]{2,1,0:T(8,128)(2,1)S(1)} %get-tuple-element.232), channel_id=1, source_target_pairs={{0,12},{4,8},{8,4},{12,0},{1,13},{5,9},{9,5},{13,1},{2,14},{6,10},... | collective-permute-start | bytes 393224 | tf_op jit(solution)/shard_map/ppermute | solution.py:29
  288.6 19.9 %collective-permute-start.49 = (bf16[2,256,128]{2,1,0:T(8,128)(2,1)S(1)}, bf16[2,256,128]{2,1,0:T(8,128)(2,1)S(1)}, u32[]{:S(2)}, u32[]{:S(2)}) collective-permute-start(bf16[2,256,128]{2,1,0:T(8,128)(2,1)S(1)} %get-tuple-element.234), channel_id=1, source_target_pairs={{0,8},{8,0},{1,9},{9,1},{2,10},{10,2},{3,11},{11,3},{4,12},{12,4},... | collective-permute-start | bytes 393224 | tf_op jit(solution)/shard_map/ppermute | solution.py:29
  289.9 18.7 %collective-permute-start.48 = (bf16[2,256,128]{2,1,0:T(8,128)(2,1)S(1)}, bf16[2,256,128]{2,1,0:T(8,128)(2,1)S(1)}, u32[]{:S(2)}, u32[]{:S(2)}) collective-permute-start(bf16[2,256,128]{2,1,0:T(8,128)(2,1)S(1)} %get-tuple-element.235), channel_id=1, source_target_pairs={{0,4},{4,0},{1,5},{5,1},{2,6},{6,2},{3,7},{7,3},{8,12},{12,8},{9,1... | collective-permute-start | bytes 393224 | tf_op jit(solution)/shard_map/ppermute | solution.py:29
  327.8 28.8 %collective-permute-start.55 = (bf16[256,1024]{1,0:T(8,128)(2,1)S(1)}, bf16[256,1024]{1,0:T(8,128)(2,1)S(1)}, u32[]{:S(2)}, u32[]{:S(2)}) collective-permute-start(bf16[256,1024]{1,0:T(8,128)(2,1)S(1)} %get-tuple-element.215), channel_id=1, source_target_pairs={{0,4},{4,0},{1,5},{5,1},{2,6},{6,2},{3,7},{7,3},{8,12},{12,8},{9,1... | collective-permute-start | bytes 1572872 | tf_op jit(solution)/shard_map/ppermute | solution.py:29
  328.5 28.1 %collective-permute-start.57 = (bf16[256,1024]{1,0:T(8,128)(2,1)S(1)}, bf16[256,1024]{1,0:T(8,128)(2,1)S(1)}, u32[]{:S(2)}, u32[]{:S(2)}) collective-permute-start(bf16[256,1024]{1,0:T(8,128)(2,1)S(1)} %get-tuple-element.216), channel_id=1, source_target_pairs={{0,12},{4,8},{8,4},{12,0},{1,13},{5,9},{9,5},{13,1},{2,14},{6,10},... | collective-permute-start | bytes 1572872 | tf_op jit(solution)/shard_map/ppermute | solution.py:29
  328.5 28.1 %collective-permute-start.56 = (bf16[256,1024]{1,0:T(8,128)(2,1)S(1)}, bf16[256,1024]{1,0:T(8,128)(2,1)S(1)}, u32[]{:S(2)}, u32[]{:S(2)}) collective-permute-start(bf16[256,1024]{1,0:T(8,128)(2,1)S(1)} %get-tuple-element.217), channel_id=1, source_target_pairs={{0,8},{8,0},{1,9},{9,1},{2,10},{10,2},{3,11},{11,3},{4,12},{12,4},... | collective-permute-start | bytes 1572872 | tf_op jit(solution)/shard_map/ppermute | solution.py:29
  358.5 13.6 %collective-permute-start.58 = (bf16[256,1024]{1,0:T(8,128)(2,1)S(1)}, bf16[256,1024]{1,0:T(8,128)(2,1)S(1)}, u32[]{:S(2)}, u32[]{:S(2)}) collective-permute-start(bf16[256,1024]{1,0:T(8,128)(2,1)S(1)} %get-tuple-element.205.refs_2_.refs_5_.refs_6_), channel_id=1, source_target_pairs={{0,2},{2,0},{1,3},{3,1},{4,6},{6,4},{5,7},{7,5},{8,10},{10,8},{9,1... | collective-permute-start | bytes 1572872 | tf_op jit(solution)/shard_map/ppermute | solution.py:29
  391.4 39.6 %collective-permute-start.60 = (bf16[2112,1024]{1,0:T(8,128)(2,1)}, bf16[2112,1024]{1,0:T(8,128)(2,1)}, u32[]{:S(2)}, u32[]{:S(2)}) collective-permute-start(bf16[2112,1024]{1,0:T(8,128)(2,1)} %feed_weight_grads.6), channel_id=1, source_target_pairs={{0,1},{1,0},{2,3},{3,2},{4,5},{5,4},{6,7},{7,6},{8,9},{9,8},{10,11... | collective-permute-start | bytes 12976136 | tf_op jit(solution)/shard_map/ppermute | solution.py:29
  391.5 14.6 %collective-permute-start.59 = (bf16[256,1024]{1,0:T(8,128)(2,1)}, bf16[256,1024]{1,0:T(8,128)(2,1)S(1)}, u32[]{:S(2)}, u32[]{:S(2)}) collective-permute-start(bf16[256,1024]{1,0:T(8,128)(2,1)} %bitcast.200), channel_id=1, source_target_pairs={{0,2},{2,0},{1,3},{3,1},{4,6},{6,4},{5,7},{7,5},{8,10},{10,8},{9,1... | collective-permute-start | bytes 1572872 | tf_op jit(solution)/shard_map/ppermute | solution.py:29
  413.0 13.8 %collective-permute-start.63 = (bf16[2,256,128]{2,1,0:T(8,128)(2,1)S(1)}, bf16[2,256,128]{2,1,0:T(8,128)(2,1)S(1)}, u32[]{:S(2)}, u32[]{:S(2)}) collective-permute-start(bf16[2,256,128]{2,1,0:T(8,128)(2,1)S(1)} %get-tuple-element.228), channel_id=1, source_target_pairs={{0,12},{4,8},{8,4},{12,0},{1,13},{5,9},{9,5},{13,1},{2,14},{6,10},... | collective-permute-start | bytes 393224 | tf_op jit(solution)/shard_map/ppermute | solution.py:29
  414.1 14.9 %collective-permute-start.62 = (bf16[2,256,128]{2,1,0:T(8,128)(2,1)S(1)}, bf16[2,256,128]{2,1,0:T(8,128)(2,1)S(1)}, u32[]{:S(2)}, u32[]{:S(2)}) collective-permute-start(bf16[2,256,128]{2,1,0:T(8,128)(2,1)S(1)} %get-tuple-element.229), channel_id=1, source_target_pairs={{0,8},{8,0},{1,9},{9,1},{2,10},{10,2},{3,11},{11,3},{4,12},{12,4},... | collective-permute-start | bytes 393224 | tf_op jit(solution)/shard_map/ppermute | solution.py:29
  416.0 13.0 %collective-permute-start.61 = (bf16[2,256,128]{2,1,0:T(8,128)(2,1)S(1)}, bf16[2,256,128]{2,1,0:T(8,128)(2,1)S(1)}, u32[]{:S(2)}, u32[]{:S(2)}) collective-permute-start(bf16[2,256,128]{2,1,0:T(8,128)(2,1)S(1)} %get-tuple-element.230), channel_id=1, source_target_pairs={{0,4},{4,0},{1,5},{5,1},{2,6},{6,2},{3,7},{7,3},{8,12},{12,8},{9,1... | collective-permute-start | bytes 393224 | tf_op jit(solution)/shard_map/ppermute | solution.py:29
  458.1 38.3 %collective-permute-start.67 = (bf16[4,1056,128]{2,1,0:T(8,128)(2,1)S(1)}, bf16[4,1056,128]{2,1,0:T(8,128)(2,1)S(1)}, u32[]{:S(2)}, u32[]{:S(2)}) collective-permute-start(bf16[4,1056,128]{2,1,0:T(8,128)(2,1)S(1)} %slice.369), channel_id=1, source_target_pairs={{0,8},{8,0},{1,9},{9,1},{2,10},{10,2},{3,11},{11,3},{4,12},{12,4},... | collective-permute-start | bytes 3244040 | tf_op jit(solution)/shard_map/ppermute | solution.py:29
  458.2 38.3 %collective-permute-start.66 = (bf16[4,1056,128]{2,1,0:T(8,128)(2,1)S(1)}, bf16[4,1056,128]{2,1,0:T(8,128)(2,1)S(1)}, u32[]{:S(2)}, u32[]{:S(2)}) collective-permute-start(bf16[4,1056,128]{2,1,0:T(8,128)(2,1)S(1)} %slice.368), channel_id=1, source_target_pairs={{0,4},{4,0},{1,5},{5,1},{2,6},{6,2},{3,7},{7,3},{8,12},{12,8},{9,1... | collective-permute-start | bytes 3244040 | tf_op jit(solution)/shard_map/ppermute | solution.py:29
  463.2 36.5 %collective-permute-start.82 = (bf16[128,1024]{1,0:T(8,128)(2,1)S(1)}, bf16[128,1024]{1,0:T(8,128)(2,1)S(1)}, u32[]{:S(2)}, u32[]{:S(2)}) collective-permute-start(bf16[128,1024]{1,0:T(8,128)(2,1)S(1)} %get-tuple-element.218), channel_id=1, source_target_pairs={{0,4},{4,0},{1,5},{5,1},{2,6},{6,2},{3,7},{7,3},{8,12},{12,8},{9,1... | collective-permute-start | bytes 786440 | tf_op jit(solution)/shard_map/ppermute | solution.py:29
  464.8 44.0 %collective-permute-start.84 = (bf16[128,1024]{1,0:T(8,128)(2,1)}, bf16[128,1024]{1,0:T(8,128)(2,1)}, u32[]{:S(2)}, u32[]{:S(2)}) collective-permute-start(bf16[128,1024]{1,0:T(8,128)(2,1)} %get-tuple-element.219), channel_id=1, source_target_pairs={{0,12},{4,8},{8,4},{12,0},{1,13},{5,9},{9,5},{13,1},{2,14},{6,10},... | collective-permute-start | bytes 786440 | tf_op jit(solution)/shard_map/ppermute | solution.py:29
  466.0 42.8 %collective-permute-start.83 = (bf16[128,1024]{1,0:T(8,128)(2,1)}, bf16[128,1024]{1,0:T(8,128)(2,1)}, u32[]{:S(2)}, u32[]{:S(2)}) collective-permute-start(bf16[128,1024]{1,0:T(8,128)(2,1)} %get-tuple-element.220), channel_id=1, source_target_pairs={{0,8},{8,0},{1,9},{9,1},{2,10},{10,2},{3,11},{11,3},{4,12},{12,4},... | collective-permute-start | bytes 786440 | tf_op jit(solution)/shard_map/ppermute | solution.py:29
  498.3 26.8 %collective-permute-start.68 = (bf16[256,1024]{1,0:T(8,128)(2,1)}, bf16[256,1024]{1,0:T(8,128)(2,1)}, u32[]{:S(2)}, u32[]{:S(2)}) collective-permute-start(bf16[256,1024]{1,0:T(8,128)(2,1)} %get-tuple-element.212), channel_id=1, source_target_pairs={{0,4},{4,0},{1,5},{5,1},{2,6},{6,2},{3,7},{7,3},{8,12},{12,8},{9,1... | collective-permute-start | bytes 1572872 | tf_op jit(solution)/shard_map/ppermute | solution.py:29
  499.5 25.5 %collective-permute-start.70 = (bf16[256,1024]{1,0:T(8,128)(2,1)}, bf16[256,1024]{1,0:T(8,128)(2,1)}, u32[]{:S(2)}, u32[]{:S(2)}) collective-permute-start(bf16[256,1024]{1,0:T(8,128)(2,1)} %get-tuple-element.213), channel_id=1, source_target_pairs={{0,12},{4,8},{8,4},{12,0},{1,13},{5,9},{9,5},{13,1},{2,14},{6,10},... | collective-permute-start | bytes 1572872 | tf_op jit(solution)/shard_map/ppermute | solution.py:29
  499.7 30.0 %collective-permute-start.69 = (bf16[256,1024]{1,0:T(8,128)(2,1)}, bf16[256,1024]{1,0:T(8,128)(2,1)}, u32[]{:S(2)}, u32[]{:S(2)}) collective-permute-start(bf16[256,1024]{1,0:T(8,128)(2,1)} %get-tuple-element.214), channel_id=1, source_target_pairs={{0,8},{8,0},{1,9},{9,1},{2,10},{10,2},{3,11},{11,3},{4,12},{12,4},... | collective-permute-start | bytes 1572872 | tf_op jit(solution)/shard_map/ppermute | solution.py:29
  536.0 15.5 %collective-permute-start.94 = (bf16[2,1056,128]{2,1,0:T(8,128)(2,1)S(1)}, bf16[2,1056,128]{2,1,0:T(8,128)(2,1)S(1)}, u32[]{:S(2)}, u32[]{:S(2)}) collective-permute-start(bf16[2,1056,128]{2,1,0:T(8,128)(2,1)S(1)} %slice.457), channel_id=1, source_target_pairs={{0,4},{4,0},{1,5},{5,1},{2,6},{6,2},{3,7},{7,3},{8,12},{12,8},{9,1... | collective-permute-start | bytes 1622024 | tf_op jit(solution)/shard_map/ppermute | solution.py:29
  538.0 32.7 %collective-permute-start.89 = (bf16[2,1056,128]{2,1,0:T(8,128)(2,1)S(1)}, bf16[2,1056,128]{2,1,0:T(8,128)(2,1)S(1)}, u32[]{:S(2)}, u32[]{:S(2)}) collective-permute-start(bf16[2,1056,128]{2,1,0:T(8,128)(2,1)S(1)} %slice.453), channel_id=1, source_target_pairs={{0,8},{8,0},{1,9},{9,1},{2,10},{10,2},{3,11},{11,3},{4,12},{12,4},... | collective-permute-start | bytes 1622024 | tf_op jit(solution)/shard_map/ppermute | solution.py:29
  539.1 19.5 %collective-permute-start.78 = (bf16[128,1024]{1,0:T(8,128)(2,1)S(1)}, bf16[128,1024]{1,0:T(8,128)(2,1)S(1)}, u32[]{:S(2)}, u32[]{:S(2)}) collective-permute-start(bf16[128,1024]{1,0:T(8,128)(2,1)S(1)} %get-tuple-element.221), channel_id=1, source_target_pairs={{0,4},{4,0},{1,5},{5,1},{2,6},{6,2},{3,7},{7,3},{8,12},{12,8},{9,1... | collective-permute-start | bytes 786440 | tf_op jit(solution)/shard_map/ppermute | solution.py:29
  539.7 24.9 %collective-permute-start.80 = (bf16[128,1024]{1,0:T(8,128)(2,1)S(1)}, bf16[128,1024]{1,0:T(8,128)(2,1)S(1)}, u32[]{:S(2)}, u32[]{:S(2)}) collective-permute-start(bf16[128,1024]{1,0:T(8,128)(2,1)S(1)} %get-tuple-element.222), channel_id=1, source_target_pairs={{0,12},{4,8},{8,4},{12,0},{1,13},{5,9},{9,5},{13,1},{2,14},{6,10},... | collective-permute-start | bytes 786440 | tf_op jit(solution)/shard_map/ppermute | solution.py:29
  542.4 26.5 %collective-permute-start.79 = (bf16[128,1024]{1,0:T(8,128)(2,1)S(1)}, bf16[128,1024]{1,0:T(8,128)(2,1)S(1)}, u32[]{:S(2)}, u32[]{:S(2)}) collective-permute-start(bf16[128,1024]{1,0:T(8,128)(2,1)S(1)} %get-tuple-element.223), channel_id=1, source_target_pairs={{0,8},{8,0},{1,9},{9,1},{2,10},{10,2},{3,11},{11,3},{4,12},{12,4},... | collective-permute-start | bytes 786440 | tf_op jit(solution)/shard_map/ppermute | solution.py:29
  551.7 20.6 %collective-permute-start.95 = (bf16[1,1056,128]{2,1,0:T(8,128)(2,1)S(1)}, bf16[1,1056,128]{2,1,0:T(8,128)(2,1)S(1)}, u32[]{:S(2)}, u32[]{:S(2)}) collective-permute-start(bf16[1,1056,128]{2,1,0:T(8,128)(2,1)S(1)} %slice.459), channel_id=1, source_target_pairs={{0,16},{16,0},{1,17},{17,1},{2,18},{18,2},{3,19},{19,3},{4,20},{20... | collective-permute-start | bytes 811016 | tf_op jit(solution)/shard_map/ppermute | solution.py:29
  569.1 23.8 %collective-permute-start.85 = (bf16[256,2,1024]{2,0,1:T(8,128)(2,1)S(1)}, bf16[256,2,1024]{2,0,1:T(8,128)(2,1)S(1)}, u32[]{:S(2)}, u32[]{:S(2)}) collective-permute-start(bf16[256,2,1024]{2,0,1:T(8,128)(2,1)S(1)} %fusion.9), channel_id=1, source_target_pairs={{0,2},{2,0},{1,3},{3,1},{4,6},{6,4},{5,7},{7,5},{8,10},{10,8},{9,1... | collective-permute-start | bytes 3145736 | tf_op jit(solution)/shard_map/ppermute | solution.py:29
  570.9 20.7 %collective-permute-start.90 = (bf16[1,1056,128]{2,1,0:T(8,128)(2,1)S(1)}, bf16[1,1056,128]{2,1,0:T(8,128)(2,1)S(1)}, u32[]{:S(2)}, u32[]{:S(2)}) collective-permute-start(bf16[1,1056,128]{2,1,0:T(8,128)(2,1)S(1)} %slice.455), channel_id=1, source_target_pairs={{0,16},{16,0},{1,17},{17,1},{2,18},{18,2},{3,19},{19,3},{4,20},{20... | collective-permute-start | bytes 811016 | tf_op jit(solution)/shard_map/ppermute | solution.py:29
  572.4 42.0 %collective-permute-start.96 = (bf16[1,1056,128]{2,1,0:T(8,128)(2,1)S(1)}, bf16[1,1056,128]{2,1,0:T(8,128)(2,1)S(1)}, u32[]{:S(2)}, u32[]{:S(2)}) collective-permute-start(bf16[1,1056,128]{2,1,0:T(8,128)(2,1)S(1)} %add_convert_fusion.7), channel_id=1, source_target_pairs={{0,16},{16,0},{1,17},{17,1},{2,18},{18,2},{3,19},{19,3},{4,20},{20... | collective-permute-start | bytes 811016 | tf_op jit(solution)/shard_map/ppermute | solution.py:29
  591.6 27.1 %collective-permute-start.91 = (bf16[1,1056,128]{2,1,0:T(8,128)(2,1)S(1)}, bf16[1,1056,128]{2,1,0:T(8,128)(2,1)S(1)}, u32[]{:S(2)}, u32[]{:S(2)}) collective-permute-start(bf16[1,1056,128]{2,1,0:T(8,128)(2,1)S(1)} %add_convert_fusion.8), channel_id=1, source_target_pairs={{0,16},{16,0},{1,17},{17,1},{2,18},{18,2},{3,19},{19,3},{4,20},{20... | collective-permute-start | bytes 811016 | tf_op jit(solution)/shard_map/ppermute | solution.py:29
  593.4 34.2 %collective-permute-start.86 = (bf16[256,2,1024]{2,0,1:T(8,128)(2,1)S(1)}, bf16[256,2,1024]{2,0,1:T(8,128)(2,1)S(1)}, u32[]{:S(2)}, u32[]{:S(2)}) collective-permute-start(bf16[256,2,1024]{2,0,1:T(8,128)(2,1)S(1)} %add_convert_fusion.3), channel_id=1, source_target_pairs={{0,0},{1,16},{16,1},{17,17},{2,2},{3,18},{18,3},{19,19},{4,4},{5,2... | collective-permute-start | bytes 3145736 | tf_op jit(solution)/shard_map/ppermute | solution.py:833
  616.2 27.7 %collective-permute-start.52 = (bf16[256,1024]{1,0:T(8,128)(2,1)S(1)}, bf16[256,1024]{1,0:T(8,128)(2,1)S(1)}, u32[]{:S(2)}, u32[]{:S(2)}) collective-permute-start(bf16[256,1024]{1,0:T(8,128)(2,1)S(1)} %bitcast.198), channel_id=1, source_target_pairs={{0,2},{2,0},{1,3},{3,1},{4,6},{6,4},{5,7},{7,5},{8,10},{10,8},{9,1... | collective-permute-start | bytes 1572872 | tf_op jit(solution)/shard_map/ppermute | solution.py:29
  618.8 22.9 %collective-permute-start.92 = (bf16[2,1056,128]{2,1,0:T(8,128)(2,1)S(1)}, bf16[2,1056,128]{2,1,0:T(8,128)(2,1)S(1)}, u32[]{:S(2)}, u32[]{:S(2)}) collective-permute-start(bf16[2,1056,128]{2,1,0:T(8,128)(2,1)S(1)} %pad_maximum_fusion.7), channel_id=1, source_target_pairs={{0,8},{8,0},{1,9},{9,1},{2,10},{10,2},{3,11},{11,3},{4,12},{12,4},... | collective-permute-start | bytes 1622024 | tf_op jit(solution)/shard_map/ppermute | solution.py:29
  625.7 39.6 %collective-permute-start.98 = (bf16[4,1056,128]{2,1,0:T(8,128)(2,1)S(1)}, bf16[4,1056,128]{2,1,0:T(8,128)(2,1)S(1)}, u32[]{:S(2)}, u32[]{:S(2)}) collective-permute-start(bf16[4,1056,128]{2,1,0:T(8,128)(2,1)S(1)} %pad_maximum_fusion.3), channel_id=1, source_target_pairs={{0,8},{8,0},{1,9},{9,1},{2,10},{10,2},{3,11},{11,3},{4,12},{12,4},... | collective-permute-start | bytes 3244040 | tf_op jit(solution)/shard_map/ppermute | solution.py:29
  627.5 31.6 %collective-permute-start.87 = (bf16[256,2,1024]{2,0,1:T(8,128)(2,1)S(1)}, bf16[256,2,1024]{2,0,1:T(8,128)(2,1)S(1)}, u32[]{:S(2)}, u32[]{:S(2)}) collective-permute-start(bf16[256,2,1024]{2,0,1:T(8,128)(2,1)S(1)} %collective-permute-done.86), channel_id=1, source_target_pairs={{0,1},{1,0},{2,3},{3,2},{4,5},{5,4},{6,7},{7,6},{8,9},{9,8},{10,11... | collective-permute-start | bytes 3145736 | tf_op jit(solution)/shard_map/ppermute | solution.py:29
  630.0 13.0 %collective-permute-start.73 = (f32[4,1024]{1,0:T(4,128)S(1)}, f32[4,1024]{1,0:T(4,128)S(1)}, u32[]{:S(2)}, u32[]{:S(2)}) collective-permute-start(f32[4,1024]{1,0:T(4,128)S(1)} %fusion.36), channel_id=1, source_target_pairs={{0,2},{2,0},{1,3},{3,1},{4,6},{6,4},{5,7},{7,5},{8,10},{10,8},{9,1... | collective-permute-start | bytes 49160 | tf_op jit(solution)/shard_map/ppermute | solution.py:29
  641.8 25.8 %collective-permute-start.93 = (bf16[4,1056,128]{2,1,0:T(8,128)(2,1)S(1)}, bf16[4,1056,128]{2,1,0:T(8,128)(2,1)S(1)}, u32[]{:S(2)}, u32[]{:S(2)}) collective-permute-start(bf16[4,1056,128]{2,1,0:T(8,128)(2,1)S(1)} %pad_maximum_fusion.2), channel_id=1, source_target_pairs={{0,4},{4,0},{1,5},{5,1},{2,6},{6,2},{3,7},{7,3},{8,12},{12,8},{9,1... | collective-permute-start | bytes 3244040 | tf_op jit(solution)/shard_map/ppermute | solution.py:29
  658.4 21.5 %collective-permute-start.71 = (bf16[2,256,1024]{2,1,0:T(8,128)(2,1)S(1)}, bf16[2,256,1024]{2,1,0:T(8,128)(2,1)S(1)}, u32[]{:S(2)}, u32[]{:S(2)}) collective-permute-start(bf16[2,256,1024]{2,1,0:T(8,128)(2,1)S(1)} %pad_maximum_fusion.6), channel_id=1, source_target_pairs={{0,0},{1,16},{16,1},{17,17},{2,2},{3,18},{18,3},{19,19},{4,4},{5,2... | collective-permute-start | bytes 3145736 | tf_op jit(solution)/shard_map/ppermute | solution.py:833
  659.6 26.0 %collective-permute-start.88 = (bf16[256,2,1024]{2,0,1:T(8,128)(2,1)S(1)}, bf16[256,2,1024]{2,0,1:T(8,128)(2,1)S(1)}, u32[]{:S(2)}, u32[]{:S(2)}) collective-permute-start(bf16[256,2,1024]{2,0,1:T(8,128)(2,1)S(1)} %add_convert_fusion.2), channel_id=1, source_target_pairs={{0,2},{2,0},{1,3},{3,1},{4,6},{6,4},{5,7},{7,5},{8,10},{10,8},{9,1... | collective-permute-start | bytes 3145736 | tf_op jit(solution)/shard_map/ppermute | solution.py:29
  (177 other events, 2030.6 us)
Sparse Core Ops, SparseCore 0:
  268.7 112.7 reduce-scatter.1
  391.7 92.3 all-gather.1

commit v3 on v2

--- a/solution.py
+++ b/solution.py
@@ -17,7 +17,8 @@
 BF16 = jnp.bfloat16
 F32 = jnp.float32
 VMEM_BYTES = 36 * 1024 * 1024
-COST_SCALE = 50
+SCALE = 0.2
+WIDE = 2.0
 
 NT = (((1,), (1,)), ((), ()))
 TN = (((0,), (0,)), ((), ()))
@@ -60,20 +61,29 @@
     return chips, [swap(c, (core,)) for c in chips]
 
 
-def reduce_blocks(kept, received, axes):
-    for axis in axes:
-        if axis != axes[0]:
-            received = swap(sent, (axis,))
-        total = (kept.astype(F32) + received.astype(F32)).astype(BF16)
-        half = total.shape[0] // 2
-        kept, sent = total[:half], total[half:]
-    return total
-
-
-def spread_blocks(block, axes):
-    for axis in reversed(axes):
-        block = jnp.concatenate([block, swap(block, (axis,))], axis=0)
-    return block
+class BlockSum:
+    def __init__(self, parts, axes):
+        self.axes, self.done = axes, 0
+        half = parts.shape[0] // 2
+        self.kept, self.sent = parts[:half], parts[half:]
+
+    def step(self, *ties):
+        count = len(self.axes)
+        if self.done < count:
+            received = swap(after(self.sent, *ties), (self.axes[self.done],))
+            total = (self.kept.astype(F32) + received.astype(F32)).astype(BF16)
+            half = total.shape[0] // 2
+            self.kept, self.sent = (total[:half], total[half:]) if half else (total, None)
+        else:
+            block = after(self.kept, *ties)
+            received = swap(block, (self.axes[2 * count - 1 - self.done],))
+            self.kept = jnp.concatenate([block, received], axis=0)
+        self.done += 1
+        return received
+
+
+def steps(sums, *ties):
+    return [part.step(*ties) for part in sums]
 
 
 def scatter_sum(mine, others, axes, core, *ties):
@@ -103,11 +113,11 @@
     return pltpu.CompilerParams(vmem_limit_bytes=VMEM_BYTES)
 
 
-def cost(flops, bytes_accessed, transcendentals):
+def cost(flops, bytes_accessed, transcendentals, scale=SCALE):
     return pl.CostEstimate(
-        flops=flops // COST_SCALE,
-        bytes_accessed=bytes_accessed // COST_SCALE,
-        transcendentals=transcendentals // COST_SCALE,
+        flops=int(flops * scale),
+        bytes_accessed=int(bytes_accessed * scale),
+        transcendentals=int(transcendentals * scale),
     )
 
 
@@ -482,66 +492,52 @@
             flops=6 * shares * rows * units * depth,
             bytes_accessed=6 * units * depth,
             transcendentals=0,
+            scale=WIDE,
         ),
         name="feed_weight_grads",
     )(*operands)
 
 
-def place_kernel(units, places, first, second, summed, *outs):
-    layer = pl.program_id(0)
-
-    def write(rows):
-        rows = rows.astype(F32)
-        for n, out in enumerate(outs):
-            out[0] = rows[n * units : (n + 1) * units]
-
-    @pl.when(layer == 0)
-    def _():
-        write(jnp.concatenate([first[0], second[0]], axis=0))
-
-    @pl.when(layer > 0)
-    def _():
-        write(summed[0])
-
-
-def place_feed(places, first, second, summed):
-    blocks, half, size = first.shape
-    layers = summed.shape[0] + 1
-    units = 2 * half // 3
-    out = jax.ShapeDtypeStruct((layers, units, blocks * size), F32)
-
-    def part(index):
+def place_kernel(units, places, *refs):
+    parts = refs[:-3]
+    outs = refs[-3:]
+    parts = [part[0] if len(part.shape) == 3 else part[...] for part in parts if part is not None]
+    rows = jnp.concatenate(parts, axis=0).astype(F32)
+    for n, out in enumerate(outs):
+        out[0] = rows[n * units : (n + 1) * units]
+
+
+def place_feed(places, parts, blocks, layer, layers, previous):
+    depth = blocks * (parts[0].shape[-1] if parts[0].ndim == 3 else parts[0].shape[-1] // blocks)
+    units = sum(part.shape[-2] for part in parts) // 3
+    size = depth // blocks
+    out = jax.ShapeDtypeStruct((layers, units, depth), F32)
+
+    def spec(index, part):
+        if part.ndim == 2:
+            return pl.BlockSpec((part.shape[0], size), lambda block, places: (0, block))
         return pl.BlockSpec(
-            (1, half, size),
-            lambda layer, block, places: (
-                jnp.where(layer == 0, block ^ places[index], (blocks - 1) ^ places[index]), 0, 0,
-            ),
+            (1, part.shape[1], size), lambda block, places: (block ^ places[index], 0, 0)
         )
 
+    def body(places, *refs):
+        place_kernel(units, places, *refs[: len(parts)], *refs[-3:])
+
     return pl.pallas_call(
-        functools.partial(place_kernel, units),
+        body,
         out_shape=(out,) * 3,
         grid_spec=pltpu.PrefetchScalarGridSpec(
             num_scalar_prefetch=1,
-            grid=(layers, blocks),
-            in_specs=[
-                part(0),
-                part(1),
-                pl.BlockSpec(
-                    (1, 2 * half, size),
-                    lambda layer, block, places: (
-                        jnp.maximum(layer - 1, 0), 0, jnp.where(layer == 0, 0, block),
-                    ),
-                ),
-            ],
-            out_specs=[
-                pl.BlockSpec((1, units, size), lambda layer, block, places: (layer, 0, block))
-            ]
+            grid=(blocks,),
+            in_specs=[spec(n, part) for n, part in enumerate(parts)]
+            + [pl.BlockSpec(memory_space=pl.ANY)] * len(previous),
+            out_specs=[pl.BlockSpec((1, units, size), lambda block, places: (layer, 0, block))]
             * 3,
         ),
+        input_output_aliases={1 + len(parts) + n: n for n in range(len(previous))},
         compiler_params=compiler_params(),
         name="place_feed_grads",
-    )(places, first, second, summed)
+    )(places, *parts, *previous)
 
 
 def head_weights_kernel(raws, *refs):
@@ -564,6 +560,7 @@
             flops=2 * len(blocks) * rows * wide * depth,
             bytes_accessed=2 * len(blocks) * rows * (wide + depth),
             transcendentals=0,
+            scale=WIDE,
         ),
         name="head_weight_grads",
     )(raws, *blocks)
@@ -657,9 +654,9 @@
     refs = list(refs)
     ids, queries, keys, values, attended = (refs.pop(0) for _ in range(5))
     near = [refs.pop(0) for _ in range(chips)]
-    far, log_totals, cosine, sine = (refs.pop(0) for _ in range(4))
+    far, log_totals, cosine, sine, weights = (refs.pop(0) for _ in range(5))
     later_layer = refs.pop(0) if layer_first else None
-    outs, grad_rows, inner, query_total, key_total, value_total = refs
+    outs, mine, others, grad_rows, inner, query_total, key_total, value_total = refs
     heads = width // HEAD_DIM
     count = 2 * chips * rows
     units = max(count // SEQ_UNIT, 1)
@@ -741,24 +738,35 @@
                 value = value + later_layer[core, chip, :, 2 * width :].astype(F32)
             else:
                 value = value.astype(BF16).astype(F32) * 0.5
-            outs[core, chip] = jnp.concatenate([query, key, value], axis=1).astype(BF16)
+            raws = jnp.concatenate([query, key, value], axis=1).astype(BF16)
+            outs[core, chip] = raws
+            term = jnp.dot(raws, weights[: 3 * width, :], preferred_element_type=F32)
+            if core:
+                others[chip] = term.astype(BF16)
+            else:
+                mine[chip] = term
 
 
 def attend_back(
-    ids, queries, keys, values, attended, near, far, log_totals, cosine, sine, later_layer
+    ids, queries, keys, values, attended, near, far, log_totals, cosine, sine, weights, later_layer
 ):
     chips, _, rows, width = attended.shape
     count = queries.shape[0]
     heads = width // HEAD_DIM
     pairs = count * count // 2
-    operands = [ids, queries, keys, values, attended, *near, far, log_totals, cosine, sine]
+    operands = [ids, queries, keys, values, attended, *near, far, log_totals, cosine, sine, weights]
+    depth = weights.shape[1]
     if later_layer is not None:
         operands.append(later_layer)
     return pl.pallas_call(
         functools.partial(attend_back_kernel, chips, rows, width, later_layer is not None),
-        out_shape=jax.ShapeDtypeStruct((2, chips, rows, 3 * width), BF16),
+        out_shape=(
+            jax.ShapeDtypeStruct((2, chips, rows, 3 * width), BF16),
+            jax.ShapeDtypeStruct((chips, rows, depth), F32),
+            jax.ShapeDtypeStruct((chips, rows, depth), BF16),
+        ),
         in_specs=[SMEM()] + [VMEM()] * (len(operands) - 1),
-        out_specs=VMEM(),
+        out_specs=(VMEM(),) * 3,
         scratch_shapes=[
             pltpu.VMEM((count, width), BF16),
             pltpu.VMEM((8, count), F32),
@@ -868,6 +876,11 @@
 
     packed = pack_heads(share_at[None].astype(jnp.int32), (w_query, w_key, w_value, w_out))
 
+    def summed_shares(part):
+        kept = lax.dynamic_slice_in_dim(part, share_at * 2 * width, 2 * width, 0)
+        sent = lax.dynamic_slice_in_dim(part, (1 - share_at) * 2 * width, 2 * width, 0)
+        return (kept.astype(F32) + swap(sent, share_axes[:1]).astype(F32)).astype(BF16)
+
     def add_received(total, sent):
         for i in range(1, 1 + sent.shape[0]):
             total = total + swap(sent[i - 1], axes_of(i, share_axes)).astype(F32)
@@ -877,9 +890,7 @@
     mlp_gains = [mlp_gain[n][None] for n in range(layers)]
     residual = turn(inputs)
     w_heads = [turn(packed[0])] + [None] * (layers - 1)
-    residual, cosine, sine, w_heads[0] = lax.optimization_barrier(
-        (residual, cosine, sine, w_heads[0])
-    )
+    residual, cosine, sine = lax.optimization_barrier((residual, cosine, sine))
     residual = residual.astype(F32)
     w_outs = [None] * layers
 
@@ -888,31 +899,33 @@
     for layer in range(layers):
         final = layer == layers - 1
         before = residual
-        w_heads[layer] = joined_shares(after(w_heads[layer], before))
-        near, far = gather(
-            normed_rows(before, attn_gains[layer]), group_axes, core, w_heads[layer]
-        )
+        normed = normed_rows(before, attn_gains[layer])
+        if layer == 0:
+            near, far = gather(normed, group_axes, core, w_heads[0])
+            w_heads[0] = joined_shares(w_heads[0])
+        else:
+            w_heads[layer] = joined_shares(after(w_heads[layer], before))
+            near, far = gather(normed, group_axes, core, w_heads[layer])
         blocks = near + far
         if layer == 0:
             ids = group_ids(after(number, near[1]))
         queries, keys, values = project(ids, blocks, w_heads[layer], cosine, sine, first_values)
         if layer == 0:
             first_values = values
-            feeds = [swap(after(w, queries), (core,)) for w in feed_all[:2]]
+            feeds = [swap(after(feed_all[0], queries), (core,))]
         out_chips = gather_chips(after(w_heads[layer][3 * width :], queries), group_axes)
         attended, log_totals = attend(ids, queries, keys, values, chips, rows)
         attended = after(attended, *out_chips[1:], *(feeds if layer == 0 else ()))
+        out_chips = jnp.concatenate(out_chips, axis=0)
+        w_outs[layer] = jnp.concatenate([out_chips, swap(out_chips, (core,))], axis=0)
         if layer == 1:
             down_in = gather_chips(after(grad, queries), share_axes)
+            attended = after(attended, down_in[-1])
         near, far = exchange(attended, group_axes, core)
-        out_chips = after(jnp.concatenate(out_chips, axis=0), near[-1])
-        w_outs[layer] = jnp.concatenate([out_chips, swap(out_chips, (core,))], axis=0)
         if layer == 0:
-            feeds.append(swap(after(feed_all[2], far), (core,)))
+            feeds += [swap(after(w, far, w_outs[0]), (core,)) for w in feed_all[1:]]
             feed_all = feed_all + tuple(feeds)
             grad = turn(after(cotangent, far))
-        if layer == 1:
-            far = after(far, down_in[-1])
         attended_rows, middle, normed = middle_step(
             near, far, w_outs[layer], before, mlp_gains[layer]
         )
@@ -933,9 +946,9 @@
                 residual = after(residual, grad)
 
     grad = grad.astype(F32)
-    attn_grads, mlp_grads = [], []
+    attn_parts, mlp_grads = [], []
     attn_gain_grads, mlp_gain_grads = [], []
-    later_layer = None
+    later_layer, sums = None, []
     by_blocks = inputs.shape[1] % (128 * 2 ** len(head_axes)) == 0
     for layer in reversed(range(layers)):
         final = layer == layers - 1
@@ -943,78 +956,105 @@
         mixed = k["mixed"]
         if not final:
             down_in = gather_chips(grad.astype(BF16), share_axes)
+            if by_blocks:
+                mixed = [after(mixed[0], sums[0][0].step())] + mixed[1:]
         own_term, sent, *rest = feed_back(layer, mixed, down_in, feed_all, final)
         received = [swap(sent[i - 1], axes_of(i, share_axes)) for i in range(1, len(mixed))]
+        if not final and by_blocks:
+            rest[3] = after(rest[3], sums[0][1].step())
         other = swap(feed_weights(rest[3:6], mixed, down_in, None), (core,))
-        ties = ()
-        if layer:
-            mlp_part = feed_weights(rest[:3], mixed, down_in, other)
-            block = lax.psum_scatter(mlp_part, head_axes, scatter_dimension=0, tiled=True)
-            mlp_grads.append(block)
-            mlp_part = (mlp_part,)
-        elif by_blocks:
+        if not final and by_blocks:
+            other = after(other, *steps(sums[0]))
+        if by_blocks:
             mlp_part = feed_weights(
                 rest[:3], mixed, down_in, other, feed_places, 2 ** len(head_axes)
             )
-            half = mlp_part[0].shape[0] // 2
-            ties = [swap(p[half:], order[:1]) for p, order in zip(mlp_part, feed_orders)]
+            sums.insert(0, [BlockSum(p, order) for p, order in zip(mlp_part, feed_orders)])
         else:
             mlp_part = (feed_weights(rest[:3], mixed, down_in, other),)
-            mlp_grads.append(lax.psum(mlp_part[0], head_axes[::-1]))
-        if not final:
-            own_term = after(own_term, mlp_grads[0])
-            mlp_grads[0] = lax.all_gather(mlp_grads[0], head_axes, axis=0, tiled=True)
+            mlp_grads.insert(0, lax.psum(mlp_part[0], head_axes if layer else head_axes[::-1]))
         middle_back, attn_in, gain_part, heads_back = middle_back_step(
             own_term, received, k["middle"], mlp_gains[layer], w_outs[layer], grad, chips
         )
         mlp_gain_grads.append(gain_part[0])
         near, far = exchange(heads_back, group_axes, core)
+        if by_blocks and layer == 0:
+            far = after(far, *steps(sums[0]))
         if final:
             block_out = add_received(k["middle"] + rest[6], after(rest[7], far)).astype(BF16)
-        raws = attend_back(
-            ids, after(k["queries"], *mlp_part), k["keys"], k["values"], k["attended"], near, far,
-            k["log_totals"], cosine, sine, later_layer,
+        raws, mine, others = attend_back(
+            ids, k["queries"], k["keys"], k["values"], k["attended"], near, far,
+            k["log_totals"], cosine, sine, w_heads[layer], later_layer,
         )
         later_layer = raws
-        into = w_heads[layer][: 3 * width]
-        others = matmul(flat(raws[1]), into).astype(BF16).reshape(chips, rows, -1)
-        mine = matmul(flat(raws[0]), into).reshape(chips, rows, -1)
+        if by_blocks:
+            others = after(others, *steps(sums[0]))
+        if final:
+            others, block_out = lax.optimization_barrier((others, block_out))
+        if layer == layers - 2:
+            block_out = turn(after(block_out, far))
+            others, block_out = lax.optimization_barrier((others, block_out))
+        ties = steps(sums[0]) if by_blocks and layer else ()
         normed_in = scatter_sum(mine, others, group_axes, core, *ties)
         part, gain_part = norm_back(k["before"], attn_gains[layer], normed_in)
         attn_gain_grads.append(gain_part)
         grad = middle_back + part
-        if not final:
-            grad = after(grad, mlp_grads[0])
-        attn_in = after(attn_in, grad)
-        out_terms = matmul_tn(k["attended_rows"], attn_in).reshape(2, chips, width, -1)
-        out_grad = scatter_sum(out_terms[0], out_terms[1].astype(BF16), group_axes, core)
-        heads_grad = head_weights(after(raws, grad), k["blocks"])
-        attn_grads.append(jnp.concatenate([heads_grad, out_grad.astype(BF16)], axis=0))
-
-    joined = jnp.stack(attn_grads[::-1], axis=1)
-    kept_part = lax.dynamic_slice_in_dim(joined, share_at * 2 * width, 2 * width, 0)
-    sent_part = lax.dynamic_slice_in_dim(joined, (1 - share_at) * 2 * width, 2 * width, 0)
-    summed = kept_part.astype(F32) + swap(sent_part, share_axes[:1]).astype(F32)
-    summed = exchange_sum(turn(summed.astype(BF16)), (core,) + share_axes[1:])
-    attn_all = joined_shares(summed).astype(F32).transpose(1, 0, 2)
-
-    given = turn(jnp.stack([block_out, grad.astype(BF16)]))
-    gains = exchange_sum(
-        jnp.stack(attn_gain_grads[::-1] + mlp_gain_grads[::-1]), hid_axes[::-1] + head_axes, F32
+        if by_blocks:
+            grad = after(grad, *steps(sums[0]))
+        attn_parts.insert(0, (raws, attn_in))
+
+    out_terms = jnp.stack(
+        [
+            matmul_tn(stored[n]["attended_rows"], after(attn_in, grad) if n else attn_in).reshape(
+                2, chips, width, -1
+            )
+            for n, (_, attn_in) in enumerate(attn_parts)
+        ],
+        axis=2,
     )
+    out_terms, grad = lax.optimization_barrier((out_terms, grad))
+    mine = out_terms[0] + swap(out_terms[1].astype(BF16), (core,)).astype(F32)
+    sent = mine.astype(BF16)
+    ties = steps(sums[0], sent) + steps(sums[1], sent) if by_blocks else ()
+    out_grads = mine[0]
+    for i in range(1, chips):
+        out_grads = out_grads + swap(sent[i], axes_of(i, group_axes)).astype(F32)
+    out_grads = out_grads.astype(BF16)
+    heads_grads = [
+        head_weights(after(raws, grad, *([] if n else ties[:2])), stored[n]["blocks"])
+        for n, (raws, _) in enumerate(attn_parts)
+    ]
+    sixth = ties[2:]
+    ties = steps(sums[0], out_grads) if by_blocks else ()
+    late = steps(sums[0]) + sixth if by_blocks else ()
+
+    gains = jnp.stack(attn_gain_grads[::-1] + mlp_gain_grads[::-1])
+    gains = exchange_sum(gains, hid_axes[::-1] + head_axes, F32)
+    part = [jnp.concatenate(pair, axis=0) for pair in zip(heads_grads, out_grads)]
+    part = summed_shares(jnp.stack(part, axis=1))
+    part, gains, *_ = lax.optimization_barrier((part, gains, *ties))
+    part = turn(part)
+    given = grad.astype(BF16)
+    part, given, *_ = lax.optimization_barrier((part, given, *late))
+    given = turn(given).astype(F32)
+    part = exchange_sum(part, (core,) + share_axes[1:])
+    attn_all = joined_shares(part).astype(F32).transpose(1, 0, 2)
+
     if by_blocks:
-        spread = [
-            spread_blocks(reduce_blocks(part[:half], received, order), order)
-            for part, received, order in zip(mlp_part, ties, feed_orders)
-        ]
-        feed_grads = place_feed(feed_places, *spread, jnp.stack(mlp_grads[::-1]))
+        feed_grads = ()
+        for layer in reversed(range(layers)):
+            while sums[layer][0].done < 2 * len(head_axes):
+                steps(sums[layer])
+            feed_grads = place_feed(
+                feed_places, [part.kept for part in sums[layer]], 2 ** len(head_axes), layer, layers, feed_grads
+            )
     else:
-        mlp_all = jnp.stack(mlp_grads[::-1]).astype(F32)
+        mlp_all = jnp.stack(mlp_grads).astype(F32)
         size = w_gate.shape[2]
         feed_grads = [mlp_all[:, n * size : (n + 1) * size] for n in range(3)]
     return (
-        given[0],
-        given[1].astype(F32),
+        block_out,
+        given,
         gains[:layers],
         attn_all[:, :width].transpose(0, 2, 1),
         attn_all[:, width : 2 * width].transpose(0, 2, 1),

time: 709 us -> 676 us (0.953)
  starting transfers between devices: 113 us -> 154 us
  waiting for transfers between devices: 353 us -> 321 us
  local copies, waits for them, and re-layouts: 57.1 us -> 33.1 us
  between operations: 19 us -> 6.3 us
  matrix products: 8.74 us -> 1.49 us
    ppermute x92 -> x100, starting transfers between devices: 106 us -> 146 us  [swap(): lax.ppermute(value, axes if len(axes) > 1 else axes[0], [(i, size - 1 - i...]
    ppermute x92 -> x100, waiting for transfers between devices: 352 us -> 321 us  [swap(): lax.ppermute(value, axes if len(axes) > 1 else axes[0], [(i, size - 1 - i...]
    unnamed x285 -> x276, local copies, waits for them, and re-layouts: 44.7 us -> 25.1 us
  transfers between devices with their start and end apart: 101 -> 108, of which waited for: 53 -> 47; matrix products, arithmetic and copies ran while one was open for 6% -> 5% of each run, Pallas kernels for 12% -> 13%
where the time goes in v3:
time: 676 us; the launch traced here: 670 us
  waiting for transfers between devices  321 us (47%)
  starting transfers between devices  154 us (23%)
  Pallas kernels  127 us (19%)
  local copies, waits for them, and re-layouts  33.1 us (5%)
  other arithmetic  27.3 us (4%)
    ppermute x100, waiting for transfers between devices, swap(): lax.ppermute(value, axes if len(axes) > 1 else axes[0], [(i, size - 1 - i...  321 us
    ppermute x100, starting transfers between devices, swap(): lax.ppermute(value, axes if len(axes) > 1 else axes[0], [(i, size - 1 - i...  146 us
    pallas_call x2, Pallas kernels, feed_back(): pl.pallas_call(functools.partial(feed_back_kernel, layer, shares, len(wei...  29.5 us
    unnamed x276, local copies, waits for them, and re-layouts  25.1 us
    pallas_call x2, Pallas kernels, attend_back(): pl.pallas_call(functools.partial(attend_back_kernel, chips, rows, width,...  25 us
    pallas_call x2, Pallas kernels, attend(): pl.pallas_call(functools.partial(attend_kernel, chips, rows, width), out_...  20 us
    pallas_call x4, Pallas kernels, feed_weights(): pl.pallas_call(functools.partial(feed_weights_kernel, shares, received is...  15.5 us
  transfers between devices with their start and end apart: 108, of which 47 were waited for; matrix products, arithmetic and copies ran while one was open for 5% of the time, Pallas kernels for 13%

profile of v3, /device:TPU:0, one launch (start us, length us, event | category | flops | bytes accessed | tf_op | source)
XLA Modules:
  0.0 670.4 jit_solution(14458486955583822924)
XLA Ops:
  9.4 3.7 fusion.9
  14.2 3.0 collective-permute-start.2
  18.8 9.1 %collective-permute-start.4 = (bf16[256,1024]{1,0:T(8,128)(2,1)S(1)}, bf16[256,1024]{1,0:T(8,128)(2,1)}, u32[]{:S(2)}, u32[]{:S(2)}) collective-permute-start(bf16[256,1024]{1,0:T(8,128)(2,1)S(1)} %fusion.3.refs_1_.refs_0_), channel_id=1, source_target_pairs={{0,1},{1,0},{2,3},{3,2},{4,5},{5,4},{6,7},{7,6},{8,9},{9,8},{10,11... | collective-permute-start | bytes 1572872 | tf_op jit(solution)/shard_map/ppermute | solution.py:30
  33.7 4.5 collective-permute-start.9
  43.0 2.9 maximum_select_fusion.1.refs_9_.refs_13_
  54.5 4.3 project_heads.2
  62.6 10.1 %attend_forward.2 = (bf16[4,2,256,128]{3,2,1,0:T(8,128)(2,1)S(1)}, f32[8,2048]{1,0:T(8,128)S(1)}) custom-call(s32[8]{0:T(128)S(1)} %pad_add_fusion.1.refs_0_, bf16[2048,128]{1,0:T(8,128)(2,1)S(1)} %get-tuple-element.132.refs_1_, bf16[2048,128]{1,0:T(8,128)(2,1)S(1)} %get-tuple-element.133.refs_2_, bf16[2048,128]{1,0:T(8,128)(2,1)S(1)} %get-tuple-element.134.refs_3_.refs_12_), custom_call_target="tpu_custom_call" | custom-call | flops 1717986944 | bytes 419430 | tf_op jit(solution)/shard_map/attend_forward/pallas_call | solution.py:635
  78.4 6.4 collective-permute-done.19.refs_3_
  89.6 9.3 %collective-permute-done.23.refs_1_.refs_4_.refs_5_ = bf16[256,1024]{1,0:T(8,128)(2,1)S(1)} collective-permute-done((bf16[256,1024]{1,0:T(8,128)(2,1)S(1)}, bf16[256,1024]{1,0:T(8,128)(2,1)S(1)}, u32[]{:S(2)}, u32[]{:S(2)}) %collective-permute-start.23) | collective-permute-done | bytes 524320 | tf_op jit(solution)/shard_map/ppermute | solution.py:30
  99.0 2.7 copy-done.101
  101.6 8.4 %feed_forward.1 = (f32[256,1024]{1,0:T(8,128)S(1)}, bf16[1,256,1024]{2,1,0:T(8,128)(2,1)S(1)}) custom-call(bf16[256,1024]{1,0:T(8,128)(2,1)S(1)} %get-tuple-element.169.refs_0_.refs_3_.refs_4_, bf16[256,1024]{1,0:T(8,128)(2,1)S(1)} %collective-permute-done.23.refs_1_.refs_4_.refs_5_, bf16[2,704,1024]{2,1,0:T(8,128)(2,1)S(1)} %bitcast.140, ...), custom_call_target="tpu_custom_call" | custom-call | flops 885836992 | bytes 1730150 | tf_op jit(solution)/shard_map/feed_forward/pallas_call | solution.py:357
  111.1 8.2 %collective-permute-done.26 = bf16[256,1024]{1,0:T(8,128)(2,1)S(1)} collective-permute-done((bf16[256,1024]{1,0:T(8,128)(2,1)S(1)}, bf16[256,1024]{1,0:T(8,128)(2,1)S(1)}, u32[]{:S(2)}, u32[]{:S(2)}) %collective-permute-start.26) | collective-permute-done | bytes 524320 | tf_op jit(solution)/shard_map/ppermute | solution.py:30
  120.1 2.5 collective-permute-start.28
  122.8 13.7 %collective-permute-start.30 = (bf16[256,1024]{1,0:T(8,128)(2,1)S(1)}, bf16[256,1024]{1,0:T(8,128)(2,1)S(1)}, u32[]{:S(2)}, u32[]{:S(2)}) collective-permute-start(bf16[256,1024]{1,0:T(8,128)(2,1)S(1)} %multiply_convert_fusion.refs_1_.refs_0_), channel_id=1, source_target_pairs={{0,1},{1,0},{2,3},{3,2},{4,5},{5,4},{6,7},{7,6},{8,9},{9,8},{10,11... | collective-permute-start | bytes 1572872 | tf_op jit(solution)/shard_map/ppermute | solution.py:30
  141.3 7.4 %collective-permute-start.34 = (bf16[256,1024]{1,0:T(8,128)(2,1)S(1)}, bf16[256,1024]{1,0:T(8,128)(2,1)S(1)}, u32[]{:S(2)}, u32[]{:S(2)}) collective-permute-start(bf16[256,1024]{1,0:T(8,128)(2,1)S(1)} %collective-permute-done.28.refs_2_.refs_1_), channel_id=1, source_target_pairs={{0,1},{1,0},{2,3},{3,2},{4,5},{5,4},{6,7},{7,6},{8,9},{9,8},{10,11... | collective-permute-start | bytes 1572872 | tf_op jit(solution)/shard_map/ppermute | solution.py:30
  148.8 4.2 collective-permute-start.36
  154.6 3.0 project_heads.3
  162.8 10.0 %attend_forward.3 = (bf16[4,2,256,128]{3,2,1,0:T(8,128)(2,1)S(1)}, f32[8,2048]{1,0:T(8,128)S(1)}) custom-call(s32[8]{0:T(128)S(1)} %pad_add_fusion.1.refs_0_, bf16[2048,128]{1,0:T(8,128)(2,1)S(1)} %get-tuple-element.153.refs_1_, bf16[2048,128]{1,0:T(8,128)(2,1)S(1)} %get-tuple-element.154.refs_2_, bf16[2048,128]{1,0:T(8,128)(2,1)S(1)} %get-tuple-element.155.refs_3_), custom_call_target="tpu_custom_call" | custom-call | flops 1717986944 | bytes 419430 | tf_op jit(solution)/shard_map/attend_forward/pallas_call | solution.py:635
  178.3 5.7 collective-permute-done.43.refs_3_
  188.9 12.5 %collective-permute-done.46.refs_1_.refs_4_.refs_5_ = bf16[256,1024]{1,0:T(8,128)(2,1)S(1)} collective-permute-done((bf16[256,1024]{1,0:T(8,128)(2,1)S(1)}, bf16[256,1024]{1,0:T(8,128)(2,1)S(1)}, u32[]{:S(2)}, u32[]{:S(2)}) %collective-permute-start.46) | collective-permute-done | bytes 524320 | tf_op jit(solution)/shard_map/ppermute | solution.py:30
  203.2 14.7 %feed_backward.2 = (f32[256,1024]{1,0:T(8,128)S(1)}, bf16[1,256,1024]{2,1,0:T(8,128)(2,1)}, bf16[512,704]{1,0:T(8,128)(2,1)S(1)}, bf16[512,704]{1,0:T(8,128)(2,1...) custom-call(bf16[256,1024]{1,0:T(8,128)(2,1)S(1)} %get-tuple-element, ...), custom_call_target="tpu_custom_call" | custom-call | flops 1771673984 | bytes 1730150 | tf_op jit(solution)/shard_map/feed_backward/pallas_call | solution.py:428
  218.0 4.5 feed_weight_grads.4
  225.5 11.8 %collective-permute-done.52.refs_1_ = bf16[256,1024]{1,0:T(8,128)(2,1)} collective-permute-done((bf16[256,1024]{1,0:T(8,128)(2,1)}, bf16[256,1024]{1,0:T(8,128)(2,1)}, u32[]{:S(2)}, u32[]{:S(2)}) %collective-permute-start.52) | collective-permute-done | bytes 524320 | tf_op jit(solution)/shard_map/ppermute | solution.py:30
  238.5 2.5 attention_out_back.2
  244.7 5.7 collective-permute-done.55.refs_8_
  250.7 5.1 feed_weight_grads.5
  260.0 11.9 %attend_backward.2 = (bf16[2,4,256,384]{3,2,1,0:T(8,128)(2,1)S(1)}, f32[4,256,1024]{2,1,0:T(8,128)S(1)}, bf16[4,256,1024]{2,1,0:T(8,128)(2,1)S(1)}) custom-call(s32[8]{0:T(128)S(1)} %pad_add_fusion.1.refs_0_, bf16[2048,128]{1,0:T(8,128)(2,1)S(1)} %copy-done.89, bf16[2048,128]{1,0:T(8,128)(2,1)S(1)} %copy-done.91, bf16[2048,128]{1,0:T(8,128)(2,1)S(1)} %copy-done.93, ...), custom_call_target="tpu_custom_call" | custom-call | flops 4294967296 | bytes 2097152 | tf_op jit(solution)/shard_map/attend_backward/pallas_call | solution.py:761
  273.3 9.0 %collective-permute-done.48 = bf16[4,1056,128]{2,1,0:T(8,128)(2,1)S(1)} collective-permute-done((bf16[4,1056,128]{2,1,0:T(8,128)(2,1)S(1)}, bf16[4,1056,128]{2,1,0:T(8,128)(2,1)S(1)}, u32[]{:S(2)}, u32[]{:S(2)}) %collective-permute-start.48) | collective-permute-done | bytes 1081376 | tf_op jit(solution)/shard_map/ppermute | solution.py:30
  285.9 12.0 %collective-permute-done.49 = bf16[2,1056,128]{2,1,0:T(8,128)(2,1)S(1)} collective-permute-done((bf16[2,1056,128]{2,1,0:T(8,128)(2,1)S(1)}, bf16[2,1056,128]{2,1,0:T(8,128)(2,1)S(1)}, u32[]{:S(2)}, u32[]{:S(2)}) %collective-permute-start.49) | collective-permute-done | bytes 540704 | tf_op jit(solution)/shard_map/ppermute | solution.py:30
  298.1 5.6 collective-permute-start.50
  308.8 7.2 %collective-permute-done.50 = bf16[1,1056,128]{2,1,0:T(8,128)(2,1)S(1)} collective-permute-done((bf16[1,1056,128]{2,1,0:T(8,128)(2,1)S(1)}, bf16[1,1056,128]{2,1,0:T(8,128)(2,1)S(1)}, u32[]{:S(2)}, u32[]{:S(2)}) %collective-permute-start.50) | collective-permute-done | bytes 270368 | tf_op jit(solution)/shard_map/ppermute | solution.py:30
  316.2 21.4 %collective-permute-done.63 = bf16[256,1024]{1,0:T(8,128)(2,1)S(1)} collective-permute-done((bf16[256,1024]{1,0:T(8,128)(2,1)S(1)}, bf16[256,1024]{1,0:T(8,128)(2,1)S(1)}, u32[]{:S(2)}, u32[]{:S(2)}) %collective-permute-start.63) | collective-permute-done | bytes 524320 | tf_op jit(solution)/shard_map/ppermute | solution.py:30
  337.6 9.4 %collective-permute-done.62 = bf16[256,1024]{1,0:T(8,128)(2,1)S(1)} collective-permute-done((bf16[256,1024]{1,0:T(8,128)(2,1)S(1)}, bf16[256,1024]{1,0:T(8,128)(2,1)S(1)}, u32[]{:S(2)}, u32[]{:S(2)}) %collective-permute-start.62) | collective-permute-done | bytes 524320 | tf_op jit(solution)/shard_map/ppermute | solution.py:30
  349.8 10.7 %collective-permute-done.65.refs_3_.refs_6_.refs_7_ = bf16[256,1024]{1,0:T(8,128)(2,1)S(1)} collective-permute-done((bf16[256,1024]{1,0:T(8,128)(2,1)S(1)}, bf16[256,1024]{1,0:T(8,128)(2,1)S(1)}, u32[]{:S(2)}, u32[]{:S(2)}) %collective-permute-start.65) | collective-permute-done | bytes 524320 | tf_op jit(solution)/shard_map/ppermute | solution.py:30
  360.5 14.8 %feed_backward.3 = (f32[256,1024]{1,0:T(8,128)S(1)}, bf16[1,256,1024]{2,1,0:T(8,128)(2,1)S(1)}, bf16[512,704]{1,0:T(8,128)(2,1)S(1)}, bf16[512,704]{1,0:T(8,128)...) custom-call(bf16[256,1024]{1,0:T(8,128)(2,1)S(1)} %copy-done.27, ...), custom_call_target="tpu_custom_call" | custom-call | flops 1771673984 | bytes 1730150 | tf_op jit(solution)/shard_map/feed_backward/pallas_call | solution.py:428
  375.3 2.4 feed_weight_grads.6
  380.4 12.2 %collective-permute-done.73 = bf16[2,1056,128]{2,1,0:T(8,128)(2,1)S(1)} collective-permute-done((bf16[2,1056,128]{2,1,0:T(8,128)(2,1)S(1)}, bf16[2,1056,128]{2,1,0:T(8,128)(2,1)S(1)}, u32[]{:S(2)}, u32[]{:S(2)}) %collective-permute-start.73) | collective-permute-done | bytes 540704 | tf_op jit(solution)/shard_map/ppermute | solution.py:30
  392.8 3.5 feed_weight_grads.7
  402.1 2.4 collective-permute-start.69
  404.5 26.0 %collective-permute-done.69.refs_8_ = bf16[2,256,128]{2,1,0:T(8,128)(2,1)S(1)} collective-permute-done((bf16[2,256,128]{2,1,0:T(8,128)(2,1)S(1)}, bf16[2,256,128]{2,1,0:T(8,128)(2,1)S(1)}, u32[]{:S(2)}, u32[]{:S(2)}) %collective-permute-start.69) | collective-permute-done | bytes 131104 | tf_op jit(solution)/shard_map/ppermute | solution.py:30
  435.8 13.2 %attend_backward.3 = (bf16[2,4,256,384]{3,2,1,0:T(8,128)(2,1)S(1)}, f32[4,256,1024]{2,1,0:T(8,128)S(1)}, bf16[4,256,1024]{2,1,0:T(8,128)(2,1)}) custom-call(s32[8]{0:T(128)S(1)} %pad_add_fusion.1.refs_0_, bf16[2048,128]{1,0:T(8,128)(2,1)S(1)} %copy-done.85, bf16[2048,128]{1,0:T(8,128)(2,1)S(1)} %copy-done.87, bf16[2048,128]{1,0:T(8,128)(2,1)S(1)} %copy-done.59, ...), custom_call_target="tpu_custom_call" | custom-call | flops 4294967296 | bytes 2097152 | tf_op jit(solution)/shard_map/attend_backward/pallas_call | solution.py:761
  454.9 2.6 collective-permute-start.84
  457.5 2.7 fusion.28
  464.2 2.9 collective-permute-start.85
  467.1 20.2 %collective-permute-done.83 = bf16[256,1024]{1,0:T(8,128)(2,1)S(1)} collective-permute-done((bf16[256,1024]{1,0:T(8,128)(2,1)S(1)}, bf16[256,1024]{1,0:T(8,128)(2,1)S(1)}, u32[]{:S(2)}, u32[]{:S(2)}) %collective-permute-start.83) | collective-permute-done | bytes 524320 | tf_op jit(solution)/shard_map/ppermute | solution.py:30
  487.3 10.1 %collective-permute-done.82 = bf16[256,1024]{1,0:T(8,128)(2,1)S(1)} collective-permute-done((bf16[256,1024]{1,0:T(8,128)(2,1)S(1)}, bf16[256,1024]{1,0:T(8,128)(2,1)S(1)}, u32[]{:S(2)}, u32[]{:S(2)}) %collective-permute-start.82) | collective-permute-done | bytes 524320 | tf_op jit(solution)/shard_map/ppermute | solution.py:30
  503.0 3.4 collective-permute-done.93
  506.4 7.6 %collective-permute-start.94 = (f32[4,1024]{1,0:T(4,128)S(1)}, f32[4,1024]{1,0:T(4,128)S(1)}, u32[]{:S(2)}, u32[]{:S(2)}) collective-permute-start(f32[4,1024]{1,0:T(4,128)S(1)} %fusion.25), channel_id=1, source_target_pairs={{0,2},{2,0},{1,3},{3,1},{4,6},{6,4},{5,7},{7,5},{8,10},{10,8},{9,1... | collective-permute-start | bytes 49160 | tf_op jit(solution)/shard_map/ppermute | solution.py:30
  516.9 3.7 collective-permute-done.95
  532.5 12.8 %collective-permute-done.87 = bf16[1,1056,128]{2,1,0:T(8,128)(2,1)S(1)} collective-permute-done((bf16[1,1056,128]{2,1,0:T(8,128)(2,1)S(1)}, bf16[1,1056,128]{2,1,0:T(8,128)(2,1)S(1)}, u32[]{:S(2)}, u32[]{:S(2)}) %collective-permute-start.87) | collective-permute-done | bytes 270368 | tf_op jit(solution)/shard_map/ppermute | solution.py:30
  546.1 4.2 collective-permute-done.88
  550.5 3.6 head_weight_grads.2
  554.1 2.7 collective-permute-done.91
  556.8 5.6 collective-permute-done.90
  569.4 8.8 %collective-permute-done.98 = bf16[2,1056,128]{2,1,0:T(8,128)(2,1)S(1)} collective-permute-done((bf16[2,1056,128]{2,1,0:T(8,128)(2,1)S(1)}, bf16[2,1056,128]{2,1,0:T(8,128)(2,1)S(1)}, u32[]{:S(2)}, u32[]{:S(2)}) %collective-permute-start.98) | collective-permute-done | bytes 540704 | tf_op jit(solution)/shard_map/ppermute | solution.py:30
  582.5 6.2 collective-permute-done.92
  589.8 14.4 %collective-permute-done.103 = bf16[4,1056,128]{2,1,0:T(8,128)(2,1)S(1)} collective-permute-done((bf16[4,1056,128]{2,1,0:T(8,128)(2,1)S(1)}, bf16[4,1056,128]{2,1,0:T(8,128)(2,1)S(1)}, u32[]{:S(2)}, u32[]{:S(2)}) %collective-permute-start.103) | collective-permute-done | bytes 1081376 | tf_op jit(solution)/shard_map/ppermute | solution.py:30
  604.2 8.3 %collective-permute-done.104 = bf16[4,1056,128]{2,1,0:T(8,128)(2,1)S(1)} collective-permute-done((bf16[4,1056,128]{2,1,0:T(8,128)(2,1)S(1)}, bf16[4,1056,128]{2,1,0:T(8,128)(2,1)S(1)}, u32[]{:S(2)}, u32[]{:S(2)}) %collective-permute-start.104) | collective-permute-done | bytes 1081376 | tf_op jit(solution)/shard_map/ppermute | solution.py:30
  612.5 13.0 %collective-permute-done.101 = bf16[4,1056,128]{2,1,0:T(8,128)(2,1)S(1)} collective-permute-done((bf16[4,1056,128]{2,1,0:T(8,128)(2,1)S(1)}, bf16[4,1056,128]{2,1,0:T(8,128)(2,1)S(1)}, u32[]{:S(2)}, u32[]{:S(2)}) %collective-permute-start.101) | collective-permute-done | bytes 1081376 | tf_op jit(solution)/shard_map/ppermute | solution.py:30
  625.6 8.0 %collective-permute-done.102 = bf16[4,1056,128]{2,1,0:T(8,128)(2,1)S(1)} collective-permute-done((bf16[4,1056,128]{2,1,0:T(8,128)(2,1)S(1)}, bf16[4,1056,128]{2,1,0:T(8,128)(2,1)S(1)}, u32[]{:S(2)}, u32[]{:S(2)}) %collective-permute-start.102) | collective-permute-done | bytes 1081376 | tf_op jit(solution)/shard_map/ppermute | solution.py:30
  633.8 2.5 collective-permute-done.106
  638.5 5.1 place_feed_grads.2
  645.3 5.1 place_feed_grads.3
  651.4 10.5 %collective-permute-done.107 = bf16[256,2,1024]{2,0,1:T(8,128)(2,1)S(1)} collective-permute-done((bf16[256,2,1024]{2,0,1:T(8,128)(2,1)S(1)}, bf16[256,2,1024]{2,0,1:T(8,128)(2,1)S(1)}, u32[]{:S(2)}, u32[]{:S(2)}) %collective-permute-start.107) | collective-permute-done | bytes 1048608 | tf_op jit(solution)/shard_map/ppermute | solution.py:30
  (587 shorter events, 162.3 us)
Async XLA Ops:
  7.8 20.1 %collective-permute-start.5 = (bf16[256,1024]{1,0:T(8,128)(2,1)S(1)}, bf16[256,1024]{1,0:T(8,128)(2,1)}, u32[]{:S(2)}, u32[]{:S(2)}) collective-permute-start(bf16[256,1024]{1,0:T(8,128)(2,1)S(1)} %get-tuple-element.276), channel_id=1, source_target_pairs={{0,0},{1,16},{16,1},{17,17},{2,2},{3,18},{18,3},{19,19},{4,4},{5,2... | collective-permute-start | bytes 1572872 | tf_op jit(solution)/shard_map/ppermute | solution.py:841
  14.2 17.3 %collective-permute-start.2 = (bf16[256,1024]{1,0:T(8,128)(2,1)S(1)}, bf16[256,1024]{1,0:T(8,128)(2,1)S(1)}, u32[]{:S(2)}, u32[]{:S(2)}) collective-permute-start(bf16[256,1024]{1,0:T(8,128)(2,1)S(1)} %fusion.3.refs_1_.refs_0_), channel_id=1, source_target_pairs={{0,4},{4,0},{1,5},{5,1},{2,6},{6,2},{3,7},{7,3},{8,12},{12,8},{9,1... | collective-permute-start | bytes 1572872 | tf_op jit(solution)/shard_map/ppermute | solution.py:30
  17.2 16.4 %collective-permute-start.3 = (bf16[256,1024]{1,0:T(8,128)(2,1)S(1)}, bf16[256,1024]{1,0:T(8,128)(2,1)}, u32[]{:S(2)}, u32[]{:S(2)}) collective-permute-start(bf16[256,1024]{1,0:T(8,128)(2,1)S(1)} %fusion.3.refs_1_.refs_0_), channel_id=1, source_target_pairs={{0,8},{8,0},{1,9},{9,1},{2,10},{10,2},{3,11},{11,3},{4,12},{12,4},... | collective-permute-start | bytes 1572872 | tf_op jit(solution)/shard_map/ppermute | solution.py:30
  18.8 14.9 %collective-permute-start.4 = (bf16[256,1024]{1,0:T(8,128)(2,1)S(1)}, bf16[256,1024]{1,0:T(8,128)(2,1)}, u32[]{:S(2)}, u32[]{:S(2)}) collective-permute-start(bf16[256,1024]{1,0:T(8,128)(2,1)S(1)} %fusion.3.refs_1_.refs_0_), channel_id=1, source_target_pairs={{0,1},{1,0},{2,3},{3,2},{4,5},{5,4},{6,7},{7,6},{8,9},{9,8},{10,11... | collective-permute-start | bytes 1572872 | tf_op jit(solution)/shard_map/ppermute | solution.py:30
  27.9 13.5 %collective-permute-start.12 = (bf16[256,1024]{1,0:T(8,128)(2,1)}, bf16[256,1024]{1,0:T(8,128)(2,1)}, u32[]{:S(2)}, u32[]{:S(2)}) collective-permute-start(bf16[256,1024]{1,0:T(8,128)(2,1)} %collective-permute-done.5), channel_id=1, source_target_pairs={{0,2},{2,0},{1,3},{3,1},{4,6},{6,4},{5,7},{7,5},{8,10},{10,8},{9,1... | collective-permute-start | bytes 1572872 | tf_op jit(solution)/shard_map/ppermute | solution.py:30
  33.7 17.9 %collective-permute-start.9 = (bf16[256,1024]{1,0:T(8,128)(2,1)S(1)}, bf16[256,1024]{1,0:T(8,128)(2,1)}, u32[]{:S(2)}, u32[]{:S(2)}) collective-permute-start(bf16[256,1024]{1,0:T(8,128)(2,1)S(1)} %collective-permute-done.2.refs_2_.refs_1_), channel_id=1, source_target_pairs={{0,1},{1,0},{2,3},{3,2},{4,5},{5,4},{6,7},{7,6},{8,9},{9,8},{10,11... | collective-permute-start | bytes 1572872 | tf_op jit(solution)/shard_map/ppermute | solution.py:30
  58.8 15.9 %collective-permute-start.16 = (bf16[2,704,1024]{2,1,0:T(8,128)(2,1)S(1)}, bf16[2,704,1024]{2,1,0:T(8,128)(2,1)S(1)}, u32[]{:S(2)}, u32[]{:S(2)}) collective-permute-start(bf16[2,704,1024]{2,1,0:T(8,128)(2,1)S(1)} %bitcast.139), channel_id=1, source_target_pairs={{0,1},{1,0},{2,3},{3,2},{4,5},{5,4},{6,7},{7,6},{8,9},{9,8},{10,11... | collective-permute-start | bytes 8650760 | tf_op jit(solution)/shard_map/ppermute | solution.py:30
  59.1 13.6 %collective-permute-start.13 = (bf16[128,1024]{1,0:T(8,128)(2,1)S(1)}, bf16[128,1024]{1,0:T(8,128)(2,1)S(1)}, u32[]{:S(2)}, u32[]{:S(2)}) collective-permute-start(bf16[128,1024]{1,0:T(8,128)(2,1)S(1)} %slice.393), channel_id=1, source_target_pairs={{0,4},{4,0},{1,5},{5,1},{2,6},{6,2},{3,7},{7,3},{8,12},{12,8},{9,1... | collective-permute-start | bytes 786440 | tf_op jit(solution)/shard_map/ppermute | solution.py:30
  60.8 13.7 %collective-permute-start.15 = (bf16[128,1024]{1,0:T(8,128)(2,1)S(1)}, bf16[128,1024]{1,0:T(8,128)(2,1)S(1)}, u32[]{:S(2)}, u32[]{:S(2)}) collective-permute-start(bf16[128,1024]{1,0:T(8,128)(2,1)S(1)} %slice.393), channel_id=1, source_target_pairs={{0,12},{4,8},{8,4},{12,0},{1,13},{5,9},{9,5},{13,1},{2,14},{6,10},... | collective-permute-start | bytes 786440 | tf_op jit(solution)/shard_map/ppermute | solution.py:30
  119.7 16.8 %collective-permute-start.31 = (bf16[256,1024]{1,0:T(8,128)(2,1)S(1)}, bf16[256,1024]{1,0:T(8,128)(2,1)S(1)}, u32[]{:S(2)}, u32[]{:S(2)}) collective-permute-start(bf16[256,1024]{1,0:T(8,128)(2,1)S(1)} %collective-permute-done.22), channel_id=1, source_target_pairs={{0,2},{2,0},{1,3},{3,1},{4,6},{6,4},{5,7},{7,5},{8,10},{10,8},{9,1... | collective-permute-start | bytes 1572872 | tf_op jit(solution)/shard_map/ppermute | solution.py:30
  120.1 17.0 %collective-permute-start.28 = (bf16[256,1024]{1,0:T(8,128)(2,1)S(1)}, bf16[256,1024]{1,0:T(8,128)(2,1)S(1)}, u32[]{:S(2)}, u32[]{:S(2)}) collective-permute-start(bf16[256,1024]{1,0:T(8,128)(2,1)S(1)} %multiply_convert_fusion.refs_1_.refs_0_), channel_id=1, source_target_pairs={{0,4},{4,0},{1,5},{5,1},{2,6},{6,2},{3,7},{7,3},{8,12},{12,8},{9,1... | collective-permute-start | bytes 1572872 | tf_op jit(solution)/shard_map/ppermute | solution.py:30
  122.6 14.5 %collective-permute-start.29 = (bf16[256,1024]{1,0:T(8,128)(2,1)S(1)}, bf16[256,1024]{1,0:T(8,128)(2,1)S(1)}, u32[]{:S(2)}, u32[]{:S(2)}) collective-permute-start(bf16[256,1024]{1,0:T(8,128)(2,1)S(1)} %multiply_convert_fusion.refs_1_.refs_0_), channel_id=1, source_target_pairs={{0,8},{8,0},{1,9},{9,1},{2,10},{10,2},{3,11},{11,3},{4,12},{12,4},... | collective-permute-start | bytes 1572872 | tf_op jit(solution)/shard_map/ppermute | solution.py:30
  122.8 15.3 %collective-permute-start.30 = (bf16[256,1024]{1,0:T(8,128)(2,1)S(1)}, bf16[256,1024]{1,0:T(8,128)(2,1)S(1)}, u32[]{:S(2)}, u32[]{:S(2)}) collective-permute-start(bf16[256,1024]{1,0:T(8,128)(2,1)S(1)} %multiply_convert_fusion.refs_1_.refs_0_), channel_id=1, source_target_pairs={{0,1},{1,0},{2,3},{3,2},{4,5},{5,4},{6,7},{7,6},{8,9},{9,8},{10,11... | collective-permute-start | bytes 1572872 | tf_op jit(solution)/shard_map/ppermute | solution.py:30
  157.8 15.0 %collective-permute-start.37 = (bf16[128,1024]{1,0:T(8,128)(2,1)S(1)}, bf16[128,1024]{1,0:T(8,128)(2,1)S(1)}, u32[]{:S(2)}, u32[]{:S(2)}) collective-permute-start(bf16[128,1024]{1,0:T(8,128)(2,1)S(1)} %slice.398), channel_id=1, source_target_pairs={{0,4},{4,0},{1,5},{5,1},{2,6},{6,2},{3,7},{7,3},{8,12},{12,8},{9,1... | collective-permute-start | bytes 786440 | tf_op jit(solution)/shard_map/ppermute | solution.py:30
  159.1 13.7 %collective-permute-start.38 = (bf16[128,1024]{1,0:T(8,128)(2,1)S(1)}, bf16[128,1024]{1,0:T(8,128)(2,1)S(1)}, u32[]{:S(2)}, u32[]{:S(2)}) collective-permute-start(bf16[128,1024]{1,0:T(8,128)(2,1)S(1)} %slice.398), channel_id=1, source_target_pairs={{0,8},{8,0},{1,9},{9,1},{2,10},{10,2},{3,11},{11,3},{4,12},{12,4},... | collective-permute-start | bytes 786440 | tf_op jit(solution)/shard_map/ppermute | solution.py:30
  187.4 14.0 %collective-permute-start.46 = (bf16[256,1024]{1,0:T(8,128)(2,1)S(1)}, bf16[256,1024]{1,0:T(8,128)(2,1)S(1)}, u32[]{:S(2)}, u32[]{:S(2)}) collective-permute-start(bf16[256,1024]{1,0:T(8,128)(2,1)S(1)} %get-tuple-element.161.refs_0_.refs_3_.refs_4_), channel_id=1, source_target_pairs={{0,2},{2,0},{1,3},{3,1},{4,6},{6,4},{5,7},{7,5},{8,10},{10,8},{9,1... | collective-permute-start | bytes 1572872 | tf_op jit(solution)/shard_map/ppermute | solution.py:30
  222.5 28.1 %collective-permute-start.47 = (bf16[2112,1024]{1,0:T(8,128)(2,1)}, bf16[2112,1024]{1,0:T(8,128)(2,1)}, u32[]{:S(2)}, u32[]{:S(2)}) collective-permute-start(bf16[2112,1024]{1,0:T(8,128)(2,1)} %feed_weight_grads.4), channel_id=1, source_target_pairs={{0,1},{1,0},{2,3},{3,2},{4,5},{5,4},{6,7},{7,6},{8,9},{9,8},{10,11... | collective-permute-start | bytes 12976136 | tf_op jit(solution)/shard_map/ppermute | solution.py:30
  222.6 14.7 %collective-permute-start.52 = (bf16[256,1024]{1,0:T(8,128)(2,1)}, bf16[256,1024]{1,0:T(8,128)(2,1)}, u32[]{:S(2)}, u32[]{:S(2)}) collective-permute-start(bf16[256,1024]{1,0:T(8,128)(2,1)} %bitcast.27), channel_id=1, source_target_pairs={{0,2},{2,0},{1,3},{3,1},{4,6},{6,4},{5,7},{7,5},{8,10},{10,8},{9,1... | collective-permute-start | bytes 1572872 | tf_op jit(solution)/shard_map/ppermute | solution.py:30
  256.0 26.3 %collective-permute-start.48 = (bf16[4,1056,128]{2,1,0:T(8,128)(2,1)S(1)}, bf16[4,1056,128]{2,1,0:T(8,128)(2,1)S(1)}, u32[]{:S(2)}, u32[]{:S(2)}) collective-permute-start(bf16[4,1056,128]{2,1,0:T(8,128)(2,1)S(1)} %slice.329), channel_id=1, source_target_pairs={{0,4},{4,0},{1,5},{5,1},{2,6},{6,2},{3,7},{7,3},{8,12},{12,8},{9,1... | collective-permute-start | bytes 3244040 | tf_op jit(solution)/shard_map/ppermute | solution.py:30
  256.8 26.0 %collective-permute-start.57 = (bf16[4,1056,128]{2,1,0:T(8,128)(2,1)S(1)}, bf16[4,1056,128]{2,1,0:T(8,128)(2,1)S(1)}, u32[]{:S(2)}, u32[]{:S(2)}) collective-permute-start(bf16[4,1056,128]{2,1,0:T(8,128)(2,1)S(1)} %slice.343), channel_id=1, source_target_pairs={{0,8},{8,0},{1,9},{9,1},{2,10},{10,2},{3,11},{11,3},{4,12},{12,4},... | collective-permute-start | bytes 3244040 | tf_op jit(solution)/shard_map/ppermute | solution.py:30
  258.4 13.7 %collective-permute-start.58 = (bf16[256,1024]{1,0:T(8,128)(2,1)S(1)}, bf16[256,1024]{1,0:T(8,128)(2,1)S(1)}, u32[]{:S(2)}, u32[]{:S(2)}) collective-permute-start(bf16[256,1024]{1,0:T(8,128)(2,1)S(1)} %bitcast.147), channel_id=1, source_target_pairs={{0,2},{2,0},{1,3},{3,1},{4,6},{6,4},{5,7},{7,5},{8,10},{10,8},{9,1... | collective-permute-start | bytes 1572872 | tf_op jit(solution)/shard_map/ppermute | solution.py:30
  282.9 20.9 %collective-permute-start.59 = (bf16[4,256,1024]{2,1,0:T(8,128)(2,1)S(1)}, bf16[4,256,1024]{2,1,0:T(8,128)(2,1)S(1)}, u32[]{:S(2)}, u32[]{:S(2)}) collective-permute-start(bf16[4,256,1024]{2,1,0:T(8,128)(2,1)S(1)} %get-tuple-element.183), channel_id=1, source_target_pairs={{0,1},{1,0},{2,3},{3,2},{4,5},{5,4},{6,7},{7,6},{8,9},{9,8},{10,11... | collective-permute-start | bytes 6291464 | tf_op jit(solution)/shard_map/ppermute | solution.py:30
  283.2 14.8 %collective-permute-start.49 = (bf16[2,1056,128]{2,1,0:T(8,128)(2,1)S(1)}, bf16[2,1056,128]{2,1,0:T(8,128)(2,1)S(1)}, u32[]{:S(2)}, u32[]{:S(2)}) collective-permute-start(bf16[2,1056,128]{2,1,0:T(8,128)(2,1)S(1)} %slice.403), channel_id=1, source_target_pairs={{0,8},{8,0},{1,9},{9,1},{2,10},{10,2},{3,11},{11,3},{4,12},{12,4},... | collective-permute-start | bytes 1622024 | tf_op jit(solution)/shard_map/ppermute | solution.py:30
  285.2 19.7 %collective-permute-start.60 = (bf16[2,1056,128]{2,1,0:T(8,128)(2,1)S(1)}, bf16[2,1056,128]{2,1,0:T(8,128)(2,1)S(1)}, u32[]{:S(2)}, u32[]{:S(2)}) collective-permute-start(bf16[2,1056,128]{2,1,0:T(8,128)(2,1)S(1)} %slice.410), channel_id=1, source_target_pairs={{0,4},{4,0},{1,5},{5,1},{2,6},{6,2},{3,7},{7,3},{8,12},{12,8},{9,1... | collective-permute-start | bytes 1622024 | tf_op jit(solution)/shard_map/ppermute | solution.py:30
  298.1 17.9 %collective-permute-start.50 = (bf16[1,1056,128]{2,1,0:T(8,128)(2,1)S(1)}, bf16[1,1056,128]{2,1,0:T(8,128)(2,1)S(1)}, u32[]{:S(2)}, u32[]{:S(2)}) collective-permute-start(bf16[1,1056,128]{2,1,0:T(8,128)(2,1)S(1)} %slice.405), channel_id=1, source_target_pairs={{0,16},{16,0},{1,17},{17,1},{2,18},{18,2},{3,19},{19,3},{4,20},{20... | collective-permute-start | bytes 811016 | tf_op jit(solution)/shard_map/ppermute | solution.py:30
  305.0 32.6 %collective-permute-start.63 = (bf16[256,1024]{1,0:T(8,128)(2,1)S(1)}, bf16[256,1024]{1,0:T(8,128)(2,1)S(1)}, u32[]{:S(2)}, u32[]{:S(2)}) collective-permute-start(bf16[256,1024]{1,0:T(8,128)(2,1)S(1)} %get-tuple-element.273), channel_id=1, source_target_pairs={{0,12},{4,8},{8,4},{12,0},{1,13},{5,9},{9,5},{13,1},{2,14},{6,10},... | collective-permute-start | bytes 1572872 | tf_op jit(solution)/shard_map/ppermute | solution.py:30
  306.3 40.7 %collective-permute-start.62 = (bf16[256,1024]{1,0:T(8,128)(2,1)S(1)}, bf16[256,1024]{1,0:T(8,128)(2,1)S(1)}, u32[]{:S(2)}, u32[]{:S(2)}) collective-permute-start(bf16[256,1024]{1,0:T(8,128)(2,1)S(1)} %get-tuple-element.274), channel_id=1, source_target_pairs={{0,8},{8,0},{1,9},{9,1},{2,10},{10,2},{3,11},{11,3},{4,12},{12,4},... | collective-permute-start | bytes 1572872 | tf_op jit(solution)/shard_map/ppermute | solution.py:30
  307.2 39.8 %collective-permute-start.61 = (bf16[256,1024]{1,0:T(8,128)(2,1)S(1)}, bf16[256,1024]{1,0:T(8,128)(2,1)S(1)}, u32[]{:S(2)}, u32[]{:S(2)}) collective-permute-start(bf16[256,1024]{1,0:T(8,128)(2,1)S(1)} %get-tuple-element.272), channel_id=1, source_target_pairs={{0,4},{4,0},{1,5},{5,1},{2,6},{6,2},{3,7},{7,3},{8,12},{12,8},{9,1... | collective-permute-start | bytes 1572872 | tf_op jit(solution)/shard_map/ppermute | solution.py:30
  308.7 39.3 %collective-permute-start.64 = (bf16[1,1056,128]{2,1,0:T(8,128)(2,1)S(1)}, bf16[1,1056,128]{2,1,0:T(8,128)(2,1)S(1)}, u32[]{:S(2)}, u32[]{:S(2)}) collective-permute-start(bf16[1,1056,128]{2,1,0:T(8,128)(2,1)S(1)} %slice.412), channel_id=1, source_target_pairs={{0,16},{16,0},{1,17},{17,1},{2,18},{18,2},{3,19},{19,3},{4,20},{20... | collective-permute-start | bytes 811016 | tf_op jit(solution)/shard_map/ppermute | solution.py:30
  316.1 33.7 %collective-permute-start.51 = (bf16[1,1056,128]{2,1,0:T(8,128)(2,1)S(1)}, bf16[1,1056,128]{2,1,0:T(8,128)(2,1)S(1)}, u32[]{:S(2)}, u32[]{:S(2)}) collective-permute-start(bf16[1,1056,128]{2,1,0:T(8,128)(2,1)S(1)} %add_convert_fusion.14), channel_id=1, source_target_pairs={{0,16},{16,0},{1,17},{17,1},{2,18},{18,2},{3,19},{19,3},{4,20},{20... | collective-permute-start | bytes 811016 | tf_op jit(solution)/shard_map/ppermute | solution.py:30
  349.7 25.6 %collective-permute-start.71 = (bf16[1,1056,128]{2,1,0:T(8,128)(2,1)S(1)}, bf16[1,1056,128]{2,1,0:T(8,128)(2,1)S(1)}, u32[]{:S(2)}, u32[]{:S(2)}) collective-permute-start(bf16[1,1056,128]{2,1,0:T(8,128)(2,1)S(1)} %add_convert_fusion.13), channel_id=1, source_target_pairs={{0,16},{16,0},{1,17},{17,1},{2,18},{18,2},{3,19},{19,3},{4,20},{20... | collective-permute-start | bytes 811016 | tf_op jit(solution)/shard_map/ppermute | solution.py:30
  377.8 15.0 %collective-permute-start.72 = (bf16[2112,1024]{1,0:T(8,128)(2,1)S(1)}, bf16[2112,1024]{1,0:T(8,128)(2,1)S(1)}, u32[]{:S(2)}, u32[]{:S(2)}) collective-permute-start(bf16[2112,1024]{1,0:T(8,128)(2,1)S(1)} %feed_weight_grads.6), channel_id=1, source_target_pairs={{0,1},{1,0},{2,3},{3,2},{4,5},{5,4},{6,7},{7,6},{8,9},{9,8},{10,11... | collective-permute-start | bytes 12976136 | tf_op jit(solution)/shard_map/ppermute | solution.py:30
  377.9 14.7 %collective-permute-start.73 = (bf16[2,1056,128]{2,1,0:T(8,128)(2,1)S(1)}, bf16[2,1056,128]{2,1,0:T(8,128)(2,1)S(1)}, u32[]{:S(2)}, u32[]{:S(2)}) collective-permute-start(bf16[2,1056,128]{2,1,0:T(8,128)(2,1)S(1)} %pad_maximum_fusion.11), channel_id=1, source_target_pairs={{0,8},{8,0},{1,9},{9,1},{2,10},{10,2},{3,11},{11,3},{4,12},{12,4},... | collective-permute-start | bytes 1622024 | tf_op jit(solution)/shard_map/ppermute | solution.py:30
  378.1 14.7 %collective-permute-start.74 = (bf16[2,1056,128]{2,1,0:T(8,128)(2,1)S(1)}, bf16[2,1056,128]{2,1,0:T(8,128)(2,1)S(1)}, u32[]{:S(2)}, u32[]{:S(2)}) collective-permute-start(bf16[2,1056,128]{2,1,0:T(8,128)(2,1)S(1)} %pad_maximum_fusion.12), channel_id=1, source_target_pairs={{0,4},{4,0},{1,5},{5,1},{2,6},{6,2},{3,7},{7,3},{8,12},{12,8},{9,1... | collective-permute-start | bytes 1622024 | tf_op jit(solution)/shard_map/ppermute | solution.py:30
  378.9 18.4 %collective-permute-start.66 = (bf16[256,1024]{1,0:T(8,128)(2,1)S(1)}, bf16[256,1024]{1,0:T(8,128)(2,1)S(1)}, u32[]{:S(2)}, u32[]{:S(2)}) collective-permute-start(bf16[256,1024]{1,0:T(8,128)(2,1)S(1)} %bitcast.148), channel_id=1, source_target_pairs={{0,2},{2,0},{1,3},{3,1},{4,6},{6,4},{5,7},{7,5},{8,10},{10,8},{9,1... | collective-permute-start | bytes 1572872 | tf_op jit(solution)/shard_map/ppermute | solution.py:30
  396.4 34.3 %collective-permute-start.75 = (bf16[4,1056,128]{2,1,0:T(8,128)(2,1)S(1)}, bf16[4,1056,128]{2,1,0:T(8,128)(2,1)S(1)}, u32[]{:S(2)}, u32[]{:S(2)}) collective-permute-start(bf16[4,1056,128]{2,1,0:T(8,128)(2,1)S(1)} %slice.362), channel_id=1, source_target_pairs={{0,4},{4,0},{1,5},{5,1},{2,6},{6,2},{3,7},{7,3},{8,12},{12,8},{9,1... | collective-permute-start | bytes 3244040 | tf_op jit(solution)/shard_map/ppermute | solution.py:30
  399.2 33.5 %collective-permute-start.76 = (bf16[4,1056,128]{2,1,0:T(8,128)(2,1)S(1)}, bf16[4,1056,128]{2,1,0:T(8,128)(2,1)S(1)}, u32[]{:S(2)}, u32[]{:S(2)}) collective-permute-start(bf16[4,1056,128]{2,1,0:T(8,128)(2,1)S(1)} %slice.363), channel_id=1, source_target_pairs={{0,8},{8,0},{1,9},{9,1},{2,10},{10,2},{3,11},{11,3},{4,12},{12,4},... | collective-permute-start | bytes 3244040 | tf_op jit(solution)/shard_map/ppermute | solution.py:30
  401.0 29.6 %collective-permute-start.67 = (bf16[2,256,128]{2,1,0:T(8,128)(2,1)S(1)}, bf16[2,256,128]{2,1,0:T(8,128)(2,1)S(1)}, u32[]{:S(2)}, u32[]{:S(2)}) collective-permute-start(bf16[2,256,128]{2,1,0:T(8,128)(2,1)S(1)} %get-tuple-element.281), channel_id=1, source_target_pairs={{0,4},{4,0},{1,5},{5,1},{2,6},{6,2},{3,7},{7,3},{8,12},{12,8},{9,1... | collective-permute-start | bytes 393224 | tf_op jit(solution)/shard_map/ppermute | solution.py:30
  401.8 28.7 %collective-permute-start.68 = (bf16[2,256,128]{2,1,0:T(8,128)(2,1)S(1)}, bf16[2,256,128]{2,1,0:T(8,128)(2,1)S(1)}, u32[]{:S(2)}, u32[]{:S(2)}) collective-permute-start(bf16[2,256,128]{2,1,0:T(8,128)(2,1)S(1)} %get-tuple-element.280), channel_id=1, source_target_pairs={{0,8},{8,0},{1,9},{9,1},{2,10},{10,2},{3,11},{11,3},{4,12},{12,4},... | collective-permute-start | bytes 393224 | tf_op jit(solution)/shard_map/ppermute | solution.py:30
  402.1 28.4 %collective-permute-start.69 = (bf16[2,256,128]{2,1,0:T(8,128)(2,1)S(1)}, bf16[2,256,128]{2,1,0:T(8,128)(2,1)S(1)}, u32[]{:S(2)}, u32[]{:S(2)}) collective-permute-start(bf16[2,256,128]{2,1,0:T(8,128)(2,1)S(1)} %get-tuple-element.279), channel_id=1, source_target_pairs={{0,12},{4,8},{8,4},{12,0},{1,13},{5,9},{9,5},{13,1},{2,14},{6,10},... | collective-permute-start | bytes 393224 | tf_op jit(solution)/shard_map/ppermute | solution.py:30
  431.1 21.0 %collective-permute-start.77 = (bf16[2,1056,128]{2,1,0:T(8,128)(2,1)S(1)}, bf16[2,1056,128]{2,1,0:T(8,128)(2,1)S(1)}, u32[]{:S(2)}, u32[]{:S(2)}) collective-permute-start(bf16[2,1056,128]{2,1,0:T(8,128)(2,1)S(1)} %slice.417), channel_id=1, source_target_pairs={{0,8},{8,0},{1,9},{9,1},{2,10},{10,2},{3,11},{11,3},{4,12},{12,4},... | collective-permute-start | bytes 1622024 | tf_op jit(solution)/shard_map/ppermute | solution.py:30
  433.0 19.2 %collective-permute-start.78 = (bf16[2,1056,128]{2,1,0:T(8,128)(2,1)S(1)}, bf16[2,1056,128]{2,1,0:T(8,128)(2,1)S(1)}, u32[]{:S(2)}, u32[]{:S(2)}) collective-permute-start(bf16[2,1056,128]{2,1,0:T(8,128)(2,1)S(1)} %slice.418), channel_id=1, source_target_pairs={{0,4},{4,0},{1,5},{5,1},{2,6},{6,2},{3,7},{7,3},{8,12},{12,8},{9,1... | collective-permute-start | bytes 1622024 | tf_op jit(solution)/shard_map/ppermute | solution.py:30
  434.3 18.6 %collective-permute-start.79 = (bf16[256,1024]{1,0:T(8,128)(2,1)S(1)}, bf16[256,1024]{1,0:T(8,128)(2,1)}, u32[]{:S(2)}, u32[]{:S(2)}) collective-permute-start(bf16[256,1024]{1,0:T(8,128)(2,1)S(1)} %copy-done.119), channel_id=1, source_target_pairs={{0,0},{1,16},{16,1},{17,17},{2,2},{3,18},{18,3},{19,19},{4,4},{5,2... | collective-permute-start | bytes 1572872 | tf_op jit(solution)/shard_map/ppermute | solution.py:841
  454.9 44.2 %collective-permute-start.84 = (bf16[1,1056,128]{2,1,0:T(8,128)(2,1)S(1)}, bf16[1,1056,128]{2,1,0:T(8,128)(2,1)S(1)}, u32[]{:S(2)}, u32[]{:S(2)}) collective-permute-start(bf16[1,1056,128]{2,1,0:T(8,128)(2,1)S(1)} %slice.424), channel_id=1, source_target_pairs={{0,16},{16,0},{1,17},{17,1},{2,18},{18,2},{3,19},{19,3},{4,20},{20... | collective-permute-start | bytes 811016 | tf_op jit(solution)/shard_map/ppermute | solution.py:30
  460.4 26.9 %collective-permute-start.83 = (bf16[256,1024]{1,0:T(8,128)(2,1)S(1)}, bf16[256,1024]{1,0:T(8,128)(2,1)S(1)}, u32[]{:S(2)}, u32[]{:S(2)}) collective-permute-start(bf16[256,1024]{1,0:T(8,128)(2,1)S(1)} %get-tuple-element.270), channel_id=1, source_target_pairs={{0,12},{4,8},{8,4},{12,0},{1,13},{5,9},{9,5},{13,1},{2,14},{6,10},... | collective-permute-start | bytes 1572872 | tf_op jit(solution)/shard_map/ppermute | solution.py:30
  461.8 35.6 %collective-permute-start.82 = (bf16[256,1024]{1,0:T(8,128)(2,1)S(1)}, bf16[256,1024]{1,0:T(8,128)(2,1)S(1)}, u32[]{:S(2)}, u32[]{:S(2)}) collective-permute-start(bf16[256,1024]{1,0:T(8,128)(2,1)S(1)} %get-tuple-element.271), channel_id=1, source_target_pairs={{0,8},{8,0},{1,9},{9,1},{2,10},{10,2},{3,11},{11,3},{4,12},{12,4},... | collective-permute-start | bytes 1572872 | tf_op jit(solution)/shard_map/ppermute | solution.py:30
  462.8 34.5 %collective-permute-start.81 = (bf16[256,1024]{1,0:T(8,128)(2,1)S(1)}, bf16[256,1024]{1,0:T(8,128)(2,1)S(1)}, u32[]{:S(2)}, u32[]{:S(2)}) collective-permute-start(bf16[256,1024]{1,0:T(8,128)(2,1)S(1)} %get-tuple-element.269), channel_id=1, source_target_pairs={{0,4},{4,0},{1,5},{5,1},{2,6},{6,2},{3,7},{7,3},{8,12},{12,8},{9,1... | collective-permute-start | bytes 1572872 | tf_op jit(solution)/shard_map/ppermute | solution.py:30
  464.2 35.0 %collective-permute-start.85 = (bf16[1,1056,128]{2,1,0:T(8,128)(2,1)S(1)}, bf16[1,1056,128]{2,1,0:T(8,128)(2,1)S(1)}, u32[]{:S(2)}, u32[]{:S(2)}) collective-permute-start(bf16[1,1056,128]{2,1,0:T(8,128)(2,1)S(1)} %slice.426), channel_id=1, source_target_pairs={{0,16},{16,0},{1,17},{17,1},{2,18},{18,2},{3,19},{19,3},{4,20},{20... | collective-permute-start | bytes 811016 | tf_op jit(solution)/shard_map/ppermute | solution.py:30
  502.1 23.6 %collective-permute-start.86 = (bf16[4,2,128,1024]{3,2,1,0:T(8,128)(2,1)S(1)}, bf16[4,2,128,1024]{3,2,1,0:T(8,128)(2,1)S(1)}, u32[]{:S(2)}, u32[]{:S(2)}) collective-permute-start(bf16[4,2,128,1024]{3,2,1,0:T(8,128)(2,1)S(1)} %fusion), channel_id=1, source_target_pairs={{0,1},{1,0},{2,3},{3,2},{4,5},{5,4},{6,7},{7,6},{8,9},{9,8},{10,11... | collective-permute-start | bytes 6291464 | tf_op jit(solution)/shard_map/ppermute | solution.py:30
  524.7 42.3 %collective-permute-start.97 = (f32[4,1024]{1,0:T(4,128)S(1)}, f32[4,1024]{1,0:T(4,128)S(1)}, u32[]{:S(2)}, u32[]{:S(2)}) collective-permute-start(f32[4,1024]{1,0:T(4,128)S(1)} %add.205), channel_id=1, source_target_pairs={{0,4},{4,0},{1,5},{5,1},{2,6},{6,2},{3,7},{7,3},{8,12},{12,8},{9,1... | collective-permute-start | bytes 49160 | tf_op jit(solution)/shard_map/ppermute | solution.py:30
  526.9 18.4 %collective-permute-start.87 = (bf16[1,1056,128]{2,1,0:T(8,128)(2,1)S(1)}, bf16[1,1056,128]{2,1,0:T(8,128)(2,1)S(1)}, u32[]{:S(2)}, u32[]{:S(2)}) collective-permute-start(bf16[1,1056,128]{2,1,0:T(8,128)(2,1)S(1)} %add_convert_fusion.12), channel_id=1, source_target_pairs={{0,16},{16,0},{1,17},{17,1},{2,18},{18,2},{3,19},{19,3},{4,20},{20... | collective-permute-start | bytes 811016 | tf_op jit(solution)/shard_map/ppermute | solution.py:30
  528.5 21.8 %collective-permute-start.88 = (bf16[1,1056,128]{2,1,0:T(8,128)(2,1)S(1)}, bf16[1,1056,128]{2,1,0:T(8,128)(2,1)S(1)}, u32[]{:S(2)}, u32[]{:S(2)}) collective-permute-start(bf16[1,1056,128]{2,1,0:T(8,128)(2,1)S(1)} %add_convert_fusion.11), channel_id=1, source_target_pairs={{0,16},{16,0},{1,17},{17,1},{2,18},{18,2},{3,19},{19,3},{4,20},{20... | collective-permute-start | bytes 811016 | tf_op jit(solution)/shard_map/ppermute | solution.py:30
  530.0 26.8 %collective-permute-start.91 = (bf16[2,128,1024]{2,1,0:T(8,128)(2,1)S(1)}, bf16[2,128,1024]{2,1,0:T(8,128)(2,1)S(1)}, u32[]{:S(2)}, u32[]{:S(2)}) collective-permute-start(bf16[2,128,1024]{2,1,0:T(8,128)(2,1)S(1)} %get-tuple-element.267), channel_id=1, source_target_pairs={{0,12},{4,8},{8,4},{12,0},{1,13},{5,9},{9,5},{13,1},{2,14},{6,10},... | collective-permute-start | bytes 1572872 | tf_op jit(solution)/shard_map/ppermute | solution.py:30
  531.0 31.5 %collective-permute-start.90 = (bf16[2,128,1024]{2,1,0:T(8,128)(2,1)S(1)}, bf16[2,128,1024]{2,1,0:T(8,128)(2,1)S(1)}, u32[]{:S(2)}, u32[]{:S(2)}) collective-permute-start(bf16[2,128,1024]{2,1,0:T(8,128)(2,1)S(1)} %get-tuple-element.268), channel_id=1, source_target_pairs={{0,8},{8,0},{1,9},{9,1},{2,10},{10,2},{3,11},{11,3},{4,12},{12,4},... | collective-permute-start | bytes 1572872 | tf_op jit(solution)/shard_map/ppermute | solution.py:30
  545.3 17.2 %collective-permute-start.89 = (bf16[2,128,1024]{2,1,0:T(8,128)(2,1)S(1)}, bf16[2,128,1024]{2,1,0:T(8,128)(2,1)S(1)}, u32[]{:S(2)}, u32[]{:S(2)}) collective-permute-start(bf16[2,128,1024]{2,1,0:T(8,128)(2,1)S(1)} %get-tuple-element.266), channel_id=1, source_target_pairs={{0,4},{4,0},{1,5},{5,1},{2,6},{6,2},{3,7},{7,3},{8,12},{12,8},{9,1... | collective-permute-start | bytes 1572872 | tf_op jit(solution)/shard_map/ppermute | solution.py:30
  562.9 15.3 %collective-permute-start.98 = (bf16[2,1056,128]{2,1,0:T(8,128)(2,1)S(1)}, bf16[2,1056,128]{2,1,0:T(8,128)(2,1)S(1)}, u32[]{:S(2)}, u32[]{:S(2)}) collective-permute-start(bf16[2,1056,128]{2,1,0:T(8,128)(2,1)S(1)} %pad_maximum_fusion.13), channel_id=1, source_target_pairs={{0,8},{8,0},{1,9},{9,1},{2,10},{10,2},{3,11},{11,3},{4,12},{12,4},... | collective-permute-start | bytes 1622024 | tf_op jit(solution)/shard_map/ppermute | solution.py:30
  563.9 24.8 %collective-permute-start.92 = (bf16[256,2,1024]{2,0,1:T(8,128)(2,1)S(1)}, bf16[256,2,1024]{2,0,1:T(8,128)(2,1)S(1)}, u32[]{:S(2)}, u32[]{:S(2)}) collective-permute-start(bf16[256,2,1024]{2,0,1:T(8,128)(2,1)S(1)} %fusion.10), channel_id=1, source_target_pairs={{0,2},{2,0},{1,3},{3,1},{4,6},{6,4},{5,7},{7,5},{8,10},{10,8},{9,1... | collective-permute-start | bytes 3145736 | tf_op jit(solution)/shard_map/ppermute | solution.py:30
  565.8 15.3 %collective-permute-start.99 = (bf16[2,1056,128]{2,1,0:T(8,128)(2,1)S(1)}, bf16[2,1056,128]{2,1,0:T(8,128)(2,1)S(1)}, u32[]{:S(2)}, u32[]{:S(2)}) collective-permute-start(bf16[2,1056,128]{2,1,0:T(8,128)(2,1)S(1)} %pad_maximum_fusion.14), channel_id=1, source_target_pairs={{0,4},{4,0},{1,5},{5,1},{2,6},{6,2},{3,7},{7,3},{8,12},{12,8},{9,1... | collective-permute-start | bytes 1622024 | tf_op jit(solution)/shard_map/ppermute | solution.py:30
  567.0 37.2 %collective-permute-start.103 = (bf16[4,1056,128]{2,1,0:T(8,128)(2,1)S(1)}, bf16[4,1056,128]{2,1,0:T(8,128)(2,1)S(1)}, u32[]{:S(2)}, u32[]{:S(2)}) collective-permute-start(bf16[4,1056,128]{2,1,0:T(8,128)(2,1)S(1)} %pad_maximum_fusion.7), channel_id=1, source_target_pairs={{0,4},{4,0},{1,5},{5,1},{2,6},{6,2},{3,7},{7,3},{8,12},{12,8},{9,1... | collective-permute-start | bytes 3244040 | tf_op jit(solution)/shard_map/ppermute | solution.py:30
  568.0 44.5 %collective-permute-start.104 = (bf16[4,1056,128]{2,1,0:T(8,128)(2,1)S(1)}, bf16[4,1056,128]{2,1,0:T(8,128)(2,1)S(1)}, u32[]{:S(2)}, u32[]{:S(2)}) collective-permute-start(bf16[4,1056,128]{2,1,0:T(8,128)(2,1)S(1)} %pad_maximum_fusion.8), channel_id=1, source_target_pairs={{0,8},{8,0},{1,9},{9,1},{2,10},{10,2},{3,11},{11,3},{4,12},{12,4},... | collective-permute-start | bytes 3244040 | tf_op jit(solution)/shard_map/ppermute | solution.py:30
  578.2 47.4 %collective-permute-start.101 = (bf16[4,1056,128]{2,1,0:T(8,128)(2,1)S(1)}, bf16[4,1056,128]{2,1,0:T(8,128)(2,1)S(1)}, u32[]{:S(2)}, u32[]{:S(2)}) collective-permute-start(bf16[4,1056,128]{2,1,0:T(8,128)(2,1)S(1)} %pad_maximum_fusion.5), channel_id=1, source_target_pairs={{0,4},{4,0},{1,5},{5,1},{2,6},{6,2},{3,7},{7,3},{8,12},{12,8},{9,1... | collective-permute-start | bytes 3244040 | tf_op jit(solution)/shard_map/ppermute | solution.py:30
  581.1 52.5 %collective-permute-start.102 = (bf16[4,1056,128]{2,1,0:T(8,128)(2,1)S(1)}, bf16[4,1056,128]{2,1,0:T(8,128)(2,1)S(1)}, u32[]{:S(2)}, u32[]{:S(2)}) collective-permute-start(bf16[4,1056,128]{2,1,0:T(8,128)(2,1)S(1)} %pad_maximum_fusion.6), channel_id=1, source_target_pairs={{0,8},{8,0},{1,9},{9,1},{2,10},{10,2},{3,11},{11,3},{4,12},{12,4},... | collective-permute-start | bytes 3244040 | tf_op jit(solution)/shard_map/ppermute | solution.py:30
  589.1 44.5 %collective-permute-start.100 = (bf16[256,2,1024]{2,0,1:T(8,128)(2,1)S(1)}, bf16[256,2,1024]{2,0,1:T(8,128)(2,1)S(1)}, u32[]{:S(2)}, u32[]{:S(2)}) collective-permute-start(bf16[256,2,1024]{2,0,1:T(8,128)(2,1)S(1)} %add_convert_fusion.5), channel_id=1, source_target_pairs={{0,0},{1,16},{16,1},{17,17},{2,2},{3,18},{18,3},{19,19},{4,4},{5,2... | collective-permute-start | bytes 3145736 | tf_op jit(solution)/shard_map/ppermute | solution.py:841
  636.7 25.3 %collective-permute-start.107 = (bf16[256,2,1024]{2,0,1:T(8,128)(2,1)S(1)}, bf16[256,2,1024]{2,0,1:T(8,128)(2,1)S(1)}, u32[]{:S(2)}, u32[]{:S(2)}) collective-permute-start(bf16[256,2,1024]{2,0,1:T(8,128)(2,1)S(1)} %add_convert_fusion.4), channel_id=1, source_target_pairs={{0,2},{2,0},{1,3},{3,1},{4,6},{6,4},{5,7},{7,5},{8,10},{10,8},{9,1... | collective-permute-start | bytes 3145736 | tf_op jit(solution)/shard_map/ppermute | solution.py:30
  (175 other events, 2122.2 us)
